TPU v7x, 32 devices: a whole 2x2x4 slice. The times are simulated.
32 devices in a mesh: frames: 2 (over y), codebook: 4 (over x, core), hidden: 4 (over z).
Axes of the slice: x: 2, y: 2, z: 4, core: 2. Of those that a mesh axis runs over, the one named last changes fastest.
Arguments:
- temporal: bfloat16 [1024, 4096], P(('frames', 'codebook'), 'hidden'), may hold values from -6 to 6
- frame_ids: int32 [1024, 4], P('frames', 'codebook'), may hold values from 0 to 2047
- proj_weight: bfloat16 [4, 4096, 1024], P('codebook', 'hidden'), may hold values from -0.09375 to 0.09375
- embed_table: bfloat16 [4, 2049, 1024], P('codebook'), may hold values from -6 to 6
- qkv_weight: bfloat16 [4, 3, 1024, 1024], P('codebook', None, None, 'hidden'), may hold values from -12 to 12
- out_weight: bfloat16 [4, 1024, 1024], P('codebook', 'hidden'), may hold values from -0.1875 to 0.1875
- gate_up: bfloat16 [4, 2, 1024, 4096], P('codebook', None, None, 'hidden'), may hold values from -0.1875 to 0.1875
- down_weight: bfloat16 [4, 4096, 1024], P('codebook', 'hidden'), may hold values from -0.09375 to 0.09375
- norm_gains: float32 [4, 2, 1024], P('codebook'), may hold values from 0.25 to 1.75
Outputs:
- depth_states: float32 [4, 1024, 1024], P('codebook', 'frames', 'hidden')
All inputs are finite; a program needn't handle non-finite values.
Results may differ from a plain program's by a relative error of at most 0.015.
Values may be sent and summed in bfloat16 or wider, within the bound.
No kernel may reach another device: no remote copies, remote signals or barrier semaphores. Data moves between devices by JAX's collectives and lax.ppermute only.
A program may use at most 192 MiB of HBM per device.

v0:
```python
import jax
import jax.numpy as jnp
from jax import lax
from jax.sharding import PartitionSpec as P

HEADS = 16


def shifted(block, axis, distance):
    devices = range(lax.axis_size(axis))
    route = [(i - distance, i) for i in devices if i - distance in devices]
    return lax.ppermute(block, axis, route)


def normalize(values, norm_gain):
    return values * lax.rsqrt(jnp.mean(values * values, axis=-1, keepdims=True) + 1e-05) * norm_gain


def gated(normed, piece):
    gate_sum = jnp.dot(normed, piece[0], preferred_element_type=jnp.float32)
    upper_sum = jnp.dot(normed, piece[1], preferred_element_type=jnp.float32)
    return (jax.nn.silu(gate_sum) * upper_sum).astype(jnp.bfloat16)


def body(
    temporal,
    frame_ids,
    proj_weight,
    embed_table,
    qkv_weight,
    out_weight,
    gate_up,
    down_weight,
    norm_gains,
):
    code_index = lax.axis_index("codebook")
    hidden_index = lax.axis_index("hidden")
    hidden_count = lax.axis_size("hidden")
    start_id = embed_table.shape[1] - 1
    token_table = embed_table[0]
    norm_gain = norm_gains[0]
    earlier = shifted(frame_ids, "codebook", 1)[:, 0]
    previous = jnp.where(code_index == 0, start_id, earlier)
    partial_sum = jnp.dot(
        lax.all_gather(temporal, "codebook", axis=0, tiled=True),
        proj_weight[0],
        preferred_element_type=jnp.float32,
    )
    row_count = partial_sum.shape[0]
    x_zero = lax.psum(partial_sum.astype(jnp.bfloat16), "hidden").astype(jnp.float32) + token_table[
        previous
    ].astype(jnp.float32)
    normed = normalize(x_zero, norm_gain[0]).astype(jnp.bfloat16)
    local_width = qkv_weight.shape[3]
    local_heads = HEADS // hidden_count
    head_size = local_width // local_heads
    triple = jnp.einsum(
        "rd,kdc->krc", normed, qkv_weight[0], preferred_element_type=jnp.float32
    ).astype(jnp.bfloat16)
    query_heads = triple[0].reshape(row_count, local_heads, head_size)
    highest = jnp.full((row_count, local_heads), -1e30, jnp.float32)
    key_piece = lax.all_gather(triple[1][None], "codebook", axis=0, tiled=True)
    value_piece = lax.all_gather(triple[2][None], "codebook", axis=0, tiled=True)
    positions = key_piece.shape[0]
    key_heads = key_piece.reshape(positions, row_count, local_heads, head_size)
    value_heads = value_piece.reshape(positions, row_count, local_heads, head_size)
    scores = jnp.einsum(
        "fhd,jfhd->jfh", query_heads, key_heads, preferred_element_type=jnp.float32
    ) * head_size ** (-0.5)
    valid = (jnp.arange(positions, dtype=jnp.int32) <= code_index)[:, None, None]
    scores = jnp.where(valid, scores, -1e30)
    new_highest = jnp.maximum(highest, jnp.max(scores, axis=0))
    weights = jnp.where(valid, jnp.exp(scores - new_highest[None]), 0.0)
    running = jnp.sum(weights, axis=0)
    summed = jnp.einsum(
        "jfh,jfhd->fhd",
        weights.astype(jnp.bfloat16),
        value_heads,
        preferred_element_type=jnp.float32,
    )
    highest, running, summed = (new_highest, running, summed)
    attended = (summed / running[..., None]).reshape(row_count, local_width).astype(jnp.bfloat16)
    attention_part = jnp.dot(attended, out_weight[0], preferred_element_type=jnp.float32)
    residual = x_zero + lax.psum(attention_part.astype(jnp.bfloat16), "hidden").astype(jnp.float32)
    normed_two = normalize(residual, norm_gain[1]).astype(jnp.bfloat16)
    activated = gated(normed_two, gate_up[0])
    down_part = jnp.dot(activated, down_weight[0], preferred_element_type=jnp.float32)
    mlp_piece = lax.psum_scatter(
        down_part.astype(jnp.bfloat16), "hidden", scatter_dimension=1, tiled=True
    ).astype(jnp.float32)
    own_residual = lax.dynamic_slice_in_dim(residual, hidden_index * local_width, local_width, 1)
    return (own_residual + mlp_piece)[None]


def solution(mesh):
    placed = (
        P(("frames", "codebook"), "hidden"),
        P("frames", "codebook"),
        P("codebook", "hidden", None),
        P("codebook", None, None),
        P("codebook", None, None, "hidden"),
        P("codebook", "hidden", None),
        P("codebook", None, None, "hidden"),
        P("codebook", "hidden", None),
        P("codebook", None, None),
    )
    return jax.shard_map(
        body,
        mesh=mesh,
        in_specs=placed,
        out_specs=P("codebook", "frames", "hidden"),
        check_vma=False,
    )
```

profile of v0, /device:TPU:0, one launch (start us, length us, event | category | flops | bytes accessed | tf_op | source)
XLA Modules:
  0.0 231.3 jit_solution(12573827764787216566)
XLA Ops:
  7.3 21.0 %all-gather.4.cloned.1.call-done = bf16[512,1024]{1,0:T(8,128)(2,1)} async-done(((bf16[128,1024]{1,0:T(8,128)(2,1)}), bf16[512,1024]{1,0:T(8,128)(2,1)}) %all-gather.4.cloned.1.call-update) | async-done | bytes 1048592 | tf_op jit(solution)/shard_map/all_gather | solution.py:45
  28.4 3.5 %fusion.12 = bf16[512,1024]{1,0:T(8,128)(2,1)} fusion(bf16[512,1024]{1,0:T(8,128)(2,1)} %all-gather.4.cloned.1.call-done, bf16[1,1024,1024]{2,1,0:T(8,128)(2,1)S(1)} %copy-done), kind=kOutput, calls=%fused_computation.22 | convolution fusion | flops 1074266112 | bytes 4194304 | tf_op jit(solution)/shard_map/dot_general | solution.py:44
  32.0 2.1 collective-permute-start
  34.9 5.5 %gather_fusion = bf16[512,1024]{1,0:T(8,128)(2,1)S(1)} fusion(bf16[2049,1024]{1,0:T(8,128)(2,1)} %bitcast.64, s32[1024]{0:T(1024)S(1)} %pad_clamp_fusion), kind=kCustom, calls=%fused_computation | custom fusion | bytes 2099200 | tf_op jit(solution)/shard_map/gather | solution.py:50
  40.4 43.5 %all-reduce.3.cloned.1.call-done = bf16[512,1024]{1,0:T(8,128)(2,1)} async-done(((bf16[512,1024]{1,0:T(8,128)(2,1)}), bf16[512,1024]{1,0:T(8,128)(2,1)}) %all-reduce.3.cloned.1.call-update) | async-done | bytes 1048592 | tf_op jit(solution)/shard_map/psum | solution.py:50
  83.9 1.7 multiply_reduce_fusion.3
  85.6 2.6 %fusion.23 = bf16[3,512,256]{1,2,0:T(8,128)(2,1)S(1)} fusion(bf16[1,3,1024,256]{3,2,1,0:T(8,128)(2,1)} %param.13, bf16[512,1024]{1,0:T(8,128)(2,1)S(1)} %gather_fusion, bf16[512,1024]{1,0:T(8,128)(2,1)S(1)} %copy-done.1, f32[1024]{0:T(1024)S(1)} %bitcast.71, f32[512]{0:T(512)S(1)} %add_rsqrt_fusion.1), kind=kOutput, calls=%fused_computation.26 | convolution fusion | flops 808845312 | bytes 4462592 | tf_op jit(solution)/shard_map/rd,kdc->krc/dot_general | solution.py:57
  88.2 0.9 fusion.38
  89.0 1.8 copy.21
  90.9 1.8 copy.23
  93.6 13.5 %all-gather.6.cloned.1.call-done = bf16[4,512,256]{2,1,0:T(8,128)(2,1)} async-done(((bf16[1,512,256]{2,1,0:T(8,128)(2,1)}), bf16[4,512,256]{2,1,0:T(8,128)(2,1)}) %all-gather.6.cloned.1.call-update) | async-done | bytes 1048592 | tf_op jit(solution)/shard_map/all_gather | solution.py:62
  107.1 2.3 copy.38
  109.4 1.7 multiply_reduce_fusion.1
  111.2 14.1 %all-gather.8.cloned.1.call-done = bf16[4,512,256]{2,1,0:T(8,128)(2,1)} async-done(((bf16[1,512,256]{2,1,0:T(8,128)(2,1)}), bf16[4,512,256]{2,1,0:T(8,128)(2,1)}) %all-gather.8.cloned.1.call-update) | async-done | bytes 1048592 | tf_op jit(solution)/shard_map/all_gather | solution.py:63
  125.4 2.3 copy.39
  127.7 1.5 multiply_reduce_fusion
  129.3 1.5 convolution_convert_fusion
  130.8 51.9 %all-reduce.5.cloned.1.call-done = bf16[512,1024]{1,0:T(8,128)(2,1)} async-done(((bf16[512,1024]{1,0:T(8,128)(2,1)}), bf16[512,1024]{1,0:T(8,128)(2,1)}) %all-reduce.5.cloned.1.call-update) | async-done | bytes 1048592 | tf_op jit(solution)/shard_map/psum | solution.py:84
  182.7 2.2 multiply_reduce_fusion.2
  185.0 1.3 copy-done.2
  186.3 2.7 %fusion.4 = f32[512,1024]{1,0:T(8,128)} fusion(bf16[1,2,1024,1024]{3,2,1,0:T(8,128)(2,1)S(1)} %copy-done.5, f32[512,1024]{1,0:T(8,128)S(1)} %get-tuple-element.6, f32[1024]{0:T(1024)S(1)} %bitcast.69, f32[512]{0:T(512)S(1)} %add_rsqrt_fusion), kind=kOutput, calls=%fused_computation.5 | convolution fusion | flops 1075314688 | bytes 6297600 | tf_op jit(solution)/shard_map/dot_general | solution.py:20
  189.0 6.8 %fusion.15 = bf16[512,1024]{1,0:T(8,128)(2,1)} fusion(bf16[1,1024,1024]{2,1,0:T(8,128)(2,1)} %param.16, f32[512,1024]{1,0:T(8,128)} %fusion.4, bf16[1,2,1024,1024]{3,2,1,0:T(8,128)(2,1)} %param.15, f32[512,1024]{1,0:T(8,128)} %copy-done.2, f32[1024]{0:T(1024)S(1)} %bitcast.70, f32[512]{0:T(512)S(1)} %add_rsqrt_fusion), kind=kOutput, calls=%fused_computation.23 | convolution fusion | flops 2152726528 | bytes 9443328 | tf_op jit(solution)/shard_map/dot_general | solution.py:87
  195.8 26.7 %reduce-scatter.2.cloned.1.call-done = bf16[512,256]{1,0:T(8,128)(2,1)} async-done(((bf16[512,1024]{1,0:T(8,128)(2,1)}), bf16[512,256]{1,0:T(8,128)(2,1)}) %reduce-scatter.2.cloned.1.call-update) | async-done | bytes 262160 | tf_op jit(solution)/shard_map/reduce_scatter | solution.py:88
  222.5 2.0 add_bitcast_fusion
  (38 shorter events, 2.9 us)
Async XLA Ops:
  6.5 21.8 %copy-start = (bf16[1,1024,1024]{2,1,0:T(8,128)(2,1)S(1)}, bf16[1,1024,1024]{2,1,0:T(8,128)(2,1)}, u32[]{:S(2)}) copy-start(bf16[1,1024,1024]{2,1,0:T(8,128)(2,1)} %param.11) | copy-start | bytes 6291460
  6.5 21.8 %all-gather.4.cloned.1.call-start = ((), (), s32[]{:S(2)}) async-start(), calls=%async_computation.1 | async-start | bytes 1310720 | tf_op jit(solution)/shard_map/all_gather | solution.py:45
  7.3 24.7 %copy-start.6 = (s32[512,1]{0,1:T(1,128)S(1)}, s32[512,1]{0,1:T(1,128)}, u32[]{:S(2)}) copy-start(s32[512,1]{0,1:T(1,128)} %param.10) | copy-start | bytes 6148
  7.3 26.8 %copy-start.4 = (f32[1,2,1024]{2,1,0:T(2,128)S(1)}, f32[1,2,1024]{2,1,0:T(2,128)}, u32[]{:S(2)}) copy-start(f32[1,2,1024]{2,1,0:T(2,128)} %param.17) | copy-start | bytes 24580
  7.3 76.6 %all-reduce.3.cloned.1.call-start = ((), (), s32[]{:S(2)}) async-start(), calls=%async_computation.2 | async-start | bytes 2097152 | tf_op jit(solution)/shard_map/psum | solution.py:50
  31.9 75.2 %all-gather.6.cloned.1.call-start = ((), (), s32[]{:S(2)}) async-start(), calls=%async_computation.3 | async-start | bytes 1310720 | tf_op jit(solution)/shard_map/all_gather | solution.py:62
  32.0 2.9 %collective-permute-start = (s32[512,1]{0,1:T(1,128)S(1)}, s32[512,1]{0,1:T(1,128)S(1)}, u32[]{:S(2)}, u32[]{:S(2)}) collective-permute-start(s32[512,1]{0,1:T(1,128)S(1)} %copy-done.6), channel_id=1, source_target_pairs={{0,4},{4,8},{8,12},{1,5},{5,9},{9,13},{2,6},{6,10},{10,14},{3,7},{... | collective-permute-start | bytes 6152 | tf_op jit(solution)/shard_map/ppermute | solution.py:12
  83.9 1.7 copy-start.1
  90.8 34.5 %all-gather.8.cloned.1.call-start = ((), (), s32[]{:S(2)}) async-start(), calls=%async_computation.4 | async-start | bytes 1310720 | tf_op jit(solution)/shard_map/all_gather | solution.py:63
  92.7 90.0 %all-reduce.5.cloned.1.call-start = ((), (), s32[]{:S(2)}) async-start(), calls=%async_computation.5 | async-start | bytes 2097152 | tf_op jit(solution)/shard_map/psum | solution.py:84
  127.7 1.6 copy-start.3
  130.8 91.8 %reduce-scatter.2.cloned.1.call-start = ((), (), s32[]{:S(2)}) async-start(), calls=%async_computation.6 | async-start | bytes 1310720 | tf_op jit(solution)/shard_map/reduce_scatter | solution.py:88
  182.7 3.6 %copy-start.5 = (bf16[1,2,1024,1024]{3,2,1,0:T(8,128)(2,1)S(1)}, bf16[1,2,1024,1024]{3,2,1,0:T(8,128)(2,1)}, u32[]{:S(2)}) copy-start(bf16[1,2,1024,1024]{3,2,1,0:T(8,128)(2,1)} %param.15) | copy-start | bytes 12582916
  185.0 1.3 copy-start.2
Sparse Core Ops, SparseCore 0:
  8.9 19.4 all-gather.3
  32.0 51.8 all-reduce.2
  91.0 16.0 all-gather.5
  108.6 16.7 all-gather.7
  130.9 51.8 all-reduce.4
  196.0 26.5 reduce-scatter.1
where the time goes:
time: 232 us; the launch traced here: 231 us
  waiting for transfers between devices  172 us (74%)
  matrix products  17 us (7%)
  local copies, waits for them, and re-layouts  15.8 us (7%)
  between operations  13.6 us (6%)
  other arithmetic  10.3 us (4%)
  starting transfers between devices  2.34 us (1%)
    psum x1, waiting for transfers between devices, body(): lax.psum(attention_part.astype(jnp.bfloat16), 'hidden').astype(jnp.float32)  51.9 us
    psum x1, waiting for transfers between devices, body(): lax.psum(partial_sum.astype(jnp.bfloat16), 'hidden').astype(jnp.float32)  43.5 us
    reduce_scatter x1, waiting for transfers between devices, body(): lax.psum_scatter(down_part.astype(jnp.bfloat16), 'hidden', scatter_dimens...  26.7 us
    all_gather x1, waiting for transfers between devices, body(): lax.all_gather(temporal, 'codebook', axis=0, tiled=True)  21 us
    all_gather x1, waiting for transfers between devices, body(): lax.all_gather(triple[2][None], 'codebook', axis=0, tiled=True)  14.1 us
    all_gather x1, waiting for transfers between devices, body(): key_piece = lax.all_gather(triple[1][None], 'codebook', axis=0, tiled=True)  13.5 us
    dot_general x1, matrix products, body(): jnp.dot(activated, down_weight[0], preferred_element_type=jnp.float32)  6.85 us
    unnamed x16, local copies, waits for them, and re-layouts  5.89 us
  transfers between devices with their start and end apart: 7, of which 7 were waited for; matrix products, arithmetic and copies ran while one was open for 5% of the time, Pallas kernels for 0%

commit v1 on v0

v1 whole, which is shorter than its diff:
```python
import functools

import jax
import jax.numpy as jnp
from jax import lax
from jax.experimental import pallas as pl
from jax.experimental.pallas import tpu as pltpu
from jax.sharding import PartitionSpec as P

HEADS = 16
CHUNKS = 2
ROW_BLOCK = 128
F32 = jnp.float32
BF16 = jnp.bfloat16


def swap(block, axis, distance):
    count = lax.axis_size(axis)
    return lax.ppermute(block, axis, [(i, i ^ distance) for i in range(count)])


def bits_of(axis):
    count = lax.axis_size(axis)
    return [1 << b for b in range(count.bit_length() - 1)]


def shifted(block, axis, distance):
    devices = range(lax.axis_size(axis))
    route = [(i - distance, i) for i in devices if i - distance in devices]
    return lax.ppermute(block, axis, route)


def gathered(block, axis):
    pieces = block[None]
    index = lax.axis_index(axis)
    for bit in reversed(bits_of(axis)):
        other = swap(pieces, axis, bit)
        upper = (index & bit) != 0
        first = jnp.where(upper, other, pieces)
        second = jnp.where(upper, pieces, other)
        pieces = jnp.stack([first, second], axis=1).reshape((-1,) + block.shape)
    return pieces


def normalize(values, norm_gain):
    return values * lax.rsqrt(jnp.mean(values * values, axis=-1, keepdims=True) + 1e-05) * norm_gain


def dot(a, b):
    return jnp.dot(a, b, preferred_element_type=F32)


def attend_kernel(slots, head_size, code_ref, query_ref, *refs):
    kv_refs = refs[: len(slots)]
    weight_refs = refs[len(slots) : -2]
    part_ref, sent_ref = refs[-2:]
    code = code_ref[0]
    width = query_ref.shape[-1]
    lanes = 128
    column = lax.broadcasted_iota(jnp.int32, (width, lanes), 0) // head_size
    head = lax.broadcasted_iota(jnp.int32, (width, lanes), 1)
    gather = (column == head).astype(F32).astype(BF16)
    head_t = lax.broadcasted_iota(jnp.int32, (lanes, width), 0)
    column_t = lax.broadcasted_iota(jnp.int32, (lanes, width), 1) // head_size
    spread = (column_t == head_t).astype(F32).astype(BF16)
    query = query_ref[...].astype(F32)
    scores = []
    for slot, kv_ref in zip(slots, kv_refs):
        product = query * kv_ref[0].astype(F32)
        high = product.astype(BF16)
        low = (product - high.astype(F32)).astype(BF16)
        score = (dot(high, gather) + dot(low, gather)) * head_size ** (-0.5)
        if slot:
            score = jnp.where((code ^ slot) <= code, score, -1e30)
        scores.append(score)
    highest = functools.reduce(jnp.maximum, scores)
    weights = [jnp.exp(score - highest) for score in scores]
    running = functools.reduce(jnp.add, weights)
    summed = None
    for kv_ref, weight in zip(kv_refs, weights):
        term = dot(weight.astype(BF16), spread) * kv_ref[1].astype(F32)
        summed = term if summed is None else summed + term
    inverse = 1.0 / running
    high = inverse.astype(BF16)
    low = (inverse - high.astype(F32)).astype(BF16)
    attended = (summed * (dot(high, spread) + dot(low, spread))).astype(BF16)
    part, start = None, 0
    for weight_ref in weight_refs:
        depth = weight_ref.shape[0]
        term = dot(attended[:, start : start + depth], weight_ref[...])
        part = term if part is None else part + term
        start += depth
    part_ref[...] = part
    sent_ref[...] = part.astype(BF16)


def attend(code_index, query, slots, kvs, weights, head_size):
    rows, width = query.shape
    block = min(rows, ROW_BLOCK)
    out_width = weights[0].shape[1]
    row_spec = pl.BlockSpec((block, width), lambda r: (r, 0))
    kv_spec = pl.BlockSpec((2, block, width), lambda r: (0, r, 0))
    out_spec = pl.BlockSpec((block, out_width), lambda r: (r, 0))
    return pl.pallas_call(
        functools.partial(attend_kernel, slots, head_size),
        grid=(rows // block,),
        in_specs=[pl.BlockSpec(memory_space=pltpu.SMEM), row_spec]
        + [kv_spec] * len(kvs)
        + [pl.BlockSpec(w.shape, lambda r: (0, 0)) for w in weights],
        out_specs=[out_spec, out_spec],
        out_shape=[
            jax.ShapeDtypeStruct((rows, out_width), F32),
            jax.ShapeDtypeStruct((rows, out_width), BF16),
        ],
        compiler_params=pltpu.CompilerParams(vmem_limit_bytes=24 * 1024 * 1024),
        name="attend",
    )(code_index.reshape(1).astype(jnp.int32), query, *kvs, *weights)


def body(
    temporal,
    frame_ids,
    proj_weight,
    embed_table,
    qkv_weight,
    out_weight,
    gate_up,
    down_weight,
    norm_gains,
):
    code_index = lax.axis_index("codebook")
    hidden_index = lax.axis_index("hidden")
    frame_index = lax.axis_index("frames")
    hidden_bits = bits_of("hidden")
    pair_bit, far_bits = hidden_bits[0], hidden_bits[1:]
    odd = (hidden_index & pair_bit) != 0
    start_id = embed_table.shape[1] - 1
    norm_gain = norm_gains[0]
    width = embed_table.shape[2]
    local_width = qkv_weight.shape[3]
    head_size = width // HEADS

    pieces = gathered(temporal, "codebook")
    row_count = pieces.shape[0] * pieces.shape[1]
    half = row_count // 2
    step = half // CHUNKS
    halves = pieces.reshape(2, CHUNKS, step, pieces.shape[2])
    kept_rows = jnp.where(odd, halves[1], halves[0])
    sent_rows = jnp.where(odd, halves[0], halves[1])

    share = local_width // lax.axis_size("frames")
    qkv_share = lax.dynamic_slice_in_dim(qkv_weight[0], frame_index * share, share, 2)
    out_share = lax.dynamic_slice_in_dim(out_weight[0], frame_index * share, share, 0)
    qkv_shares = [swap(qkv_share, "hidden", pair_bit)]
    out_shares = [swap(out_share, "hidden", pair_bit)]
    for bit in bits_of("frames"):
        qkv_shares += [swap(piece, "frames", bit) for piece in qkv_shares]
        out_shares += [swap(piece, "frames", bit) for piece in out_shares]
    qkv_pieces = [qkv_weight[0]] + qkv_shares
    out_pieces = [out_weight[0]] + out_shares

    earlier = shifted(frame_ids, "codebook", 1)[:, 0]
    previous = jnp.where(code_index == 0, start_id, earlier).reshape(2, half)
    previous = jnp.where(odd, previous[1], previous[0])
    embedded = embed_table[0][previous].reshape(CHUNKS, step, width)

    order = hidden_index ^ jnp.array([i & ~pair_bit for i in range(lax.axis_size("hidden")) if not i & pair_bit])
    down_blocks = jnp.moveaxis(down_weight[0].reshape(-1, lax.axis_size("hidden"), local_width), 1, 0)
    down_kept = [lax.dynamic_index_in_dim(down_blocks, o, 0, False) for o in order]
    down_sent = [lax.dynamic_index_in_dim(down_blocks, o ^ pair_bit, 0, False) for o in order]

    results = []
    for c in range(CHUNKS):
        sent = dot(sent_rows[c], proj_weight[0]).astype(BF16)
        arrived = swap(sent, "hidden", pair_bit)
        total = dot(kept_rows[c], proj_weight[0]) + arrived.astype(F32)
        for bit in far_bits:
            total = total + swap(total.astype(BF16), "hidden", bit).astype(F32)
        x_zero = total + embedded[c].astype(F32)
        normed = normalize(x_zero, norm_gain[0]).astype(BF16)
        triples = [
            jnp.einsum("rd,kdc->krc", normed, piece, preferred_element_type=F32).astype(BF16)
            for piece in qkv_pieces
        ]
        triple = jnp.concatenate(triples, axis=2)
        query, kv = triple[0], triple[1:]
        kvs = {0: kv}
        for bit in reversed(bits_of("codebook")):
            kvs.update({slot ^ bit: swap(block, "codebook", bit) for slot, block in kvs.items()})
        slots = tuple(kvs)
        part, part_sent = attend(
            code_index, query, slots, [kvs[s] for s in slots], out_pieces, head_size
        )
        total = part
        part_sent = part_sent
        for i, bit in enumerate(far_bits):
            total = total + swap(part_sent if i == 0 else total.astype(BF16), "hidden", bit).astype(F32)
        residual = x_zero + total
        other = swap(residual.astype(BF16), "hidden", pair_bit).astype(F32)
        sums_kept, sums_sent = [], []
        for rows in (residual, other):
            normed_two = normalize(rows, norm_gain[1]).astype(BF16)
            gate_sum = dot(normed_two, gate_up[0, 0])
            upper_sum = dot(normed_two, gate_up[0, 1])
            activated = (jax.nn.silu(gate_sum) * upper_sum).astype(BF16)
            sums_sent.append(jnp.stack([dot(activated, w) for w in down_sent]).astype(BF16))
            sums_kept.append(jnp.stack([dot(activated, w) for w in down_kept]))
        arrived = swap(jnp.stack(sums_sent), "hidden", pair_bit).astype(F32)
        sums = jnp.stack(sums_kept) + arrived[::-1]
        blocks = sums.shape[1]
        for bit in far_bits[::-1]:
            blocks //= 2
            sums = sums[:, :blocks] + swap(sums[:, blocks:].astype(BF16), "hidden", bit).astype(F32)
        sums = sums[:, 0]
        start = hidden_index * local_width
        own = lax.dynamic_slice_in_dim(residual, start, local_width, 1) + sums[0]
        far = lax.dynamic_slice_in_dim(other, start, local_width, 1) + sums[1]
        results.append(jnp.stack([jnp.where(odd, far, own), jnp.where(odd, own, far)]))
    return jnp.stack(results, axis=1).reshape(1, row_count, local_width)


def solution(mesh):
    placed = (
        P(("frames", "codebook"), "hidden"),
        P("frames", "codebook"),
        P("codebook", "hidden", None),
        P("codebook", None, None),
        P("codebook", None, None, "hidden"),
        P("codebook", "hidden", None),
        P("codebook", None, None, "hidden"),
        P("codebook", "hidden", None),
        P("codebook", None, None),
    )
    return jax.shard_map(
        body,
        mesh=mesh,
        in_specs=placed,
        out_specs=P("codebook", "frames", "hidden"),
        check_vma=False,
    )
```

time: 232 us -> 166 us (0.72)
  waiting for transfers between devices: 172 us -> 87.2 us
  starting transfers between devices: 2.34 us -> 27.1 us
  between operations: 13.6 us -> 5.8 us
  Pallas kernels: 0 us -> 4.09 us
  other arithmetic: 10.3 us -> 7.38 us
    psum x2 -> x0, waiting for transfers between devices: 95.4 us -> none  [the longest x1 51.9 us: body(): lax.psum(attention_part.astype(jnp.bfloat16), 'hidden').astype(jnp.float32)]
    ppermute x0 -> x24, waiting for transfers between devices: none -> 87.2 us  [swap(): return lax.ppermute(block, axis, [(i, i ^ distance) for i in range(count)])]
    all_gather x3 -> x0, waiting for transfers between devices: 48.6 us -> none  [the longest x1 21 us: body(): lax.all_gather(temporal, 'codebook', axis=0, tiled=True)]
    reduce_scatter x1 -> x0, waiting for transfers between devices: 26.7 us -> none  [body(): lax.psum_scatter(down_part.astype(jnp.bfloat16), 'hidden', scatter_dimens...]
    ppermute x0 -> x24, starting transfers between devices: none -> 25.6 us  [swap(): return lax.ppermute(block, axis, [(i, i ^ distance) for i in range(count)])]
    slice x4 -> x3, local copies, waits for them, and re-layouts: 4.42 us -> 0.04 us  [the longest x2 0.03 us: body(): sums[:, blocks:].astype(BF16)]
    pallas_call x0 -> x2, Pallas kernels: none -> 4.09 us  [attend(): pl.pallas_call(functools.partial(attend_kernel, slots, head_size), grid=(...]
    dynamic_slice x0 -> x3, local copies, waits for them, and re-layouts: none -> 4.05 us  [the longest x2 2.38 us: body(): lax.dynamic_slice_in_dim(qkv_weight[0], frame_index * share, share, 2)]
  transfers between devices with their start and end apart: 7 -> 25, of which waited for: 7 -> 14; matrix products, arithmetic and copies ran while one was open for 5% -> 19% of each run, Pallas kernels for 0% -> 2%
where the time goes in v1:
time: 166 us; the launch traced here: 165 us
  waiting for transfers between devices  87.2 us (53%)
  starting transfers between devices  27.1 us (16%)
  matrix products  17.7 us (11%)
  local copies, waits for them, and re-layouts  15.9 us (10%)
  other arithmetic  7.38 us (4%)
  between operations  5.8 us (3%)
  Pallas kernels  4.09 us (2%)
    ppermute x24, waiting for transfers between devices, swap(): return lax.ppermute(block, axis, [(i, i ^ distance) for i in range(count)])  87.2 us
    ppermute x24, starting transfers between devices, swap(): return lax.ppermute(block, axis, [(i, i ^ distance) for i in range(count)])  25.6 us
    dot_general x28, matrix products, dot(): return jnp.dot(a, b, preferred_element_type=F32)  12.7 us
    unnamed x35, local copies, waits for them, and re-layouts  6 us
    dot_general x6, matrix products, body(): jnp.einsum('rd,kdc->krc', normed, piece, preferred_element_type=F32)  4.99 us
    gather x1, local copies, waits for them, and re-layouts, body(): embedded = embed_table[0][previous].reshape(CHUNKS, step, width)  4.29 us
    pallas_call x2, Pallas kernels, attend(): pl.pallas_call(functools.partial(attend_kernel, slots, head_size), grid=(...  4.09 us
    reduce_sum x5, other arithmetic, normalize(): jnp.mean(values * values, axis=-1, keepdims=True) + 1e-05  3.4 us
  transfers between devices with their start and end apart: 25, of which 14 were waited for; matrix products, arithmetic and copies ran while one was open for 19% of the time, Pallas kernels for 2%

profile of v1, /device:TPU:0, one launch (start us, length us, event | category | flops | bytes accessed | tf_op | source)
XLA Modules:
  0.0 165.1 jit_solution(11459240059135527703)
XLA Ops:
  0.0 2.9 %collective-permute-start = (bf16[1,128,1024]{2,1,0:T(8,128)(2,1)}, bf16[1,128,1024]{2,1,0:T(8,128)(2,1)}, u32[]{:S(2)}, u32[]{:S(2)}) collective-permute-start(bf16[1,128,1024]{2,1,0:T(8,128)(2,1)} %bitcast.312), channel_id=1, source_target_pairs={{0,8},{4,12},{8,0},{12,4},{1,9},{5,13},{9,1},{13,5},{2,10},{6,14},... | collective-permute-start | bytes 786440 | tf_op jit(solution)/shard_map/ppermute | solution.py:19
  15.2 1.8 %collective-permute-start.2 = (bf16[128,1024]{1,0:T(8,128)(2,1)S(1)}, bf16[128,1024]{1,0:T(8,128)(2,1)S(1)}, u32[]{:S(2)}, u32[]{:S(2)}) collective-permute-start(bf16[128,1024]{1,0:T(8,128)(2,1)S(1)} %fusion.48), channel_id=1, source_target_pairs={{0,1},{1,0},{2,3},{3,2},{4,5},{5,4},{6,7},{7,6},{8,9},{9,8},{10,11... | collective-permute-start | bytes 786440 | tf_op jit(solution)/shard_map/ppermute | solution.py:19
  17.9 20.0 %collective-permute-done.2 = bf16[128,1024]{1,0:T(8,128)(2,1)S(1)} collective-permute-done((bf16[128,1024]{1,0:T(8,128)(2,1)S(1)}, bf16[128,1024]{1,0:T(8,128)(2,1)S(1)}, u32[]{:S(2)}, u32[]{:S(2)}) %collective-permute-start.2) | collective-permute-done | bytes 262176 | tf_op jit(solution)/shard_map/ppermute | solution.py:19
  39.0 2.4 %collective-permute-start.3 = (bf16[128,1024]{1,0:T(8,128)(2,1)}, bf16[128,1024]{1,0:T(8,128)(2,1)}, u32[]{:S(2)}, u32[]{:S(2)}) collective-permute-start(bf16[128,1024]{1,0:T(8,128)(2,1)} %get-tuple-element.39), channel_id=1, source_target_pairs={{0,2},{1,3},{2,0},{3,1},{4,6},{5,7},{6,4},{7,5},{8,10},{9,11},{10,... | collective-permute-start | bytes 786440 | tf_op jit(solution)/shard_map/ppermute | solution.py:19
  41.4 4.6 %collective-permute-done.16 = bf16[128,1024]{1,0:T(8,128)(2,1)S(1)} collective-permute-done((bf16[128,1024]{1,0:T(8,128)(2,1)S(1)}, bf16[128,1024]{1,0:T(8,128)(2,1)S(1)}, u32[]{:S(2)}, u32[]{:S(2)}) %collective-permute-start.16) | collective-permute-done | bytes 262176 | tf_op jit(solution)/shard_map/ppermute | solution.py:19
  47.4 4.3 %gather_fusion = bf16[256,1024]{1,0:T(8,128)(2,1)S(1)} fusion(bf16[2049,1024]{1,0:T(8,128)(2,1)} %bitcast.310, s32[1024]{0:T(1024)S(1)} %pad_clamp_fusion), kind=kCustom, calls=%fused_computation | custom fusion | bytes 1049600 | tf_op jit(solution)/shard_map/gather | solution.py:165
  53.1 7.4 %collective-permute-done.3 = bf16[128,1024]{1,0:T(8,128)(2,1)} collective-permute-done((bf16[128,1024]{1,0:T(8,128)(2,1)}, bf16[128,1024]{1,0:T(8,128)(2,1)}, u32[]{:S(2)}, u32[]{:S(2)}) %collective-permute-start.3) | collective-permute-done | bytes 262176 | tf_op jit(solution)/shard_map/ppermute | solution.py:19
  60.6 5.1 %collective-permute-done.17 = bf16[128,1024]{1,0:T(8,128)(2,1)} collective-permute-done((bf16[128,1024]{1,0:T(8,128)(2,1)}, bf16[128,1024]{1,0:T(8,128)(2,1)}, u32[]{:S(2)}, u32[]{:S(2)}) %collective-permute-start.17) | collective-permute-done | bytes 262176 | tf_op jit(solution)/shard_map/ppermute | solution.py:19
  67.6 2.0 %fusion.80 = bf16[3,128,128]{2,1,0:T(8,128)(2,1)S(1)} fusion(bf16[3,1024,128]{1,2,0:T(8,128)(2,1)} %collective-permute-done.5, bf16[128,1024,1]{1,0,2:T(8,128)(2,1)S(1)} %get-tuple-element.36), kind=kOutput, calls=%fused_computation.65 | convolution fusion | flops 100712448 | bytes 1146880 | tf_op jit(solution)/shard_map/rd,kdc->krc/dot_general | solution.py:182
  72.9 2.1 %collective-permute-start.7 = (bf16[2,128,512]{2,1,0:T(8,128)(2,1)S(1)}, bf16[2,128,512]{2,1,0:T(8,128)(2,1)}, u32[]{:S(2)}, u32[]{:S(2)}) collective-permute-start(bf16[2,128,512]{2,1,0:T(8,128)(2,1)S(1)} %pad_maximum_fusion.4.refs_0_), channel_id=1, source_target_pairs={{0,8},{4,12},{8,0},{12,4},{1,9},{5,13},{9,1},{13,5},{2,10},{6,14},... | collective-permute-start | bytes 786440 | tf_op jit(solution)/shard_map/ppermute | solution.py:19
  76.6 5.1 %collective-permute-done.18.refs_1_ = bf16[2,128,512]{2,1,0:T(8,128)(2,1)S(1)} collective-permute-done((bf16[2,128,512]{2,1,0:T(8,128)(2,1)S(1)}, bf16[2,128,512]{2,1,0:T(8,128)(2,1)S(1)}, u32[]{:S(2)}, u32[]{:S(2)}) %collective-permute-start.18) | collective-permute-done | bytes 262176 | tf_op jit(solution)/shard_map/ppermute | solution.py:19
  82.2 3.8 %collective-permute-done.7.refs_1_ = bf16[2,128,512]{2,1,0:T(8,128)(2,1)} collective-permute-done((bf16[2,128,512]{2,1,0:T(8,128)(2,1)S(1)}, bf16[2,128,512]{2,1,0:T(8,128)(2,1)}, u32[]{:S(2)}, u32[]{:S(2)}) %collective-permute-start.7) | collective-permute-done | bytes 262176 | tf_op jit(solution)/shard_map/ppermute | solution.py:19
  88.7 1.9 %collective-permute-start.21 = (bf16[128,1024]{1,0:T(8,128)(2,1)}, bf16[128,1024]{1,0:T(8,128)(2,1)}, u32[]{:S(2)}, u32[]{:S(2)}) collective-permute-start(bf16[128,1024]{1,0:T(8,128)(2,1)} %get-tuple-element.12), channel_id=1, source_target_pairs={{0,2},{1,3},{2,0},{3,1},{4,6},{5,7},{6,4},{7,5},{8,10},{9,11},{10,... | collective-permute-start | bytes 786440 | tf_op jit(solution)/shard_map/ppermute | solution.py:19
  95.0 4.1 %copy.25 = bf16[1,1024,1024]{1,2,0:T(8,128)(2,1)} copy(bf16[1,1024,1024]{2,1,0:T(8,128)(2,1)} %param.17) | data formatting | bytes 4194304 | tf_op args[7]
  101.4 2.3 %attend.2 = (f32[128,1024]{1,0:T(8,128)S(1)}, bf16[128,1024]{1,0:T(8,128)(2,1)S(1)}) custom-call(s32[1]{0:T(128)} %bitcast.11.code_ref, bf16[128,512]{1,0:T(8,128)(2,1)S(1)} %maximum_bitcast_fusion.8.query_ref, bf16[2,128,512]{2,1,0:T(8,128)(2,1)S(1)} %pad_maximum_fusion.4.refs_0_, bf16[2,128,512]{2,1,0:T(8,128)(2,1)} %collective-permute-done.7.refs_1_, ...), custom_call_target="tpu_custom_call" | custom-call | tf_op jit(solution)/shard_map/attend/pallas_call | solution.py:104
  106.1 12.6 %collective-permute-done.12 = bf16[128,1024]{1,0:T(8,128)(2,1)S(1)} collective-permute-done((bf16[128,1024]{1,0:T(8,128)(2,1)S(1)}, bf16[128,1024]{1,0:T(8,128)(2,1)S(1)}, u32[]{:S(2)}, u32[]{:S(2)}) %collective-permute-start.12) | collective-permute-done | bytes 262176 | tf_op jit(solution)/shard_map/ppermute | solution.py:19
  124.1 2.0 %collective-permute-start.13 = (bf16[128,1024]{1,0:T(8,128)(2,1)S(1)}, bf16[128,1024]{1,0:T(8,128)(2,1)S(1)}, u32[]{:S(2)}, u32[]{:S(2)}) collective-permute-start(bf16[128,1024]{1,0:T(8,128)(2,1)S(1)} %convert_element_type.173), channel_id=1, source_target_pairs={{0,1},{1,0},{2,3},{3,2},{4,5},{5,4},{6,7},{7,6},{8,9},{9,8},{10,11... | collective-permute-start | bytes 786440 | tf_op jit(solution)/shard_map/ppermute | solution.py:19
  126.9 6.5 %collective-permute-done.22 = bf16[128,1024]{1,0:T(8,128)(2,1)S(1)} collective-permute-done((bf16[128,1024]{1,0:T(8,128)(2,1)S(1)}, bf16[128,1024]{1,0:T(8,128)(2,1)S(1)}, u32[]{:S(2)}, u32[]{:S(2)}) %collective-permute-start.22) | collective-permute-done | bytes 262176 | tf_op jit(solution)/shard_map/ppermute | solution.py:19
  135.2 2.1 %collective-permute-done.13 = bf16[128,1024]{1,0:T(8,128)(2,1)S(1)} collective-permute-done((bf16[128,1024]{1,0:T(8,128)(2,1)S(1)}, bf16[128,1024]{1,0:T(8,128)(2,1)S(1)}, u32[]{:S(2)}, u32[]{:S(2)}) %collective-permute-start.13) | collective-permute-done | bytes 262176 | tf_op jit(solution)/shard_map/ppermute | solution.py:19
  140.6 1.8 %collective-permute-start.23 = (bf16[2,2,128,256]{3,2,1,0:T(8,128)(2,1)S(1)}, bf16[2,2,128,256]{3,2,1,0:T(8,128)(2,1)S(1)}, u32[]{:S(2)}, u32[]{:S(2)}) collective-permute-start(bf16[2,2,128,256]{3,2,1,0:T(8,128)(2,1)S(1)} %maximum_maximum_fusion.1), channel_id=1, source_target_pairs={{0,1},{1,0},{2,3},{3,2},{4,5},{5,4},{6,7},{7,6},{8,9},{9,8},{10,11... | collective-permute-start | bytes 786440 | tf_op jit(solution)/shard_map/ppermute | solution.py:19
  142.8 8.2 %collective-permute-done.14 = bf16[2,2,128,256]{3,2,1,0:T(8,128)(2,1)S(1)} collective-permute-done((bf16[2,2,128,256]{3,2,1,0:T(8,128)(2,1)S(1)}, bf16[2,2,128,256]{3,2,1,0:T(8,128)(2,1)S(1)}, u32[]{:S(2)}, u32[]{:S(2)}) %collective-permute-start.14) | collective-permute-done | bytes 262176 | tf_op jit(solution)/shard_map/ppermute | solution.py:19
  151.3 2.7 %collective-permute-done.23 = bf16[2,2,128,256]{3,2,1,0:T(8,128)(2,1)S(1)} collective-permute-done((bf16[2,2,128,256]{3,2,1,0:T(8,128)(2,1)S(1)}, bf16[2,2,128,256]{3,2,1,0:T(8,128)(2,1)S(1)}, u32[]{:S(2)}, u32[]{:S(2)}) %collective-permute-start.23) | collective-permute-done | bytes 262176 | tf_op jit(solution)/shard_map/ppermute | solution.py:19
  154.1 2.6 %collective-permute-start.24 = (bf16[2,1,128,256]{3,2,1,0:T(8,128)(2,1)S(1)}, bf16[2,1,128,256]{3,2,1,0:T(8,128)(2,1)S(1)}, u32[]{:S(2)}, u32[]{:S(2)}) collective-permute-start(bf16[2,1,128,256]{3,2,1,0:T(8,128)(2,1)S(1)} %slice.260), channel_id=1, source_target_pairs={{0,2},{1,3},{2,0},{3,1},{4,6},{5,7},{6,4},{7,5},{8,10},{9,11},{10,... | collective-permute-start | bytes 393224 | tf_op jit(solution)/shard_map/ppermute | solution.py:19
  156.7 5.9 %collective-permute-done.15 = bf16[2,1,128,256]{3,2,1,0:T(8,128)(2,1)S(1)} collective-permute-done((bf16[2,1,128,256]{3,2,1,0:T(8,128)(2,1)S(1)}, bf16[2,1,128,256]{3,2,1,0:T(8,128)(2,1)S(1)}, u32[]{:S(2)}, u32[]{:S(2)}) %collective-permute-start.15) | collective-permute-done | bytes 131104 | tf_op jit(solution)/shard_map/ppermute | solution.py:19
  (151 shorter events, 44.9 us)
Async XLA Ops:
  0.0 10.5 %collective-permute-start = (bf16[1,128,1024]{2,1,0:T(8,128)(2,1)}, bf16[1,128,1024]{2,1,0:T(8,128)(2,1)}, u32[]{:S(2)}, u32[]{:S(2)}) collective-permute-start(bf16[1,128,1024]{2,1,0:T(8,128)(2,1)} %bitcast.312), channel_id=1, source_target_pairs={{0,8},{4,12},{8,0},{12,4},{1,9},{5,13},{9,1},{13,5},{2,10},{6,14},... | collective-permute-start | bytes 786440 | tf_op jit(solution)/shard_map/ppermute | solution.py:19
  2.9 9.9 %collective-permute-start.4 = (s32[512,1]{0,1:T(1,128)}, s32[512,1]{0,1:T(1,128)S(1)}, u32[]{:S(2)}, u32[]{:S(2)}) collective-permute-start(s32[512,1]{0,1:T(1,128)} %param.11), channel_id=1, source_target_pairs={{0,4},{4,8},{8,12},{1,5},{5,9},{9,13},{2,6},{6,10},{10,14},{3,7},{... | collective-permute-start | bytes 6152 | tf_op jit(solution)/shard_map/ppermute | solution.py:30
  6.1 68.9 %collective-permute-start.10 = (bf16[128,1024]{1,0:T(8,128)(2,1)}, bf16[128,1024]{1,0:T(8,128)(2,1)S(1)}, u32[]{:S(2)}, u32[]{:S(2)}) collective-permute-start(bf16[128,1024]{1,0:T(8,128)(2,1)} %dynamic-slice_bitcast_fusion), channel_id=1, source_target_pairs={{0,1},{1,0},{2,3},{3,2},{4,5},{5,4},{6,7},{7,6},{8,9},{9,8},{10,11... | collective-permute-start | bytes 786440 | tf_op jit(solution)/shard_map/ppermute | solution.py:19
  10.0 41.6 %collective-permute-start.5 = (bf16[3,1024,128]{1,2,0:T(8,128)(2,1)}, bf16[3,1024,128]{1,2,0:T(8,128)(2,1)}, u32[]{:S(2)}, u32[]{:S(2)}) collective-permute-start(bf16[3,1024,128]{1,2,0:T(8,128)(2,1)} %bitcast.311), channel_id=1, source_target_pairs={{0,1},{1,0},{2,3},{3,2},{4,5},{5,4},{6,7},{7,6},{8,9},{9,8},{10,11... | collective-permute-start | bytes 2359304 | tf_op jit(solution)/shard_map/ppermute | solution.py:19
  15.2 22.6 %collective-permute-start.2 = (bf16[128,1024]{1,0:T(8,128)(2,1)S(1)}, bf16[128,1024]{1,0:T(8,128)(2,1)S(1)}, u32[]{:S(2)}, u32[]{:S(2)}) collective-permute-start(bf16[128,1024]{1,0:T(8,128)(2,1)S(1)} %fusion.48), channel_id=1, source_target_pairs={{0,1},{1,0},{2,3},{3,2},{4,5},{5,4},{6,7},{7,6},{8,9},{9,8},{10,11... | collective-permute-start | bytes 786440 | tf_op jit(solution)/shard_map/ppermute | solution.py:19
  17.5 28.5 %collective-permute-start.16 = (bf16[128,1024]{1,0:T(8,128)(2,1)S(1)}, bf16[128,1024]{1,0:T(8,128)(2,1)S(1)}, u32[]{:S(2)}, u32[]{:S(2)}) collective-permute-start(bf16[128,1024]{1,0:T(8,128)(2,1)S(1)} %fusion.51), channel_id=1, source_target_pairs={{0,1},{1,0},{2,3},{3,2},{4,5},{5,4},{6,7},{7,6},{8,9},{9,8},{10,11... | collective-permute-start | bytes 786440 | tf_op jit(solution)/shard_map/ppermute | solution.py:19
  39.0 21.6 %collective-permute-start.3 = (bf16[128,1024]{1,0:T(8,128)(2,1)}, bf16[128,1024]{1,0:T(8,128)(2,1)}, u32[]{:S(2)}, u32[]{:S(2)}) collective-permute-start(bf16[128,1024]{1,0:T(8,128)(2,1)} %get-tuple-element.39), channel_id=1, source_target_pairs={{0,2},{1,3},{2,0},{3,1},{4,6},{5,7},{6,4},{7,5},{8,10},{9,11},{10,... | collective-permute-start | bytes 786440 | tf_op jit(solution)/shard_map/ppermute | solution.py:19
  47.3 18.4 %collective-permute-start.17 = (bf16[128,1024]{1,0:T(8,128)(2,1)}, bf16[128,1024]{1,0:T(8,128)(2,1)}, u32[]{:S(2)}, u32[]{:S(2)}) collective-permute-start(bf16[128,1024]{1,0:T(8,128)(2,1)} %get-tuple-element.41), channel_id=1, source_target_pairs={{0,2},{1,3},{2,0},{3,1},{4,6},{5,7},{6,4},{7,5},{8,10},{9,11},{10,... | collective-permute-start | bytes 786440 | tf_op jit(solution)/shard_map/ppermute | solution.py:19
  51.7 20.3 %collective-permute-start.6 = (bf16[3,1024,128]{1,2,0:T(8,128)(2,1)}, bf16[3,1024,128]{1,2,0:T(8,128)(2,1)S(1)}, u32[]{:S(2)}, u32[]{:S(2)}) collective-permute-start(bf16[3,1024,128]{1,2,0:T(8,128)(2,1)} %collective-permute-done.5), channel_id=1, source_target_pairs={{0,16},{16,0},{1,17},{17,1},{2,18},{18,2},{3,19},{19,3},{4,20},{20... | collective-permute-start | bytes 2359304 | tf_op jit(solution)/shard_map/ppermute | solution.py:19
  72.4 9.3 %collective-permute-start.18 = (bf16[2,128,512]{2,1,0:T(8,128)(2,1)S(1)}, bf16[2,128,512]{2,1,0:T(8,128)(2,1)S(1)}, u32[]{:S(2)}, u32[]{:S(2)}) collective-permute-start(bf16[2,128,512]{2,1,0:T(8,128)(2,1)S(1)} %pad_maximum_fusion.2.refs_0_), channel_id=1, source_target_pairs={{0,8},{4,12},{8,0},{12,4},{1,9},{5,13},{9,1},{13,5},{2,10},{6,14},... | collective-permute-start | bytes 786440 | tf_op jit(solution)/shard_map/ppermute | solution.py:19
  72.9 13.1 %collective-permute-start.7 = (bf16[2,128,512]{2,1,0:T(8,128)(2,1)S(1)}, bf16[2,128,512]{2,1,0:T(8,128)(2,1)}, u32[]{:S(2)}, u32[]{:S(2)}) collective-permute-start(bf16[2,128,512]{2,1,0:T(8,128)(2,1)S(1)} %pad_maximum_fusion.4.refs_0_), channel_id=1, source_target_pairs={{0,8},{4,12},{8,0},{12,4},{1,9},{5,13},{9,1},{13,5},{2,10},{6,14},... | collective-permute-start | bytes 786440 | tf_op jit(solution)/shard_map/ppermute | solution.py:19
  75.0 11.0 %collective-permute-start.11 = (bf16[128,1024]{1,0:T(8,128)(2,1)S(1)}, bf16[128,1024]{1,0:T(8,128)(2,1)S(1)}, u32[]{:S(2)}, u32[]{:S(2)}) collective-permute-start(bf16[128,1024]{1,0:T(8,128)(2,1)S(1)} %collective-permute-done.10.refs_5_), channel_id=1, source_target_pairs={{0,16},{16,0},{1,17},{17,1},{2,18},{18,2},{3,19},{19,3},{4,20},{20... | collective-permute-start | bytes 786440 | tf_op jit(solution)/shard_map/ppermute | solution.py:19
  76.6 9.5 %collective-permute-start.19 = (bf16[2,128,512]{2,1,0:T(8,128)(2,1)S(1)}, bf16[2,128,512]{2,1,0:T(8,128)(2,1)S(1)}, u32[]{:S(2)}, u32[]{:S(2)}) collective-permute-start(bf16[2,128,512]{2,1,0:T(8,128)(2,1)S(1)} %pad_maximum_fusion.2.refs_0_), channel_id=1, source_target_pairs={{0,4},{4,0},{8,12},{12,8},{1,5},{5,1},{9,13},{13,9},{2,6},{6,2},{1... | collective-permute-start | bytes 786440 | tf_op jit(solution)/shard_map/ppermute | solution.py:19
  81.7 4.4 %collective-permute-start.20 = (bf16[2,128,512]{2,1,0:T(8,128)(2,1)S(1)}, bf16[2,128,512]{2,1,0:T(8,128)(2,1)S(1)}, u32[]{:S(2)}, u32[]{:S(2)}) collective-permute-start(bf16[2,128,512]{2,1,0:T(8,128)(2,1)S(1)} %collective-permute-done.18.refs_1_), channel_id=1, source_target_pairs={{0,4},{4,0},{8,12},{12,8},{1,5},{5,1},{9,13},{13,9},{2,6},{6,2},{1... | collective-permute-start | bytes 786440 | tf_op jit(solution)/shard_map/ppermute | solution.py:19
  81.7 19.7 %collective-permute-start.8 = (bf16[2,128,512]{2,1,0:T(8,128)(2,1)S(1)}, bf16[2,128,512]{2,1,0:T(8,128)(2,1)}, u32[]{:S(2)}, u32[]{:S(2)}) collective-permute-start(bf16[2,128,512]{2,1,0:T(8,128)(2,1)S(1)} %pad_maximum_fusion.4.refs_0_), channel_id=1, source_target_pairs={{0,4},{4,0},{8,12},{12,8},{1,5},{5,1},{9,13},{13,9},{2,6},{6,2},{1... | collective-permute-start | bytes 786440 | tf_op jit(solution)/shard_map/ppermute | solution.py:19
  86.0 15.4 %collective-permute-start.9 = (bf16[2,128,512]{2,1,0:T(8,128)(2,1)}, bf16[2,128,512]{2,1,0:T(8,128)(2,1)}, u32[]{:S(2)}, u32[]{:S(2)}) collective-permute-start(bf16[2,128,512]{2,1,0:T(8,128)(2,1)} %collective-permute-done.7.refs_1_), channel_id=1, source_target_pairs={{0,4},{4,0},{8,12},{12,8},{1,5},{5,1},{9,13},{13,9},{2,6},{6,2},{1... | collective-permute-start | bytes 786440 | tf_op jit(solution)/shard_map/ppermute | solution.py:19
  88.7 16.1 %collective-permute-start.21 = (bf16[128,1024]{1,0:T(8,128)(2,1)}, bf16[128,1024]{1,0:T(8,128)(2,1)}, u32[]{:S(2)}, u32[]{:S(2)}) collective-permute-start(bf16[128,1024]{1,0:T(8,128)(2,1)} %get-tuple-element.12), channel_id=1, source_target_pairs={{0,2},{1,3},{2,0},{3,1},{4,6},{5,7},{6,4},{7,5},{8,10},{9,11},{10,... | collective-permute-start | bytes 786440 | tf_op jit(solution)/shard_map/ppermute | solution.py:19
  103.7 15.0 %collective-permute-start.12 = (bf16[128,1024]{1,0:T(8,128)(2,1)S(1)}, bf16[128,1024]{1,0:T(8,128)(2,1)S(1)}, u32[]{:S(2)}, u32[]{:S(2)}) collective-permute-start(bf16[128,1024]{1,0:T(8,128)(2,1)S(1)} %get-tuple-element.10), channel_id=1, source_target_pairs={{0,2},{1,3},{2,0},{3,1},{4,6},{5,7},{6,4},{7,5},{8,10},{9,11},{10,... | collective-permute-start | bytes 786440 | tf_op jit(solution)/shard_map/ppermute | solution.py:19
  124.1 9.3 %collective-permute-start.22 = (bf16[128,1024]{1,0:T(8,128)(2,1)S(1)}, bf16[128,1024]{1,0:T(8,128)(2,1)S(1)}, u32[]{:S(2)}, u32[]{:S(2)}) collective-permute-start(bf16[128,1024]{1,0:T(8,128)(2,1)S(1)} %convert_element_type.194), channel_id=1, source_target_pairs={{0,1},{1,0},{2,3},{3,2},{4,5},{5,4},{6,7},{7,6},{8,9},{9,8},{10,11... | collective-permute-start | bytes 786440 | tf_op jit(solution)/shard_map/ppermute | solution.py:19
  124.1 13.2 %collective-permute-start.13 = (bf16[128,1024]{1,0:T(8,128)(2,1)S(1)}, bf16[128,1024]{1,0:T(8,128)(2,1)S(1)}, u32[]{:S(2)}, u32[]{:S(2)}) collective-permute-start(bf16[128,1024]{1,0:T(8,128)(2,1)S(1)} %convert_element_type.173), channel_id=1, source_target_pairs={{0,1},{1,0},{2,3},{3,2},{4,5},{5,4},{6,7},{7,6},{8,9},{9,8},{10,11... | collective-permute-start | bytes 786440 | tf_op jit(solution)/shard_map/ppermute | solution.py:19
  140.2 10.7 %collective-permute-start.14 = (bf16[2,2,128,256]{3,2,1,0:T(8,128)(2,1)S(1)}, bf16[2,2,128,256]{3,2,1,0:T(8,128)(2,1)S(1)}, u32[]{:S(2)}, u32[]{:S(2)}) collective-permute-start(bf16[2,2,128,256]{3,2,1,0:T(8,128)(2,1)S(1)} %maximum_maximum_fusion), channel_id=1, source_target_pairs={{0,1},{1,0},{2,3},{3,2},{4,5},{5,4},{6,7},{7,6},{8,9},{9,8},{10,11... | collective-permute-start | bytes 786440 | tf_op jit(solution)/shard_map/ppermute | solution.py:19
  140.6 13.4 %collective-permute-start.23 = (bf16[2,2,128,256]{3,2,1,0:T(8,128)(2,1)S(1)}, bf16[2,2,128,256]{3,2,1,0:T(8,128)(2,1)S(1)}, u32[]{:S(2)}, u32[]{:S(2)}) collective-permute-start(bf16[2,2,128,256]{3,2,1,0:T(8,128)(2,1)S(1)} %maximum_maximum_fusion.1), channel_id=1, source_target_pairs={{0,1},{1,0},{2,3},{3,2},{4,5},{5,4},{6,7},{7,6},{8,9},{9,8},{10,11... | collective-permute-start | bytes 786440 | tf_op jit(solution)/shard_map/ppermute | solution.py:19
  151.1 11.5 %collective-permute-start.15 = (bf16[2,1,128,256]{3,2,1,0:T(8,128)(2,1)S(1)}, bf16[2,1,128,256]{3,2,1,0:T(8,128)(2,1)S(1)}, u32[]{:S(2)}, u32[]{:S(2)}) collective-permute-start(bf16[2,1,128,256]{3,2,1,0:T(8,128)(2,1)S(1)} %slice.261), channel_id=1, source_target_pairs={{0,2},{1,3},{2,0},{3,1},{4,6},{5,7},{6,4},{7,5},{8,10},{9,11},{10,... | collective-permute-start | bytes 393224 | tf_op jit(solution)/shard_map/ppermute | solution.py:19
  154.1 9.8 %collective-permute-start.24 = (bf16[2,1,128,256]{3,2,1,0:T(8,128)(2,1)S(1)}, bf16[2,1,128,256]{3,2,1,0:T(8,128)(2,1)S(1)}, u32[]{:S(2)}, u32[]{:S(2)}) collective-permute-start(bf16[2,1,128,256]{3,2,1,0:T(8,128)(2,1)S(1)} %slice.260), channel_id=1, source_target_pairs={{0,2},{1,3},{2,0},{3,1},{4,6},{5,7},{6,4},{7,5},{8,10},{9,11},{10,... | collective-permute-start | bytes 393224 | tf_op jit(solution)/shard_map/ppermute | solution.py:19
  (18 other events, 125.5 us)

commit v2 on v0

v2 whole, which is shorter than its diff:
```python
import functools

import jax
import jax.numpy as jnp
from jax import lax
from jax.experimental import pallas as pl
from jax.experimental.pallas import tpu as pltpu
from jax.sharding import PartitionSpec as P

HEADS = 16
CHUNKS = 2
F32 = jnp.float32
BF16 = jnp.bfloat16


def swap(block, axis, distance):
    count = lax.axis_size(axis)
    return lax.ppermute(block, axis, [(i, i ^ distance) for i in range(count)])


def bits_of(axis):
    count = lax.axis_size(axis)
    return [1 << b for b in range(count.bit_length() - 1)]


def shifted(block, axis, distance):
    devices = range(lax.axis_size(axis))
    route = [(i - distance, i) for i in devices if i - distance in devices]
    return lax.ppermute(block, axis, route)


def slots_of(block, axis):
    slots = {0: block}
    for bit in reversed(bits_of(axis)):
        slots.update({slot ^ bit: swap(piece, axis, bit) for slot, piece in slots.items()})
    return slots


def dot(a, b):
    return jnp.dot(a, b, preferred_element_type=F32)


def normalize(values, norm_gain):
    return values * lax.rsqrt(jnp.mean(values * values, axis=-1, keepdims=True) + 1e-05) * norm_gain


def call(kernel, name, outs, args, scratch=()):
    return pl.pallas_call(
        kernel,
        name=name,
        out_shape=[jax.ShapeDtypeStruct(shape, dtype) for shape, dtype in outs],
        in_specs=[pl.BlockSpec(memory_space=pltpu.VMEM)] * len(args),
        out_specs=[pl.BlockSpec(memory_space=pltpu.VMEM)] * len(outs),
        scratch_shapes=list(scratch),
        cost_estimate=pl.CostEstimate(flops=1000, bytes_accessed=1000, transcendentals=0),
        compiler_params=pltpu.CompilerParams(vmem_limit_bytes=48 * 1024 * 1024),
    )(*args)


def row_blocks(rows):
    size = min(rows, 128)
    return [pl.ds(start, size) for start in range(0, rows, size)]


def proj_kernel(slots, chunk, flip, *refs):
    piece_refs, weight_ref, out_ref, rows_ref = refs[: len(slots)], *refs[len(slots) :]
    code = lax.axis_index("codebook")
    half = (lax.axis_index("hidden") & 1) ^ flip
    count = len(slots)
    each = count // 2 // CHUNKS
    size = piece_refs[0].shape[0]
    for i in range(each):
        wanted = code ^ (half * (count // 2) + chunk * each + i)
        for slot, piece_ref in zip(slots, piece_refs):

            @pl.when(wanted == slot)
            def _():
                rows_ref[...] = piece_ref[...]

        out_ref[pl.ds(i * size, size), :] = dot(rows_ref[...], weight_ref[0]).astype(out_ref.dtype)


def embed_kernel(chunk, ids_ref, table_ref, out_ref):
    half = lax.axis_index("hidden") & 1
    first = lax.axis_index("codebook") == 0
    rows = out_ref.shape[0]
    start_id = table_ref.shape[0] - 1
    for block in row_blocks(rows):
        offset = half * (ids_ref.shape[0] // 2) + chunk * rows + block.start
        ids = ids_ref[pl.ds(pl.multiple_of(offset, 8), block.size), :]
        ids = jnp.where(first, start_id, ids)
        token = lax.broadcasted_iota(jnp.int32, (block.size, start_id), 1)
        chosen = (token == ids).astype(F32).astype(BF16)
        started = jnp.where(ids == start_id, 1.0, 0.0) * table_ref[start_id:, :].astype(F32)
        out_ref[block, :] = (dot(chosen, table_ref[:start_id, :]) + started).astype(BF16)


def qkv_kernel(rows_ref, gain_ref, weight_ref, query_ref, kv_ref):
    for block in row_blocks(rows_ref.shape[0]):
        normed = normalize(rows_ref[block, :].astype(F32), gain_ref[0, 0:1, :]).astype(BF16)
        query_ref[block, :] = dot(normed, weight_ref[0, 0]).astype(BF16)
        kv_ref[0, block, :] = dot(normed, weight_ref[0, 1]).astype(BF16)
        kv_ref[1, block, :] = dot(normed, weight_ref[0, 2]).astype(BF16)


def attend_kernel(slots, head_size, query_ref, *refs):
    kv_refs = refs[: len(slots)]
    weight_ref, part_ref = refs[len(slots) :]
    code = lax.axis_index("codebook")
    width = query_ref.shape[-1]
    lanes = 128
    column = lax.broadcasted_iota(jnp.int32, (width, lanes), 0) // head_size
    head = lax.broadcasted_iota(jnp.int32, (width, lanes), 1)
    gather = (column == head).astype(F32).astype(BF16)
    head_t = lax.broadcasted_iota(jnp.int32, (lanes, width), 0)
    column_t = lax.broadcasted_iota(jnp.int32, (lanes, width), 1) // head_size
    spread = (column_t == head_t).astype(F32).astype(BF16)
    for block in row_blocks(query_ref.shape[0]):
        query = query_ref[block, :].astype(F32)
        scores = []
        for slot, kv_ref in zip(slots, kv_refs):
            product = query * kv_ref[0, block, :].astype(F32)
            high = product.astype(BF16)
            low = (product - high.astype(F32)).astype(BF16)
            score = (dot(high, gather) + dot(low, gather)) * head_size ** (-0.5)
            if slot:
                score = jnp.where((code ^ slot) <= code, score, -1e30)
            scores.append(score)
        highest = functools.reduce(jnp.maximum, scores)
        weights = [jnp.exp(score - highest) for score in scores]
        running = functools.reduce(jnp.add, weights)
        summed = None
        for kv_ref, weight in zip(kv_refs, weights):
            term = dot(weight.astype(BF16), spread) * kv_ref[1, block, :].astype(F32)
            summed = term if summed is None else summed + term
        inverse = 1.0 / running
        high = inverse.astype(BF16)
        low = (inverse - high.astype(F32)).astype(BF16)
        attended = (summed * (dot(high, spread) + dot(low, spread))).astype(BF16)
        part_ref[block, :] = dot(attended, weight_ref[0]).astype(part_ref.dtype)


def mlp_kernel(count, rows_ref, gain_ref, gate_up_ref, down_ref, kept_ref, sent_ref, act_ref):
    index = lax.axis_index("hidden")
    hidden = act_ref.shape[1]
    step = min(hidden, 256)
    width = kept_ref.shape[2]
    for block in row_blocks(rows_ref.shape[0]):
        normed = normalize(rows_ref[block, :].astype(F32), gain_ref[0, 1:2, :]).astype(BF16)
        for start in range(0, hidden, step):
            columns = pl.ds(start, step)
            gate_sum = dot(normed, gate_up_ref[0, 0, :, columns])
            upper_sum = dot(normed, gate_up_ref[0, 1, :, columns])
            act_ref[:, columns] = (jax.nn.silu(gate_sum) * upper_sum).astype(BF16)
        for i in range(count // 2):
            owner = index ^ (2 * i)
            columns = pl.ds(pl.multiple_of((owner ^ 1) * width, width), width)
            sent_ref[i, block, :] = dot(act_ref[...], down_ref[0, :, columns]).astype(BF16)
        for i in range(count // 2):
            owner = index ^ (2 * i)
            columns = pl.ds(pl.multiple_of(owner * width, width), width)
            total = dot(act_ref[...], down_ref[0, :, columns])
            if i == 0:
                total = total + rows_ref[block, columns].astype(F32)
            kept_ref[i, block, :] = total


def body(
    temporal,
    frame_ids,
    proj_weight,
    embed_table,
    qkv_weight,
    out_weight,
    gate_up,
    down_weight,
    norm_gains,
):
    hidden_count = lax.axis_size("hidden")
    pair_bit, *far_bits = bits_of("hidden")
    odd = (lax.axis_index("hidden") & pair_bit) != 0
    width = embed_table.shape[2]
    local_width = qkv_weight.shape[3]
    head_size = width // HEADS
    table = embed_table[0]

    pieces = slots_of(temporal, "codebook")
    slots = tuple(pieces)
    pieces = [pieces[slot] for slot in slots]
    row_count = len(slots) * temporal.shape[0]
    rows = row_count // 2 // CHUNKS
    earlier = shifted(frame_ids, "codebook", 1)

    def project(c, flip, dtype):
        return call(
            functools.partial(proj_kernel, slots, c, flip),
            "project",
            [((rows, width), dtype)],
            [*pieces, proj_weight],
            [pltpu.VMEM(temporal.shape, BF16)],
        )[0]

    def qkv(block):
        return call(
            qkv_kernel,
            "qkv",
            [((rows, local_width), BF16), ((2, rows, local_width), BF16)],
            [block, norm_gains, qkv_weight],
        )

    def attend(query, kv, dtype):
        kvs = slots_of(kv, "codebook")
        order = tuple(sorted(kvs))
        return call(
            functools.partial(attend_kernel, order, head_size),
            "attend",
            [((rows, width), dtype)],
            [query, *[kvs[slot] for slot in order], out_weight],
        )[0]

    def mlp(block):
        shape = (hidden_count // 2, rows, local_width)
        return call(
            functools.partial(mlp_kernel, hidden_count),
            "mlp",
            [(shape, F32), (shape, BF16)],
            [block, norm_gains, gate_up, down_weight],
            [pltpu.VMEM((min(rows, 128), gate_up.shape[3]), BF16)],
        )

    results = []
    for c in range(CHUNKS):
        arrived = swap(project(c, 1, BF16), "hidden", pair_bit)
        total = project(c, 0, F32) + arrived.astype(F32)
        embedded = call(
            functools.partial(embed_kernel, c), "embed", [((rows, width), BF16)], [earlier, table]
        )[0]
        for bit in far_bits:
            total = total + swap(total.astype(BF16), "hidden", bit).astype(F32)
        x_zero = total + embedded.astype(F32)
        x_other = swap(x_zero.astype(BF16), "hidden", pair_bit)
        part_own = attend(*qkv(x_zero), F32)
        part_other = attend(*qkv(x_other), BF16)
        total = part_own + swap(part_other, "hidden", pair_bit).astype(F32)
        for bit in far_bits:
            total = total + swap(total.astype(BF16), "hidden", bit).astype(F32)
        residual = x_zero + total
        other = swap(residual.astype(BF16), "hidden", pair_bit)
        own_kept, own_sent = mlp(residual)
        other_kept, other_sent = mlp(other)
        arrived = swap(jnp.stack([other_sent, own_sent]), "hidden", pair_bit).astype(F32)
        sums = jnp.stack([own_kept, other_kept]) + arrived
        blocks = sums.shape[1]
        for bit in far_bits[::-1]:
            blocks //= 2
            sums = sums[:, :blocks] + swap(sums[:, blocks:].astype(BF16), "hidden", bit).astype(F32)
        own, far = sums[0, 0], sums[1, 0]
        results.append(jnp.stack([jnp.where(odd, far, own), jnp.where(odd, own, far)]))
    return jnp.stack(results, axis=1).reshape(1, row_count, local_width)


def solution(mesh):
    placed = (
        P(("frames", "codebook"), "hidden"),
        P("frames", "codebook"),
        P("codebook", "hidden", None),
        P("codebook", None, None),
        P("codebook", None, None, "hidden"),
        P("codebook", "hidden", None),
        P("codebook", None, None, "hidden"),
        P("codebook", "hidden", None),
        P("codebook", None, None),
    )
    return jax.shard_map(
        body,
        mesh=mesh,
        in_specs=placed,
        out_specs=P("codebook", "frames", "hidden"),
        check_vma=False,
    )
```

time: 232 us -> 137 us (0.59)
  waiting for transfers between devices: 172 us -> 76.3 us
  starting transfers between devices: 2.34 us -> 30.8 us
  Pallas kernels: 0 us -> 21.5 us
  matrix products: 17 us -> 0 us
  between operations: 13.6 us -> 0.44 us
  local copies, waits for them, and re-layouts: 15.8 us -> 6.57 us
  other arithmetic: 10.3 us -> 1.17 us
    psum x2 -> x0, waiting for transfers between devices: 95.4 us -> none  [the longest x1 51.9 us: body(): lax.psum(attention_part.astype(jnp.bfloat16), 'hidden').astype(jnp.float32)]
    ppermute x0 -> x31, waiting for transfers between devices: none -> 75.1 us  [swap(): return lax.ppermute(block, axis, [(i, i ^ distance) for i in range(count)])]
    all_gather x3 -> x0, waiting for transfers between devices: 48.6 us -> none  [the longest x1 21 us: body(): lax.all_gather(temporal, 'codebook', axis=0, tiled=True)]
    ppermute x0 -> x31, starting transfers between devices: none -> 29.5 us  [swap(): return lax.ppermute(block, axis, [(i, i ^ distance) for i in range(count)])]
    reduce_scatter x1 -> x0, waiting for transfers between devices: 26.7 us -> none  [body(): lax.psum_scatter(down_part.astype(jnp.bfloat16), 'hidden', scatter_dimens...]
    pallas_call x0 -> x18, Pallas kernels: none -> 21.5 us  [call(): pl.pallas_call(kernel, name=name, out_shape=[jax.ShapeDtypeStruct(shape,...]
    dot_general x5 -> x0, matrix products: 17 us -> none  [the longest x1 6.85 us: body(): jnp.dot(activated, down_weight[0], preferred_element_type=jnp.float32)]
    gather x1 -> x0, local copies, waits for them, and re-layouts: 5.46 us -> none  [body(): token_table[previous].astype(jnp.float32)]
  transfers between devices with their start and end apart: 7 -> 32, of which waited for: 7 -> 16; matrix products, arithmetic and copies ran while one was open for 5% -> 1% of each run, Pallas kernels for 0% -> 15%
where the time goes in v2:
time: 137 us
  waiting for transfers between devices  76.3 us (56%)
  starting transfers between devices  30.8 us (22%)
  Pallas kernels  21.5 us (16%)
  local copies, waits for them, and re-layouts  6.57 us (5%)
    ppermute x31, waiting for transfers between devices, swap(): return lax.ppermute(block, axis, [(i, i ^ distance) for i in range(count)])  75.1 us
    ppermute x31, starting transfers between devices, swap(): return lax.ppermute(block, axis, [(i, i ^ distance) for i in range(count)])  29.5 us
    pallas_call x18, Pallas kernels, call(): pl.pallas_call(kernel, name=name, out_shape=[jax.ShapeDtypeStruct(shape,...  21.5 us
    unnamed x21, local copies, waits for them, and re-layouts  5.71 us
  transfers between devices with their start and end apart: 32, of which 16 were waited for; matrix products, arithmetic and copies ran while one was open for 1% of the time, Pallas kernels for 15%

profile of v2, /device:TPU:0, one launch (start us, length us, event | category | flops | bytes accessed | tf_op | source)
XLA Modules:
  0.0 136.8 jit_solution(4106324751532349729)
XLA Ops:
  0.0 2.9 %collective-permute-start = (bf16[128,1024]{1,0:T(8,128)(2,1)}, bf16[128,1024]{1,0:T(8,128)(2,1)S(1)}, u32[]{:S(2)}, u32[]{:S(2)}) collective-permute-start(bf16[128,1024]{1,0:T(8,128)(2,1)} %refs_0_.7), channel_id=1, source_target_pairs={{0,8},{4,12},{8,0},{12,4},{1,9},{5,13},{9,1},{13,5},{2,10},{6,14},... | collective-permute-start | bytes 786440 | tf_op jit(solution)/shard_map/ppermute | solution.py:18
  2.9 6.5 %collective-permute-done.refs_1_ = bf16[128,1024]{1,0:T(8,128)(2,1)S(1)} collective-permute-done((bf16[128,1024]{1,0:T(8,128)(2,1)}, bf16[128,1024]{1,0:T(8,128)(2,1)S(1)}, u32[]{:S(2)}, u32[]{:S(2)}) %collective-permute-start) | collective-permute-done | bytes 262176 | tf_op jit(solution)/shard_map/ppermute | solution.py:18
  17.1 6.1 %collective-permute-done.3 = bf16[128,1024]{1,0:T(8,128)(2,1)S(1)} collective-permute-done((bf16[128,1024]{1,0:T(8,128)(2,1)S(1)}, bf16[128,1024]{1,0:T(8,128)(2,1)S(1)}, u32[]{:S(2)}, u32[]{:S(2)}) %collective-permute-start.3) | collective-permute-done | bytes 262176 | tf_op jit(solution)/shard_map/ppermute | solution.py:18
  23.3 2.9 %collective-permute-start.4 = (bf16[128,1024]{1,0:T(8,128)(2,1)S(1)}, bf16[128,1024]{1,0:T(8,128)(2,1)S(1)}, u32[]{:S(2)}, u32[]{:S(2)}) collective-permute-start(bf16[128,1024]{1,0:T(8,128)(2,1)S(1)} %fusion), channel_id=1, source_target_pairs={{0,2},{1,3},{2,0},{3,1},{4,6},{5,7},{6,4},{7,5},{8,10},{9,11},{10,... | collective-permute-start | bytes 786440 | tf_op jit(solution)/shard_map/ppermute | solution.py:18
  28.8 2.2 %copy-done.4 = bf16[1,2049,1024]{2,1,0:T(8,128)(2,1)S(1)} copy-done((bf16[1,2049,1024]{2,1,0:T(8,128)(2,1)S(1)}, bf16[1,2049,1024]{2,1,0:T(8,128)(2,1)}, u32[]{:S(2)}) %copy-start.4) | copy-done | bytes 4196376
  34.3 2.6 %collective-permute-done.4 = bf16[128,1024]{1,0:T(8,128)(2,1)S(1)} collective-permute-done((bf16[128,1024]{1,0:T(8,128)(2,1)S(1)}, bf16[128,1024]{1,0:T(8,128)(2,1)S(1)}, u32[]{:S(2)}, u32[]{:S(2)}) %collective-permute-start.4) | collective-permute-done | bytes 262176 | tf_op jit(solution)/shard_map/ppermute | solution.py:18
  37.0 3.7 %collective-permute-start.9 = (bf16[128,1024]{1,0:T(8,128)(2,1)S(1)}, bf16[128,1024]{1,0:T(8,128)(2,1)S(1)}, u32[]{:S(2)}, u32[]{:S(2)}) collective-permute-start(bf16[128,1024]{1,0:T(8,128)(2,1)S(1)} %get-tuple-element.39), channel_id=1, source_target_pairs={{0,1},{1,0},{2,3},{3,2},{4,5},{5,4},{6,7},{7,6},{8,9},{9,8},{10,11... | collective-permute-start | bytes 786440 | tf_op jit(solution)/shard_map/ppermute | solution.py:18
  40.7 8.1 %collective-permute-done.19 = bf16[128,1024]{1,0:T(8,128)(2,1)S(1)} collective-permute-done((bf16[128,1024]{1,0:T(8,128)(2,1)S(1)}, bf16[128,1024]{1,0:T(8,128)(2,1)S(1)}, u32[]{:S(2)}, u32[]{:S(2)}) %collective-permute-start.19) | collective-permute-done | bytes 262176 | tf_op jit(solution)/shard_map/ppermute | solution.py:18
  49.1 2.5 %collective-permute-done.9.rows_ref = bf16[128,1024]{1,0:T(8,128)(2,1)S(1)} collective-permute-done((bf16[128,1024]{1,0:T(8,128)(2,1)S(1)}, bf16[128,1024]{1,0:T(8,128)(2,1)S(1)}, u32[]{:S(2)}, u32[]{:S(2)}) %collective-permute-start.9) | collective-permute-done | bytes 262176 | tf_op jit(solution)/shard_map/ppermute | solution.py:18
  52.4 4.7 %collective-permute-done.11.refs_2_ = bf16[2,128,256]{2,1,0:T(8,128)(2,1)S(1)} collective-permute-done((bf16[2,128,256]{2,1,0:T(8,128)(2,1)S(1)}, bf16[2,128,256]{2,1,0:T(8,128)(2,1)S(1)}, u32[]{:S(2)}, u32[]{:S(2)}) %collective-permute-start.11) | collective-permute-done | bytes 131104 | tf_op jit(solution)/shard_map/ppermute | solution.py:18
  64.5 2.2 %collective-permute-done.25.refs_2_ = bf16[2,128,256]{2,1,0:T(8,128)(2,1)S(1)} collective-permute-done((bf16[2,128,256]{2,1,0:T(8,128)(2,1)S(1)}, bf16[2,128,256]{2,1,0:T(8,128)(2,1)S(1)}, u32[]{:S(2)}, u32[]{:S(2)}) %collective-permute-start.25) | collective-permute-done | bytes 131104 | tf_op jit(solution)/shard_map/ppermute | solution.py:18
  66.7 2.4 %collective-permute-done.21.refs_2_ = bf16[2,128,256]{2,1,0:T(8,128)(2,1)S(1)} collective-permute-done((bf16[2,128,256]{2,1,0:T(8,128)(2,1)S(1)}, bf16[2,128,256]{2,1,0:T(8,128)(2,1)S(1)}, u32[]{:S(2)}, u32[]{:S(2)}) %collective-permute-start.21) | collective-permute-done | bytes 131104 | tf_op jit(solution)/shard_map/ppermute | solution.py:18
  72.0 5.9 %collective-permute-start.14 = (bf16[128,1024]{1,0:T(8,128)(2,1)S(1)}, bf16[128,1024]{1,0:T(8,128)(2,1)S(1)}, u32[]{:S(2)}, u32[]{:S(2)}) collective-permute-start(bf16[128,1024]{1,0:T(8,128)(2,1)S(1)} %fusion.1), channel_id=1, source_target_pairs={{0,2},{1,3},{2,0},{3,1},{4,6},{5,7},{6,4},{7,5},{8,10},{9,11},{10,... | collective-permute-start | bytes 786440 | tf_op jit(solution)/shard_map/ppermute | solution.py:18
  78.6 6.1 %collective-permute-done.27 = bf16[128,1024]{1,0:T(8,128)(2,1)S(1)} collective-permute-done((bf16[128,1024]{1,0:T(8,128)(2,1)S(1)}, bf16[128,1024]{1,0:T(8,128)(2,1)S(1)}, u32[]{:S(2)}, u32[]{:S(2)}) %collective-permute-start.27) | collective-permute-done | bytes 262176 | tf_op jit(solution)/shard_map/ppermute | solution.py:18
  85.0 10.7 %collective-permute-done.14 = bf16[128,1024]{1,0:T(8,128)(2,1)S(1)} collective-permute-done((bf16[128,1024]{1,0:T(8,128)(2,1)S(1)}, bf16[128,1024]{1,0:T(8,128)(2,1)S(1)}, u32[]{:S(2)}, u32[]{:S(2)}) %collective-permute-start.14) | collective-permute-done | bytes 262176 | tf_op jit(solution)/shard_map/ppermute | solution.py:18
  96.1 5.0 %collective-permute-done.28 = bf16[128,1024]{1,0:T(8,128)(2,1)S(1)} collective-permute-done((bf16[128,1024]{1,0:T(8,128)(2,1)S(1)}, bf16[128,1024]{1,0:T(8,128)(2,1)S(1)}, u32[]{:S(2)}, u32[]{:S(2)}) %collective-permute-start.28) | collective-permute-done | bytes 262176 | tf_op jit(solution)/shard_map/ppermute | solution.py:18
  101.3 3.3 %mlp.4 = (f32[2,128,256]{2,1,0:T(8,128)S(1)}, bf16[2,128,256]{2,1,0:T(8,128)(2,1)S(1)}) custom-call(f32[128,1024]{1,0:T(8,128)S(1)} %get-tuple-element.38.rows_ref, f32[1,2,1024]{2,1,0:T(2,128)S(1)} %copy-done.8, bf16[1,2,1024,1024]{3,2,1,0:T(8,128)(2,1)} %gate_up_ref.7, bf16[1,1024,1024]{2,1,0:T(8,128)(2,1)S(1)} %copy-done.2), custom_call_target="tpu_custom_call" | custom-call | flops 1000 | bytes 1000 | tf_op jit(solution)/shard_map/mlp/pallas_call | solution.py:48
  104.6 2.1 %collective-permute-done.15.rows_ref = bf16[128,1024]{1,0:T(8,128)(2,1)S(1)} collective-permute-done((bf16[128,1024]{1,0:T(8,128)(2,1)S(1)}, bf16[128,1024]{1,0:T(8,128)(2,1)S(1)}, u32[]{:S(2)}, u32[]{:S(2)}) %collective-permute-start.15) | collective-permute-done | bytes 262176 | tf_op jit(solution)/shard_map/ppermute | solution.py:18
  106.7 3.3 %mlp.5 = (f32[2,128,256]{2,1,0:T(8,128)S(1)}, bf16[2,128,256]{2,1,0:T(8,128)(2,1)S(1)}) custom-call(bf16[128,1024]{1,0:T(8,128)(2,1)S(1)} %collective-permute-done.15.rows_ref, f32[1,2,1024]{2,1,0:T(2,128)S(1)} %copy-done.8, bf16[1,2,1024,1024]{3,2,1,0:T(8,128)(2,1)} %gate_up_ref.7, bf16[1,1024,1024]{2,1,0:T(8,128)(2,1)S(1)} %copy-done.2), custom_call_target="tpu_custom_call" | custom-call | flops 1000 | bytes 1000 | tf_op jit(solution)/shard_map/mlp/pallas_call | solution.py:48
  110.1 3.3 %mlp.6 = (f32[2,128,256]{2,1,0:T(8,128)S(1)}, bf16[2,128,256]{2,1,0:T(8,128)(2,1)S(1)}) custom-call(f32[128,1024]{1,0:T(8,128)S(1)} %get-tuple-element.42.rows_ref, f32[1,2,1024]{2,1,0:T(2,128)S(1)} %copy-done.8, bf16[1,2,1024,1024]{3,2,1,0:T(8,128)(2,1)} %gate_up_ref.7, bf16[1,1024,1024]{2,1,0:T(8,128)(2,1)S(1)} %copy-done.2), custom_call_target="tpu_custom_call" | custom-call | flops 1000 | bytes 1000 | tf_op jit(solution)/shard_map/mlp/pallas_call | solution.py:48
  113.4 3.3 %mlp.7 = (f32[2,128,256]{2,1,0:T(8,128)S(1)}, bf16[2,128,256]{2,1,0:T(8,128)(2,1)S(1)}) custom-call(bf16[128,1024]{1,0:T(8,128)(2,1)S(1)} %collective-permute-done.29.rows_ref, f32[1,2,1024]{2,1,0:T(2,128)S(1)} %copy-done.8, bf16[1,2,1024,1024]{3,2,1,0:T(8,128)(2,1)} %gate_up_ref.7, bf16[1,1024,1024]{2,1,0:T(8,128)(2,1)S(1)} %copy-done.2), custom_call_target="tpu_custom_call" | custom-call | flops 1000 | bytes 1000 | tf_op jit(solution)/shard_map/mlp/pallas_call | solution.py:48
  116.7 2.1 %collective-permute-start.30 = (bf16[2,2,128,256]{3,2,1,0:T(8,128)(2,1)S(1)}, bf16[2,2,128,256]{3,2,1,0:T(8,128)(2,1)S(1)}, u32[]{:S(2)}, u32[]{:S(2)}) collective-permute-start(bf16[2,2,128,256]{3,2,1,0:T(8,128)(2,1)S(1)} %pad_maximum_fusion.2), channel_id=1, source_target_pairs={{0,1},{1,0},{2,3},{3,2},{4,5},{5,4},{6,7},{7,6},{8,9},{9,8},{10,11... | collective-permute-start | bytes 786440 | tf_op jit(solution)/shard_map/ppermute | solution.py:18
  119.9 7.8 %collective-permute-done.30 = bf16[2,2,128,256]{3,2,1,0:T(8,128)(2,1)S(1)} collective-permute-done((bf16[2,2,128,256]{3,2,1,0:T(8,128)(2,1)S(1)}, bf16[2,2,128,256]{3,2,1,0:T(8,128)(2,1)S(1)}, u32[]{:S(2)}, u32[]{:S(2)}) %collective-permute-start.30) | collective-permute-done | bytes 262176 | tf_op jit(solution)/shard_map/ppermute | solution.py:18
  129.1 6.7 %collective-permute-done.31 = bf16[2,1,128,256]{3,2,1,0:T(8,128)(2,1)S(1)} collective-permute-done((bf16[2,1,128,256]{3,2,1,0:T(8,128)(2,1)S(1)}, bf16[2,1,128,256]{3,2,1,0:T(8,128)(2,1)S(1)}, u32[]{:S(2)}, u32[]{:S(2)}) %collective-permute-start.31) | collective-permute-done | bytes 131104 | tf_op jit(solution)/shard_map/ppermute | solution.py:18
  (100 shorter events, 30.0 us)
Async XLA Ops:
  0.0 9.5 %collective-permute-start = (bf16[128,1024]{1,0:T(8,128)(2,1)}, bf16[128,1024]{1,0:T(8,128)(2,1)S(1)}, u32[]{:S(2)}, u32[]{:S(2)}) collective-permute-start(bf16[128,1024]{1,0:T(8,128)(2,1)} %refs_0_.7), channel_id=1, source_target_pairs={{0,8},{4,12},{8,0},{12,4},{1,9},{5,13},{9,1},{13,5},{2,10},{6,14},... | collective-permute-start | bytes 786440 | tf_op jit(solution)/shard_map/ppermute | solution.py:18
  2.9 6.5 %collective-permute-start.1 = (bf16[128,1024]{1,0:T(8,128)(2,1)}, bf16[128,1024]{1,0:T(8,128)(2,1)S(1)}, u32[]{:S(2)}, u32[]{:S(2)}) collective-permute-start(bf16[128,1024]{1,0:T(8,128)(2,1)} %refs_0_.7), channel_id=1, source_target_pairs={{0,4},{4,0},{8,12},{12,8},{1,5},{5,1},{9,13},{13,9},{2,6},{6,2},{1... | collective-permute-start | bytes 786440 | tf_op jit(solution)/shard_map/ppermute | solution.py:18
  14.0 9.2 %collective-permute-start.3 = (bf16[128,1024]{1,0:T(8,128)(2,1)S(1)}, bf16[128,1024]{1,0:T(8,128)(2,1)S(1)}, u32[]{:S(2)}, u32[]{:S(2)}) collective-permute-start(bf16[128,1024]{1,0:T(8,128)(2,1)S(1)} %project.5), channel_id=1, source_target_pairs={{0,1},{1,0},{2,3},{3,2},{4,5},{5,4},{6,7},{7,6},{8,9},{9,8},{10,11... | collective-permute-start | bytes 786440 | tf_op jit(solution)/shard_map/ppermute | solution.py:18
  16.4 17.6 %collective-permute-start.18 = (bf16[128,1024]{1,0:T(8,128)(2,1)S(1)}, bf16[128,1024]{1,0:T(8,128)(2,1)S(1)}, u32[]{:S(2)}, u32[]{:S(2)}) collective-permute-start(bf16[128,1024]{1,0:T(8,128)(2,1)S(1)} %project.7), channel_id=1, source_target_pairs={{0,1},{1,0},{2,3},{3,2},{4,5},{5,4},{6,7},{7,6},{8,9},{9,8},{10,11... | collective-permute-start | bytes 786440 | tf_op jit(solution)/shard_map/ppermute | solution.py:18
  23.3 13.5 %collective-permute-start.4 = (bf16[128,1024]{1,0:T(8,128)(2,1)S(1)}, bf16[128,1024]{1,0:T(8,128)(2,1)S(1)}, u32[]{:S(2)}, u32[]{:S(2)}) collective-permute-start(bf16[128,1024]{1,0:T(8,128)(2,1)S(1)} %fusion), channel_id=1, source_target_pairs={{0,2},{1,3},{2,0},{3,1},{4,6},{5,7},{6,4},{7,5},{8,10},{9,11},{10,... | collective-permute-start | bytes 786440 | tf_op jit(solution)/shard_map/ppermute | solution.py:18
  34.1 14.7 %collective-permute-start.19 = (bf16[128,1024]{1,0:T(8,128)(2,1)S(1)}, bf16[128,1024]{1,0:T(8,128)(2,1)S(1)}, u32[]{:S(2)}, u32[]{:S(2)}) collective-permute-start(bf16[128,1024]{1,0:T(8,128)(2,1)S(1)} %fusion.2), channel_id=1, source_target_pairs={{0,2},{1,3},{2,0},{3,1},{4,6},{5,7},{6,4},{7,5},{8,10},{9,11},{10,... | collective-permute-start | bytes 786440 | tf_op jit(solution)/shard_map/ppermute | solution.py:18
  37.0 14.6 %collective-permute-start.9 = (bf16[128,1024]{1,0:T(8,128)(2,1)S(1)}, bf16[128,1024]{1,0:T(8,128)(2,1)S(1)}, u32[]{:S(2)}, u32[]{:S(2)}) collective-permute-start(bf16[128,1024]{1,0:T(8,128)(2,1)S(1)} %get-tuple-element.39), channel_id=1, source_target_pairs={{0,1},{1,0},{2,3},{3,2},{4,5},{5,4},{6,7},{7,6},{8,9},{9,8},{10,11... | collective-permute-start | bytes 786440 | tf_op jit(solution)/shard_map/ppermute | solution.py:18
  49.0 9.2 %collective-permute-start.23 = (bf16[128,1024]{1,0:T(8,128)(2,1)S(1)}, bf16[128,1024]{1,0:T(8,128)(2,1)S(1)}, u32[]{:S(2)}, u32[]{:S(2)}) collective-permute-start(bf16[128,1024]{1,0:T(8,128)(2,1)S(1)} %get-tuple-element.43), channel_id=1, source_target_pairs={{0,1},{1,0},{2,3},{3,2},{4,5},{5,4},{6,7},{7,6},{8,9},{9,8},{10,11... | collective-permute-start | bytes 786440 | tf_op jit(solution)/shard_map/ppermute | solution.py:18
  52.4 8.0 %collective-permute-start.10 = (bf16[2,128,256]{2,1,0:T(8,128)(2,1)S(1)}, bf16[2,128,256]{2,1,0:T(8,128)(2,1)S(1)}, u32[]{:S(2)}, u32[]{:S(2)}) collective-permute-start(bf16[2,128,256]{2,1,0:T(8,128)(2,1)S(1)} %get-tuple-element.24.refs_0_), channel_id=1, source_target_pairs={{0,4},{4,0},{8,12},{12,8},{1,5},{5,1},{9,13},{13,9},{2,6},{6,2},{1... | collective-permute-start | bytes 393224 | tf_op jit(solution)/shard_map/ppermute | solution.py:18
  57.5 6.5 %collective-permute-start.7 = (bf16[2,128,256]{2,1,0:T(8,128)(2,1)S(1)}, bf16[2,128,256]{2,1,0:T(8,128)(2,1)S(1)}, u32[]{:S(2)}, u32[]{:S(2)}) collective-permute-start(bf16[2,128,256]{2,1,0:T(8,128)(2,1)S(1)} %get-tuple-element.22.refs_0_), channel_id=1, source_target_pairs={{0,8},{4,12},{8,0},{12,4},{1,9},{5,13},{9,1},{13,5},{2,10},{6,14},... | collective-permute-start | bytes 393224 | tf_op jit(solution)/shard_map/ppermute | solution.py:18
  58.7 8.0 %collective-permute-start.25 = (bf16[2,128,256]{2,1,0:T(8,128)(2,1)S(1)}, bf16[2,128,256]{2,1,0:T(8,128)(2,1)S(1)}, u32[]{:S(2)}, u32[]{:S(2)}) collective-permute-start(bf16[2,128,256]{2,1,0:T(8,128)(2,1)S(1)} %get-tuple-element.32.refs_0_), channel_id=1, source_target_pairs={{0,8},{4,12},{8,0},{12,4},{1,9},{5,13},{9,1},{13,5},{2,10},{6,14},... | collective-permute-start | bytes 393224 | tf_op jit(solution)/shard_map/ppermute | solution.py:18
  61.2 10.7 %collective-permute-start.13 = (bf16[128,1024]{1,0:T(8,128)(2,1)S(1)}, bf16[128,1024]{1,0:T(8,128)(2,1)S(1)}, u32[]{:S(2)}, u32[]{:S(2)}) collective-permute-start(bf16[128,1024]{1,0:T(8,128)(2,1)S(1)} %attend.5), channel_id=1, source_target_pairs={{0,1},{1,0},{2,3},{3,2},{4,5},{5,4},{6,7},{7,6},{8,9},{9,8},{10,11... | collective-permute-start | bytes 786440 | tf_op jit(solution)/shard_map/ppermute | solution.py:18
  62.3 6.8 %collective-permute-start.21 = (bf16[2,128,256]{2,1,0:T(8,128)(2,1)S(1)}, bf16[2,128,256]{2,1,0:T(8,128)(2,1)S(1)}, u32[]{:S(2)}, u32[]{:S(2)}) collective-permute-start(bf16[2,128,256]{2,1,0:T(8,128)(2,1)S(1)} %get-tuple-element.30.refs_0_), channel_id=1, source_target_pairs={{0,8},{4,12},{8,0},{12,4},{1,9},{5,13},{9,1},{13,5},{2,10},{6,14},... | collective-permute-start | bytes 393224 | tf_op jit(solution)/shard_map/ppermute | solution.py:18
  69.1 8.7 %collective-permute-start.20 = (bf16[2,128,256]{2,1,0:T(8,128)(2,1)S(1)}, bf16[2,128,256]{2,1,0:T(8,128)(2,1)S(1)}, u32[]{:S(2)}, u32[]{:S(2)}) collective-permute-start(bf16[2,128,256]{2,1,0:T(8,128)(2,1)S(1)} %get-tuple-element.30.refs_0_), channel_id=1, source_target_pairs={{0,4},{4,0},{8,12},{12,8},{1,5},{5,1},{9,13},{13,9},{2,6},{6,2},{1... | collective-permute-start | bytes 393224 | tf_op jit(solution)/shard_map/ppermute | solution.py:18
  69.1 8.7 %collective-permute-start.22 = (bf16[2,128,256]{2,1,0:T(8,128)(2,1)S(1)}, bf16[2,128,256]{2,1,0:T(8,128)(2,1)S(1)}, u32[]{:S(2)}, u32[]{:S(2)}) collective-permute-start(bf16[2,128,256]{2,1,0:T(8,128)(2,1)S(1)} %collective-permute-done.21.refs_2_), channel_id=1, source_target_pairs={{0,4},{4,0},{8,12},{12,8},{1,5},{5,1},{9,13},{13,9},{2,6},{6,2},{1... | collective-permute-start | bytes 393224 | tf_op jit(solution)/shard_map/ppermute | solution.py:18
  71.2 13.5 %collective-permute-start.27 = (bf16[128,1024]{1,0:T(8,128)(2,1)S(1)}, bf16[128,1024]{1,0:T(8,128)(2,1)S(1)}, u32[]{:S(2)}, u32[]{:S(2)}) collective-permute-start(bf16[128,1024]{1,0:T(8,128)(2,1)S(1)} %attend.7), channel_id=1, source_target_pairs={{0,1},{1,0},{2,3},{3,2},{4,5},{5,4},{6,7},{7,6},{8,9},{9,8},{10,11... | collective-permute-start | bytes 786440 | tf_op jit(solution)/shard_map/ppermute | solution.py:18
  72.0 23.7 %collective-permute-start.14 = (bf16[128,1024]{1,0:T(8,128)(2,1)S(1)}, bf16[128,1024]{1,0:T(8,128)(2,1)S(1)}, u32[]{:S(2)}, u32[]{:S(2)}) collective-permute-start(bf16[128,1024]{1,0:T(8,128)(2,1)S(1)} %fusion.1), channel_id=1, source_target_pairs={{0,2},{1,3},{2,0},{3,1},{4,6},{5,7},{6,4},{7,5},{8,10},{9,11},{10,... | collective-permute-start | bytes 786440 | tf_op jit(solution)/shard_map/ppermute | solution.py:18
  84.8 16.3 %collective-permute-start.28 = (bf16[128,1024]{1,0:T(8,128)(2,1)S(1)}, bf16[128,1024]{1,0:T(8,128)(2,1)S(1)}, u32[]{:S(2)}, u32[]{:S(2)}) collective-permute-start(bf16[128,1024]{1,0:T(8,128)(2,1)S(1)} %fusion.3), channel_id=1, source_target_pairs={{0,2},{1,3},{2,0},{3,1},{4,6},{5,7},{6,4},{7,5},{8,10},{9,11},{10,... | collective-permute-start | bytes 786440 | tf_op jit(solution)/shard_map/ppermute | solution.py:18
  95.8 10.8 %collective-permute-start.15 = (bf16[128,1024]{1,0:T(8,128)(2,1)S(1)}, bf16[128,1024]{1,0:T(8,128)(2,1)S(1)}, u32[]{:S(2)}, u32[]{:S(2)}) collective-permute-start(bf16[128,1024]{1,0:T(8,128)(2,1)S(1)} %get-tuple-element.37), channel_id=1, source_target_pairs={{0,1},{1,0},{2,3},{3,2},{4,5},{5,4},{6,7},{7,6},{8,9},{9,8},{10,11... | collective-permute-start | bytes 786440 | tf_op jit(solution)/shard_map/ppermute | solution.py:18
  101.2 12.2 %collective-permute-start.29 = (bf16[128,1024]{1,0:T(8,128)(2,1)S(1)}, bf16[128,1024]{1,0:T(8,128)(2,1)S(1)}, u32[]{:S(2)}, u32[]{:S(2)}) collective-permute-start(bf16[128,1024]{1,0:T(8,128)(2,1)S(1)} %get-tuple-element.41), channel_id=1, source_target_pairs={{0,1},{1,0},{2,3},{3,2},{4,5},{5,4},{6,7},{7,6},{8,9},{9,8},{10,11... | collective-permute-start | bytes 786440 | tf_op jit(solution)/shard_map/ppermute | solution.py:18
  110.0 8.8 %collective-permute-start.16 = (bf16[2,2,128,256]{3,2,1,0:T(8,128)(2,1)S(1)}, bf16[2,2,128,256]{3,2,1,0:T(8,128)(2,1)S(1)}, u32[]{:S(2)}, u32[]{:S(2)}) collective-permute-start(bf16[2,2,128,256]{3,2,1,0:T(8,128)(2,1)S(1)} %pad_maximum_fusion.1), channel_id=1, source_target_pairs={{0,1},{1,0},{2,3},{3,2},{4,5},{5,4},{6,7},{7,6},{8,9},{9,8},{10,11... | collective-permute-start | bytes 786440 | tf_op jit(solution)/shard_map/ppermute | solution.py:18
  116.7 11.0 %collective-permute-start.30 = (bf16[2,2,128,256]{3,2,1,0:T(8,128)(2,1)S(1)}, bf16[2,2,128,256]{3,2,1,0:T(8,128)(2,1)S(1)}, u32[]{:S(2)}, u32[]{:S(2)}) collective-permute-start(bf16[2,2,128,256]{3,2,1,0:T(8,128)(2,1)S(1)} %pad_maximum_fusion.2), channel_id=1, source_target_pairs={{0,1},{1,0},{2,3},{3,2},{4,5},{5,4},{6,7},{7,6},{8,9},{9,8},{10,11... | collective-permute-start | bytes 786440 | tf_op jit(solution)/shard_map/ppermute | solution.py:18
  118.9 10.2 %collective-permute-start.17 = (bf16[2,1,128,256]{3,2,1,0:T(8,128)(2,1)S(1)}, bf16[2,1,128,256]{3,2,1,0:T(8,128)(2,1)S(1)}, u32[]{:S(2)}, u32[]{:S(2)}) collective-permute-start(bf16[2,1,128,256]{3,2,1,0:T(8,128)(2,1)S(1)} %slice.55), channel_id=1, source_target_pairs={{0,2},{1,3},{2,0},{3,1},{4,6},{5,7},{6,4},{7,5},{8,10},{9,11},{10,... | collective-permute-start | bytes 393224 | tf_op jit(solution)/shard_map/ppermute | solution.py:18
  127.8 8.0 %collective-permute-start.31 = (bf16[2,1,128,256]{3,2,1,0:T(8,128)(2,1)S(1)}, bf16[2,1,128,256]{3,2,1,0:T(8,128)(2,1)S(1)}, u32[]{:S(2)}, u32[]{:S(2)}) collective-permute-start(bf16[2,1,128,256]{3,2,1,0:T(8,128)(2,1)S(1)} %slice.54), channel_id=1, source_target_pairs={{0,2},{1,3},{2,0},{3,1},{4,6},{5,7},{6,4},{7,5},{8,10},{9,11},{10,... | collective-permute-start | bytes 393224 | tf_op jit(solution)/shard_map/ppermute | solution.py:18
  (18 other events, 111.3 us)

commit v3 on v2

v3 whole, which is shorter than its diff:
```python
import functools
import math

import jax
import jax.numpy as jnp
from jax import lax
from jax.experimental import pallas as pl
from jax.experimental.pallas import tpu as pltpu
from jax.sharding import PartitionSpec as P

HEADS = 16
CHUNKS = 4
SPLITS = 2
F32 = jnp.float32
BF16 = jnp.bfloat16
VMEM = pl.BlockSpec(memory_space=pltpu.VMEM)


def swap(block, axis, distance):
    count = lax.axis_size(axis)
    return lax.ppermute(block, axis, [(i, i ^ distance) for i in range(count)])


def middle_swap(block):
    ends, codes = lax.axis_size("hidden"), lax.axis_size("codebook")
    route = []
    for code in range(codes):
        for i in range(ends):
            other = (code, ends - 1 - i) if 0 < i < ends - 1 else (code ^ 1, i)
            route.append((code * ends + i, other[0] * ends + other[1]))
    return lax.ppermute(block, ("codebook", "hidden"), route)


def is_middle():
    index = lax.axis_index("hidden")
    return (index > 0) & (index < lax.axis_size("hidden") - 1)


def bits_of(axis):
    count = lax.axis_size(axis)
    return [1 << b for b in range(count.bit_length() - 1)]


def shifted(block, axis, distance):
    devices = range(lax.axis_size(axis))
    route = [(i - distance, i) for i in devices if i - distance in devices]
    return lax.ppermute(block, axis, route)


def slots_of(block, axis):
    slots = {0: block}
    for bit in reversed(bits_of(axis)):
        slots.update({slot ^ bit: swap(piece, axis, bit) for slot, piece in slots.items()})
    return [slots[slot] for slot in range(len(slots))]


def dot(a, b):
    return jnp.dot(a, b, preferred_element_type=F32)


def normalize(values, norm_gain):
    return values * lax.rsqrt(jnp.mean(values * values, axis=-1, keepdims=True) + 1e-05) * norm_gain


class Steps:
    def __init__(self):
        self.token = None

    def __call__(self, kernel, name, outs, args, scratch=(), aliases=None, out_space=pltpu.VMEM):
        tokens = [] if self.token is None else [self.token]
        count, given = len(outs), len(args)
        held = [(a.shape, a.dtype) for a in args] + list(outs)
        size = sum(math.prod(shape) * jnp.dtype(dtype).itemsize for shape, dtype in held)

        def with_token(*refs):
            inputs, rest = refs[:given], refs[given + len(tokens) :]
            outputs, token_ref, scratches = rest[:count], rest[count], rest[count + 1 :]
            kernel(*inputs, *outputs, *scratches)
            token_ref[...] = jnp.zeros_like(token_ref)

        *results, self.token = pl.pallas_call(
            with_token,
            name=name,
            out_shape=[jax.ShapeDtypeStruct(shape, dtype) for shape, dtype in outs]
            + [jax.ShapeDtypeStruct((8, 128), F32)],
            in_specs=[VMEM] * (given + len(tokens)),
            out_specs=[pl.BlockSpec(memory_space=out_space)] * count + [VMEM],
            scratch_shapes=list(scratch),
            input_output_aliases=aliases or {},
            cost_estimate=pl.CostEstimate(flops=1000, bytes_accessed=1000, transcendentals=0),
            compiler_params=pltpu.CompilerParams(vmem_limit_bytes=size + (6 << 20)),
        )(*args, *tokens)
        return results


def row_blocks(rows):
    size = min(rows, 128)
    return [pl.ds(start, size) for start in range(0, rows, size)]


def proj_kernel(start, *refs):
    *piece_refs, weight_ref, out_ref, rows_ref = refs
    code = lax.axis_index("codebook")
    size = rows_ref.shape[0] // len(piece_refs)
    for i in range(len(piece_refs)):
        for slot, piece_ref in enumerate(piece_refs):

            @pl.when(code ^ i == slot)
            def _():
                rows_ref[i * size : (i + 1) * size, :] = piece_ref[start : start + size, :]

    for block in row_blocks(rows_ref.shape[0]):
        out_ref[block, :] = dot(rows_ref[block, :], weight_ref[0])


def embed_kernel(chunk, ids_ref, table_ref, out_ref):
    first = lax.axis_index("codebook") == 0
    start_id = table_ref.shape[1] - 1
    count, length = ids_ref.shape
    size = out_ref.shape[0] // count
    diagonal = lax.broadcasted_iota(jnp.int32, (length, length), 0) == lax.broadcasted_iota(
        jnp.int32, (length, length), 1
    )
    columns = []
    for i in range(count):
        line = ids_ref[i : i + 1, :].astype(F32)
        column = jnp.sum(jnp.where(diagonal, line, 0.0), axis=1, keepdims=True).astype(jnp.int32)
        columns.append(column[chunk * size : (chunk + 1) * size])
    all_ids = jnp.where(first, start_id, jnp.concatenate(columns, axis=0))
    for block in row_blocks(out_ref.shape[0]):
        ids = all_ids[block.start : block.start + block.size]
        token = lax.broadcasted_iota(jnp.int32, (block.size, start_id), 1)
        chosen = (token == ids).astype(F32).astype(BF16)
        started = jnp.where(ids == start_id, 1.0, 0.0) * table_ref[0, start_id:, :].astype(F32)
        out_ref[block, :] = (dot(chosen, table_ref[0, :start_id, :]) + started).astype(BF16)


def sum_kernel(*refs):
    *term_refs, wide_ref, sent_ref = refs
    total = term_refs[0][...].astype(F32)
    for term_ref in term_refs[1:]:
        total = total + term_ref[...].astype(F32)
    wide_ref[...] = total
    sent_ref[...] = total.astype(BF16)


def pass_kernel(given_ref, taken_ref):
    pass


def mix_kernel(terms, *refs):
    outs = 2 if terms else 1
    sent_ref = refs[-1]
    part_refs, term_refs = refs[: len(refs) - outs - terms], refs[len(refs) - outs - terms : -outs]

    def send_part():
        sent_ref[...] = part_refs[0][...].astype(BF16)

    def send_rows():
        total = term_refs[0][...].astype(F32)
        for term_ref in term_refs[1:]:
            total = total + term_ref[...].astype(F32)
        refs[-2][...] = total
        sent_ref[...] = total.astype(BF16)

    if not term_refs:
        send_part()
    elif not part_refs:
        send_rows()
    else:
        pl.when(is_middle())(send_rows)
        pl.when(jnp.logical_not(is_middle()))(send_part)


def choose(wide_ref, arrived_ref, rows_ref):
    @pl.when(is_middle())
    def _():
        rows_ref[...] = wide_ref[...]

    @pl.when(jnp.logical_not(is_middle()))
    def _():
        rows_ref[...] = arrived_ref[...].astype(F32)


def qkv_kernel(wide_ref, arrived_ref, gain_ref, weight_ref, query_ref, kv_ref, rows_ref):
    choose(wide_ref, arrived_ref, rows_ref)
    for block in row_blocks(rows_ref.shape[0]):
        normed = normalize(rows_ref[block, :].astype(F32), gain_ref[0, 0:1, :]).astype(BF16)
        query_ref[block, :] = dot(normed, weight_ref[0, 0]).astype(BF16)
        kv_ref[0, block, :] = dot(normed, weight_ref[0, 1]).astype(BF16)
        kv_ref[1, block, :] = dot(normed, weight_ref[0, 2]).astype(BF16)


def attend_kernel(head_size, query_ref, *refs):
    *kv_refs, weight_ref, part_ref = refs
    code = lax.axis_index("codebook")
    width = query_ref.shape[-1]
    lanes = 128
    column = lax.broadcasted_iota(jnp.int32, (width, lanes), 0) // head_size
    head = lax.broadcasted_iota(jnp.int32, (width, lanes), 1)
    gather = (column == head).astype(F32).astype(BF16)
    head_t = lax.broadcasted_iota(jnp.int32, (lanes, width), 0)
    column_t = lax.broadcasted_iota(jnp.int32, (lanes, width), 1) // head_size
    spread = (column_t == head_t).astype(F32).astype(BF16)
    for block in row_blocks(query_ref.shape[0]):
        query = query_ref[block, :].astype(F32)
        scores = []
        for slot, kv_ref in enumerate(kv_refs):
            product = query * kv_ref[0, block, :].astype(F32)
            high = product.astype(BF16)
            low = (product - high.astype(F32)).astype(BF16)
            score = (dot(high, gather) + dot(low, gather)) * head_size ** (-0.5)
            if slot:
                score = jnp.where((code ^ slot) <= code, score, -1e30)
            scores.append(score)
        highest = functools.reduce(jnp.maximum, scores)
        weights = [jnp.exp(score - highest) for score in scores]
        running = functools.reduce(jnp.add, weights)
        summed = None
        for kv_ref, weight in zip(kv_refs, weights):
            term = dot(weight.astype(BF16), spread) * kv_ref[1, block, :].astype(F32)
            summed = term if summed is None else summed + term
        inverse = 1.0 / running
        high = inverse.astype(BF16)
        low = (inverse - high.astype(F32)).astype(BF16)
        attended = (summed * (dot(high, spread) + dot(low, spread))).astype(BF16)
        part_ref[block, :] = dot(attended, weight_ref[0]).astype(part_ref.dtype)


def mlp_kernel(
    count, wide_ref, arrived_ref, gain_ref, gate_up_ref, down_ref, kept_ref, sent_ref, rows_ref, act_ref
):
    choose(wide_ref, arrived_ref, rows_ref)
    index = lax.axis_index("hidden")
    hidden = act_ref.shape[1]
    step = min(hidden, 256)
    width = kept_ref.shape[2]
    for block in row_blocks(rows_ref.shape[0]):
        normed = normalize(rows_ref[block, :], gain_ref[0, 1:2, :]).astype(BF16)
        for start in range(0, hidden, step):
            columns = pl.ds(start, step)
            gate_sum = dot(normed, gate_up_ref[0, 0, :, columns])
            upper_sum = dot(normed, gate_up_ref[0, 1, :, columns])
            act_ref[:, columns] = (jax.nn.silu(gate_sum) * upper_sum).astype(BF16)
        for i in range(count // 2):
            owner = index ^ (2 * i)
            columns = pl.ds(pl.multiple_of((owner ^ 1) * width, width), width)
            sent_ref[i, block, :] = dot(act_ref[...], down_ref[0, :, columns]).astype(BF16)
        for i in range(count // 2):
            owner = index ^ (2 * i)
            columns = pl.ds(pl.multiple_of(owner * width, width), width)
            total = dot(act_ref[...], down_ref[0, :, columns])
            if i == 0:
                total = total + rows_ref[block, columns]
            kept_ref[i, block, :] = total


def halve_kernel(mine_ref, arrived_ref, wide_ref, sent_ref):
    kept = wide_ref.shape[0]
    wide_ref[...] = mine_ref[:kept] + arrived_ref[:kept].astype(F32)
    sent_ref[...] = (mine_ref[kept:] + arrived_ref[kept:].astype(F32)).astype(BF16)


def final_kernel(count, *refs):
    *in_refs, out_ref, rows_ref, sems = refs
    chunks = len(in_refs) // 2
    stride = out_ref.shape[1] // count
    size = stride // chunks
    copies = []
    for chunk in range(chunks):
        wide_ref, arrived_ref = in_refs[2 * chunk : 2 * chunk + 2]
        rows_ref[chunk] = wide_ref[0] + arrived_ref[0].astype(F32)
        for i in range(count):
            source = rows_ref.at[chunk, pl.ds(i * size, size), :]
            target = out_ref.at[0, pl.ds(i * stride + chunk * size, size), :]
            copies.append(pltpu.make_async_copy(source, target, sems.at[chunk, i]))
            copies[-1].start()
    for copy in copies:
        copy.wait()


def body(
    temporal,
    frame_ids,
    proj_weight,
    embed_table,
    qkv_weight,
    out_weight,
    gate_up,
    down_weight,
    norm_gains,
):
    hidden_count = lax.axis_size("hidden")
    code_count = lax.axis_size("codebook")
    pair_bit, far_bit = bits_of("hidden")
    code_bits = bits_of("codebook")[::-1]
    width = embed_table.shape[2]
    local_width = qkv_weight.shape[3]
    head_size = width // HEADS

    block_rows = temporal.shape[0]
    size = block_rows // CHUNKS
    rows = code_count * size
    row_count = code_count * block_rows
    split = block_rows // SPLITS
    pieces = [slots_of(temporal[i * split : (i + 1) * split], "codebook") for i in range(SPLITS)]
    earlier = shifted(frame_ids.reshape(code_count, -1), "codebook", 1)
    step = Steps()
    wide, sent = ((rows, width), F32), ((rows, width), BF16)
    states = [{} for _ in range(CHUNKS)]

    def get(c):
        return states[c] if 0 <= c < CHUNKS else None

    def project(c):
        if (s := get(c)) is not None:
            s["part"] = step(
                functools.partial(proj_kernel, c * size % split),
                "project",
                [wide],
                [*pieces[c * size // split], proj_weight],
                [pltpu.VMEM((rows, temporal.shape[1]), BF16)],
            )[0]

    def embed(c):
        if (s := get(c)) is not None:
            s["embedded"] = step(
                functools.partial(embed_kernel, c), "embed", [sent], [earlier, embed_table]
            )[0]

    def mix(c, older, part, terms, names):
        s, o = get(c), get(older)
        if s is None and o is None:
            return
        args = [s[part]] if s is not None else []
        given = [o[term] for term in terms] if o is not None else []
        outs = [wide, sent] if given else [sent]
        *finished, out = step(
            functools.partial(mix_kernel, len(given)), names[0], outs, [*args, *given]
        )
        arrived = swap(out, "hidden", pair_bit)
        if s is not None:
            s["arrived"] = arrived
        if o is not None:
            o[names[0]], o[names[1]] = finished[0], arrived

    def pair_sum(c):
        if (s := get(c)) is not None:
            s["total"], out = step(sum_kernel, "pair_sum", [wide, sent], [s["part"], s["arrived"]])
            s["far"] = middle_swap(out)

    def qkv(c):
        if (s := get(c)) is not None:
            s["query"], kv = step(
                qkv_kernel,
                "qkv",
                [((rows, local_width), BF16), ((2, rows, local_width), BF16)],
                [s["x_zero"], s["x_arrived"], norm_gains, qkv_weight],
                [pltpu.VMEM((rows, width), F32)],
            )
            s["kvs"] = {0: kv} | {bit: swap(kv, "codebook", bit) for bit in code_bits}

    def forward(c):
        if (s := get(c)) is not None:
            for bit in code_bits:
                for slot in [slot for slot in s["kvs"] if slot > bit and not slot & (2 * bit - 1)]:
                    (kv,) = step(pass_kernel, "pass", [((2, rows, local_width), BF16)], [s["kvs"][slot]], aliases={0: 0})
                    s["kvs"][slot ^ bit] = swap(kv, "codebook", bit)

    def attend(c):
        if (s := get(c)) is not None:
            s["part"] = step(
                functools.partial(attend_kernel, head_size),
                "attend",
                [wide],
                [s["query"], *[s["kvs"][slot] for slot in range(code_count)], out_weight],
            )[0]

    def mlp(c):
        if (s := get(c)) is not None:
            shape = (hidden_count // 2, rows, local_width)
            s["sums"], out = step(
                functools.partial(mlp_kernel, hidden_count),
                "mlp",
                [(shape, F32), (shape, BF16)],
                [s["residual"], s["residual_arrived"], norm_gains, gate_up, down_weight],
                [pltpu.VMEM((rows, width), F32), pltpu.VMEM((min(rows, 128), gate_up.shape[3]), BF16)],
            )
            s["sums_arrived"] = swap(out, "hidden", pair_bit)

    def halve(c):
        if (s := get(c)) is not None:
            shape = (hidden_count // 4, rows, local_width)
            s["wide"], out = step(
                halve_kernel, "halve", [(shape, F32), (shape, BF16)], [s["sums"], s["sums_arrived"]]
            )
            s["last"] = swap(out, "hidden", far_bit)

    def final():
        args = [s[name] for s in states for name in ("wide", "last")]
        return step(
            functools.partial(final_kernel, code_count),
            "final",
            [((1, row_count, local_width), F32)],
            args,
            [pltpu.VMEM((CHUNKS, rows, local_width), F32), pltpu.SemaphoreType.DMA((CHUNKS, code_count))],
            out_space=pl.ANY,
        )[0]

    stages = 9
    project(0)
    for t in range(CHUNKS + stages - 1):
        pair_sum(t - 1)
        mix(t, t - 2, "part", ["total", "far", "embedded"], ["x_zero", "x_arrived"])
        qkv(t - 3)
        attend(t - 4)
        mlp(t - 7)
        mix(t - 4, t - 6, "part", ["x_zero", "total", "far"], ["residual", "residual_arrived"])
        pair_sum(t - 5)
        halve(t - 8)
        project(t + 1)
        embed(t - 1)
        forward(t - 3)
    return final()


def solution(mesh):
    placed = (
        P(("frames", "codebook"), "hidden"),
        P("frames", "codebook"),
        P("codebook", "hidden", None),
        P("codebook", None, None),
        P("codebook", None, None, "hidden"),
        P("codebook", "hidden", None),
        P("codebook", None, None, "hidden"),
        P("codebook", "hidden", None),
        P("codebook", None, None),
    )
    return jax.shard_map(
        body,
        mesh=mesh,
        in_specs=placed,
        out_specs=P("codebook", "frames", "hidden"),
        check_vma=False,
    )
```

time: 137 us -> 124 us (0.905)
  waiting for transfers between devices: 76.3 us -> 61.2 us
  starting transfers between devices: 30.8 us -> 40.5 us
  local copies, waits for them, and re-layouts: 6.57 us -> 2.66 us
  Pallas kernels: 21.5 us -> 18.4 us
    ppermute x31 -> x38, waiting for transfers between devices: 75.1 us -> 60.9 us  [swap(): return lax.ppermute(block, axis, [(i, i ^ distance) for i in range(count)])]
    ppermute x31 -> x38, starting transfers between devices: 29.5 us -> 37.2 us  [swap(): return lax.ppermute(block, axis, [(i, i ^ distance) for i in range(count)])]
    unnamed x21 -> x22, local copies, waits for them, and re-layouts: 5.71 us -> 1.67 us
    pallas_call x18 -> x49, Pallas kernels: 21.5 us -> 18.4 us  [__call__(): pl.pallas_call(with_token, name=name, out_shape=[jax.ShapeDtypeStruct(sha...]
  transfers between devices with their start and end apart: 32 -> 47, of which waited for: 16 -> 23; matrix products, arithmetic and copies ran while one was open for 1% -> 0% of each run, Pallas kernels for 15% -> 13%
where the time goes in v3:
time: 124 us; the launch traced here: 123 us
  waiting for transfers between devices  61.2 us (49%)
  starting transfers between devices  40.5 us (33%)
  Pallas kernels  18.4 us (15%)
  local copies, waits for them, and re-layouts  2.66 us (2%)
    ppermute x38, waiting for transfers between devices, swap(): return lax.ppermute(block, axis, [(i, i ^ distance) for i in range(count)])  60.9 us
    ppermute x38, starting transfers between devices, swap(): return lax.ppermute(block, axis, [(i, i ^ distance) for i in range(count)])  37.2 us
    pallas_call x49, Pallas kernels, __call__(): pl.pallas_call(with_token, name=name, out_shape=[jax.ShapeDtypeStruct(sha...  18.4 us
  transfers between devices with their start and end apart: 47, of which 23 were waited for; matrix products, arithmetic and copies ran while one was open for 0% of the time, Pallas kernels for 13%

profile of v3, /device:TPU:0, one launch (start us, length us, event | category | flops | bytes accessed | tf_op | source)
XLA Modules:
  0.0 123.4 jit_solution(16357765867892889601)
XLA Ops:
  1.0 3.0 %collective-permute-start.4 = (bf16[64,1024]{1,0:T(8,128)(2,1)S(1)}, bf16[64,1024]{1,0:T(8,128)(2,1)S(1)}, u32[]{:S(2)}, u32[]{:S(2)}) collective-permute-start(bf16[64,1024]{1,0:T(8,128)(2,1)S(1)} %get-tuple-element.255.refs_0_), channel_id=1, source_target_pairs={{0,8},{4,12},{8,0},{12,4},{1,9},{5,13},{9,1},{13,5},{2,10},{6,14},... | collective-permute-start | bytes 393224 | tf_op jit(solution)/shard_map/ppermute | solution.py:21
  4.0 3.5 %collective-permute-done.4.refs_2_ = bf16[64,1024]{1,0:T(8,128)(2,1)S(1)} collective-permute-done((bf16[64,1024]{1,0:T(8,128)(2,1)S(1)}, bf16[64,1024]{1,0:T(8,128)(2,1)S(1)}, u32[]{:S(2)}, u32[]{:S(2)}) %collective-permute-start.4) | collective-permute-done | bytes 131104 | tf_op jit(solution)/shard_map/ppermute | solution.py:21
  11.0 1.9 %collective-permute-start.6 = (bf16[128,1024]{1,0:T(8,128)(2,1)S(1)}, bf16[128,1024]{1,0:T(8,128)(2,1)S(1)}, u32[]{:S(2)}, u32[]{:S(2)}) collective-permute-start(bf16[128,1024]{1,0:T(8,128)(2,1)S(1)} %get-tuple-element.134), channel_id=1, source_target_pairs={{0,1},{1,0},{2,3},{3,2},{4,5},{5,4},{6,7},{7,6},{8,9},{9,8},{10,11... | collective-permute-start | bytes 786440 | tf_op jit(solution)/shard_map/ppermute | solution.py:21
  14.9 4.6 %collective-permute-done.6.refs_1_ = bf16[128,1024]{1,0:T(8,128)(2,1)S(1)} collective-permute-done((bf16[128,1024]{1,0:T(8,128)(2,1)S(1)}, bf16[128,1024]{1,0:T(8,128)(2,1)S(1)}, u32[]{:S(2)}, u32[]{:S(2)}) %collective-permute-start.6) | collective-permute-done | bytes 262176 | tf_op jit(solution)/shard_map/ppermute | solution.py:21
  19.6 1.8 %collective-permute-start.9 = (bf16[128,1024]{1,0:T(8,128)(2,1)S(1)}, bf16[128,1024]{1,0:T(8,128)(2,1)S(1)}, u32[]{:S(2)}, u32[]{:S(2)}) collective-permute-start(bf16[128,1024]{1,0:T(8,128)(2,1)S(1)} %get-tuple-element.143), channel_id=1, source_target_pairs={{0,1},{1,0},{2,3},{3,2},{4,5},{5,4},{6,7},{7,6},{8,9},{9,8},{10,11... | collective-permute-start | bytes 786440 | tf_op jit(solution)/shard_map/ppermute | solution.py:21
  22.0 2.4 %collective-permute-start.8 = (s32[4,128]{1,0:T(4,128)S(1)}, s32[4,128]{1,0:T(4,128)S(1)}, u32[]{:S(2)}, u32[]{:S(2)}) collective-permute-start(s32[4,128]{1,0:T(4,128)S(1)} %bitcast.1), channel_id=1, source_target_pairs={{0,4},{4,8},{8,12},{1,5},{5,9},{9,13},{2,6},{6,10},{10,14},{3,7},{... | collective-permute-start | bytes 6152 | tf_op jit(solution)/shard_map/ppermute | solution.py:47
  27.5 2.8 %collective-permute-start.10 = (bf16[128,1024]{1,0:T(8,128)(2,1)S(1)}, bf16[128,1024]{1,0:T(8,128)(2,1)S(1)}, u32[]{:S(2)}, u32[]{:S(2)}) collective-permute-start(bf16[128,1024]{1,0:T(8,128)(2,1)S(1)} %get-tuple-element.146), channel_id=1, source_target_pairs={{0,1},{1,0},{2,3},{3,2},{4,5},{5,4},{6,7},{7,6},{8,9},{9,8},{10,11... | collective-permute-start | bytes 786440 | tf_op jit(solution)/shard_map/ppermute | solution.py:21
  31.7 5.3 %collective-permute-done.10.refs_1_ = bf16[128,1024]{1,0:T(8,128)(2,1)S(1)} collective-permute-done((bf16[128,1024]{1,0:T(8,128)(2,1)S(1)}, bf16[128,1024]{1,0:T(8,128)(2,1)S(1)}, u32[]{:S(2)}, u32[]{:S(2)}) %collective-permute-start.10) | collective-permute-done | bytes 262176 | tf_op jit(solution)/shard_map/ppermute | solution.py:21
  37.1 1.9 %collective-permute-start.13 = (bf16[128,1024]{1,0:T(8,128)(2,1)S(1)}, bf16[128,1024]{1,0:T(8,128)(2,1)S(1)}, u32[]{:S(2)}, u32[]{:S(2)}) collective-permute-start(bf16[128,1024]{1,0:T(8,128)(2,1)S(1)} %get-tuple-element.161), channel_id=1, source_target_pairs={{0,1},{1,0},{2,3},{3,2},{4,5},{5,4},{6,7},{7,6},{8,9},{9,8},{10,11... | collective-permute-start | bytes 786440 | tf_op jit(solution)/shard_map/ppermute | solution.py:21
  41.0 4.5 %collective-permute-done.14.refs_3_ = bf16[2,128,256]{2,1,0:T(8,128)(2,1)S(1)} collective-permute-done((bf16[2,128,256]{2,1,0:T(8,128)(2,1)S(1)}, bf16[2,128,256]{2,1,0:T(8,128)(2,1)S(1)}, u32[]{:S(2)}, u32[]{:S(2)}) %collective-permute-start.14) | collective-permute-done | bytes 131104 | tf_op jit(solution)/shard_map/ppermute | solution.py:21
  51.1 2.0 %collective-permute-done.19.refs_3_ = bf16[2,128,256]{2,1,0:T(8,128)(2,1)S(1)} collective-permute-done((bf16[2,128,256]{2,1,0:T(8,128)(2,1)S(1)}, bf16[2,128,256]{2,1,0:T(8,128)(2,1)S(1)}, u32[]{:S(2)}, u32[]{:S(2)}) %collective-permute-start.19) | collective-permute-done | bytes 131104 | tf_op jit(solution)/shard_map/ppermute | solution.py:21
  53.4 2.2 %collective-permute-done.15.refs_1_ = bf16[128,1024]{1,0:T(8,128)(2,1)S(1)} collective-permute-done((bf16[128,1024]{1,0:T(8,128)(2,1)S(1)}, bf16[128,1024]{1,0:T(8,128)(2,1)S(1)}, u32[]{:S(2)}, u32[]{:S(2)}) %collective-permute-start.15) | collective-permute-done | bytes 262176 | tf_op jit(solution)/shard_map/ppermute | solution.py:21
  58.1 3.1 %collective-permute-done.22.refs_1_ = bf16[128,1024]{1,0:T(8,128)(2,1)S(1)} collective-permute-done((bf16[128,1024]{1,0:T(8,128)(2,1)S(1)}, bf16[128,1024]{1,0:T(8,128)(2,1)S(1)}, u32[]{:S(2)}, u32[]{:S(2)}) %collective-permute-start.22) | collective-permute-done | bytes 262176 | tf_op jit(solution)/shard_map/ppermute | solution.py:21
  61.4 2.5 %collective-permute-start.31 = (bf16[128,1024]{1,0:T(8,128)(2,1)S(1)}, bf16[128,1024]{1,0:T(8,128)(2,1)S(1)}, u32[]{:S(2)}, u32[]{:S(2)}) collective-permute-start(bf16[128,1024]{1,0:T(8,128)(2,1)S(1)} %get-tuple-element.206), channel_id=1, source_target_pairs={{0,1},{1,0},{2,3},{3,2},{4,5},{5,4},{6,7},{7,6},{8,9},{9,8},{10,11... | collective-permute-start | bytes 786440 | tf_op jit(solution)/shard_map/ppermute | solution.py:21
  64.5 2.3 %collective-permute-done.26.refs_1_ = bf16[128,1024]{1,0:T(8,128)(2,1)S(1)} collective-permute-done((bf16[128,1024]{1,0:T(8,128)(2,1)S(1)}, bf16[128,1024]{1,0:T(8,128)(2,1)S(1)}, u32[]{:S(2)}, u32[]{:S(2)}) %collective-permute-start.26) | collective-permute-done | bytes 262176 | tf_op jit(solution)/shard_map/ppermute | solution.py:21
  70.0 2.4 %collective-permute-done.31.refs_1_ = bf16[128,1024]{1,0:T(8,128)(2,1)S(1)} collective-permute-done((bf16[128,1024]{1,0:T(8,128)(2,1)S(1)}, bf16[128,1024]{1,0:T(8,128)(2,1)S(1)}, u32[]{:S(2)}, u32[]{:S(2)}) %collective-permute-start.31) | collective-permute-done | bytes 262176 | tf_op jit(solution)/shard_map/ppermute | solution.py:21
  75.3 1.8 %collective-permute-done.28.refs_1_ = bf16[128,1024]{1,0:T(8,128)(2,1)S(1)} collective-permute-done((bf16[128,1024]{1,0:T(8,128)(2,1)S(1)}, bf16[128,1024]{1,0:T(8,128)(2,1)S(1)}, u32[]{:S(2)}, u32[]{:S(2)}) %collective-permute-start.28) | collective-permute-done | bytes 262176 | tf_op jit(solution)/shard_map/ppermute | solution.py:21
  78.3 2.1 %collective-permute-start.35 = (bf16[128,1024]{1,0:T(8,128)(2,1)S(1)}, bf16[128,1024]{1,0:T(8,128)(2,1)S(1)}, u32[]{:S(2)}, u32[]{:S(2)}) collective-permute-start(bf16[128,1024]{1,0:T(8,128)(2,1)S(1)} %get-tuple-element.218), channel_id=1, source_target_pairs={{0,1},{1,0},{2,3},{3,2},{4,5},{5,4},{6,7},{7,6},{8,9},{9,8},{10,11... | collective-permute-start | bytes 786440 | tf_op jit(solution)/shard_map/ppermute | solution.py:21
  80.7 4.8 %collective-permute-done.35.refs_1_ = bf16[128,1024]{1,0:T(8,128)(2,1)S(1)} collective-permute-done((bf16[128,1024]{1,0:T(8,128)(2,1)S(1)}, bf16[128,1024]{1,0:T(8,128)(2,1)S(1)}, u32[]{:S(2)}, u32[]{:S(2)}) %collective-permute-start.35) | collective-permute-done | bytes 262176 | tf_op jit(solution)/shard_map/ppermute | solution.py:21
  89.6 6.4 %collective-permute-done.33.refs_1_ = bf16[2,128,256]{2,1,0:T(8,128)(2,1)S(1)} collective-permute-done((bf16[2,128,256]{2,1,0:T(8,128)(2,1)S(1)}, bf16[2,128,256]{2,1,0:T(8,128)(2,1)S(1)}, u32[]{:S(2)}, u32[]{:S(2)}) %collective-permute-start.33) | collective-permute-done | bytes 131104 | tf_op jit(solution)/shard_map/ppermute | solution.py:21
  101.1 7.5 %collective-permute-done.38.refs_1_ = bf16[2,128,256]{2,1,0:T(8,128)(2,1)S(1)} collective-permute-done((bf16[2,128,256]{2,1,0:T(8,128)(2,1)S(1)}, bf16[2,128,256]{2,1,0:T(8,128)(2,1)S(1)}, u32[]{:S(2)}, u32[]{:S(2)}) %collective-permute-start.38) | collective-permute-done | bytes 131104 | tf_op jit(solution)/shard_map/ppermute | solution.py:21
  110.1 1.8 %collective-permute-start.37 = (bf16[1,128,256]{2,1,0:T(8,128)(2,1)S(1)}, bf16[1,128,256]{2,1,0:T(8,128)(2,1)S(1)}, u32[]{:S(2)}, u32[]{:S(2)}) collective-permute-start(bf16[1,128,256]{2,1,0:T(8,128)(2,1)S(1)} %get-tuple-element.228), channel_id=1, source_target_pairs={{0,2},{1,3},{2,0},{3,1},{4,6},{5,7},{6,4},{7,5},{8,10},{9,11},{10,... | collective-permute-start | bytes 196616 | tf_op jit(solution)/shard_map/ppermute | solution.py:21
  113.1 1.9 %collective-permute-start.44 = (bf16[1,128,256]{2,1,0:T(8,128)(2,1)S(1)}, bf16[1,128,256]{2,1,0:T(8,128)(2,1)S(1)}, u32[]{:S(2)}, u32[]{:S(2)}) collective-permute-start(bf16[1,128,256]{2,1,0:T(8,128)(2,1)S(1)} %get-tuple-element.247), channel_id=1, source_target_pairs={{0,2},{1,3},{2,0},{3,1},{4,6},{5,7},{6,4},{7,5},{8,10},{9,11},{10,... | collective-permute-start | bytes 196616 | tf_op jit(solution)/shard_map/ppermute | solution.py:21
  117.7 1.9 %collective-permute-done.41.refs_3_ = bf16[1,128,256]{2,1,0:T(8,128)(2,1)S(1)} collective-permute-done((bf16[1,128,256]{2,1,0:T(8,128)(2,1)S(1)}, bf16[1,128,256]{2,1,0:T(8,128)(2,1)S(1)}, u32[]{:S(2)}, u32[]{:S(2)}) %collective-permute-start.41) | collective-permute-done | bytes 65568 | tf_op jit(solution)/shard_map/ppermute | solution.py:21
  (142 shorter events, 48.1 us)
Async XLA Ops:
  11.0 8.5 %collective-permute-start.6 = (bf16[128,1024]{1,0:T(8,128)(2,1)S(1)}, bf16[128,1024]{1,0:T(8,128)(2,1)S(1)}, u32[]{:S(2)}, u32[]{:S(2)}) collective-permute-start(bf16[128,1024]{1,0:T(8,128)(2,1)S(1)} %get-tuple-element.134), channel_id=1, source_target_pairs={{0,1},{1,0},{2,3},{3,2},{4,5},{5,4},{6,7},{7,6},{8,9},{9,8},{10,11... | collective-permute-start | bytes 786440 | tf_op jit(solution)/shard_map/ppermute | solution.py:21
  12.9 9.1 %collective-permute-start.1 = (bf16[64,1024]{1,0:T(8,128)(2,1)S(1)}, bf16[64,1024]{1,0:T(8,128)(2,1)S(1)}, u32[]{:S(2)}, u32[]{:S(2)}) collective-permute-start(bf16[64,1024]{1,0:T(8,128)(2,1)S(1)} %get-tuple-element.256.refs_0_), channel_id=1, source_target_pairs={{0,8},{4,12},{8,0},{12,4},{1,9},{5,13},{9,1},{13,5},{2,10},{6,14},... | collective-permute-start | bytes 393224 | tf_op jit(solution)/shard_map/ppermute | solution.py:21
  19.6 7.7 %collective-permute-start.9 = (bf16[128,1024]{1,0:T(8,128)(2,1)S(1)}, bf16[128,1024]{1,0:T(8,128)(2,1)S(1)}, u32[]{:S(2)}, u32[]{:S(2)}) collective-permute-start(bf16[128,1024]{1,0:T(8,128)(2,1)S(1)} %get-tuple-element.143), channel_id=1, source_target_pairs={{0,1},{1,0},{2,3},{3,2},{4,5},{5,4},{6,7},{7,6},{8,9},{9,8},{10,11... | collective-permute-start | bytes 786440 | tf_op jit(solution)/shard_map/ppermute | solution.py:21
  27.5 9.5 %collective-permute-start.10 = (bf16[128,1024]{1,0:T(8,128)(2,1)S(1)}, bf16[128,1024]{1,0:T(8,128)(2,1)S(1)}, u32[]{:S(2)}, u32[]{:S(2)}) collective-permute-start(bf16[128,1024]{1,0:T(8,128)(2,1)S(1)} %get-tuple-element.146), channel_id=1, source_target_pairs={{0,1},{1,0},{2,3},{3,2},{4,5},{5,4},{6,7},{7,6},{8,9},{9,8},{10,11... | collective-permute-start | bytes 786440 | tf_op jit(solution)/shard_map/ppermute | solution.py:21
  37.1 8.5 %collective-permute-start.13 = (bf16[128,1024]{1,0:T(8,128)(2,1)S(1)}, bf16[128,1024]{1,0:T(8,128)(2,1)S(1)}, u32[]{:S(2)}, u32[]{:S(2)}) collective-permute-start(bf16[128,1024]{1,0:T(8,128)(2,1)S(1)} %get-tuple-element.161), channel_id=1, source_target_pairs={{0,1},{1,0},{2,3},{3,2},{4,5},{5,4},{6,7},{7,6},{8,9},{9,8},{10,11... | collective-permute-start | bytes 786440 | tf_op jit(solution)/shard_map/ppermute | solution.py:21
  39.0 7.3 %collective-permute-start.11 = (bf16[128,1024]{1,0:T(8,128)(2,1)S(1)}, bf16[128,1024]{1,0:T(8,128)(2,1)S(1)}, u32[]{:S(2)}, u32[]{:S(2)}) collective-permute-start(bf16[128,1024]{1,0:T(8,128)(2,1)S(1)} %get-tuple-element.151), channel_id=1, source_target_pairs={{0,4},{1,2},{2,1},{3,7},{4,0},{5,6},{6,5},{7,3},{8,12},{9,10},{10,... | collective-permute-start | bytes 786440 | tf_op jit(solution)/shard_map/ppermute | solution.py:31
  39.9 8.2 %collective-permute-start.17 = (bf16[2,128,256]{2,1,0:T(8,128)(2,1)S(1)}, bf16[2,128,256]{2,1,0:T(8,128)(2,1)S(1)}, u32[]{:S(2)}, u32[]{:S(2)}) collective-permute-start(bf16[2,128,256]{2,1,0:T(8,128)(2,1)S(1)} %get-tuple-element.162.refs_1_), channel_id=1, source_target_pairs={{0,4},{4,0},{8,12},{12,8},{1,5},{5,1},{9,13},{13,9},{2,6},{6,2},{1... | collective-permute-start | bytes 393224 | tf_op jit(solution)/shard_map/ppermute | solution.py:21
  45.7 7.6 %collective-permute-start.16 = (bf16[128,1024]{1,0:T(8,128)(2,1)S(1)}, bf16[128,1024]{1,0:T(8,128)(2,1)S(1)}, u32[]{:S(2)}, u32[]{:S(2)}) collective-permute-start(bf16[128,1024]{1,0:T(8,128)(2,1)S(1)} %get-tuple-element.169), channel_id=1, source_target_pairs={{0,4},{1,2},{2,1},{3,7},{4,0},{5,6},{6,5},{7,3},{8,12},{9,10},{10,... | collective-permute-start | bytes 786440 | tf_op jit(solution)/shard_map/ppermute | solution.py:31
  46.4 9.2 %collective-permute-start.15 = (bf16[128,1024]{1,0:T(8,128)(2,1)S(1)}, bf16[128,1024]{1,0:T(8,128)(2,1)S(1)}, u32[]{:S(2)}, u32[]{:S(2)}) collective-permute-start(bf16[128,1024]{1,0:T(8,128)(2,1)S(1)} %get-tuple-element.167), channel_id=1, source_target_pairs={{0,1},{1,0},{2,3},{3,2},{4,5},{5,4},{6,7},{7,6},{8,9},{9,8},{10,11... | collective-permute-start | bytes 786440 | tf_op jit(solution)/shard_map/ppermute | solution.py:21
  49.0 12.2 %collective-permute-start.22 = (bf16[128,1024]{1,0:T(8,128)(2,1)S(1)}, bf16[128,1024]{1,0:T(8,128)(2,1)S(1)}, u32[]{:S(2)}, u32[]{:S(2)}) collective-permute-start(bf16[128,1024]{1,0:T(8,128)(2,1)S(1)} %get-tuple-element.185), channel_id=1, source_target_pairs={{0,1},{1,0},{2,3},{3,2},{4,5},{5,4},{6,7},{7,6},{8,9},{9,8},{10,11... | collective-permute-start | bytes 786440 | tf_op jit(solution)/shard_map/ppermute | solution.py:21
  56.1 7.8 %collective-permute-start.21 = (bf16[2,128,256]{2,1,0:T(8,128)(2,1)S(1)}, bf16[2,128,256]{2,1,0:T(8,128)(2,1)S(1)}, u32[]{:S(2)}, u32[]{:S(2)}) collective-permute-start(bf16[2,128,256]{2,1,0:T(8,128)(2,1)S(1)} %get-tuple-element.184.refs_1_), channel_id=1, source_target_pairs={{0,8},{4,12},{8,0},{12,4},{1,9},{5,13},{9,1},{13,5},{2,10},{6,14},... | collective-permute-start | bytes 393224 | tf_op jit(solution)/shard_map/ppermute | solution.py:21
  56.5 10.3 %collective-permute-start.26 = (bf16[128,1024]{1,0:T(8,128)(2,1)S(1)}, bf16[128,1024]{1,0:T(8,128)(2,1)S(1)}, u32[]{:S(2)}, u32[]{:S(2)}) collective-permute-start(bf16[128,1024]{1,0:T(8,128)(2,1)S(1)} %get-tuple-element.195), channel_id=1, source_target_pairs={{0,1},{1,0},{2,3},{3,2},{4,5},{5,4},{6,7},{7,6},{8,9},{9,8},{10,11... | collective-permute-start | bytes 786440 | tf_op jit(solution)/shard_map/ppermute | solution.py:21
  61.3 7.5 %collective-permute-start.27 = (bf16[128,1024]{1,0:T(8,128)(2,1)S(1)}, bf16[128,1024]{1,0:T(8,128)(2,1)S(1)}, u32[]{:S(2)}, u32[]{:S(2)}) collective-permute-start(bf16[128,1024]{1,0:T(8,128)(2,1)S(1)} %get-tuple-element.200), channel_id=1, source_target_pairs={{0,4},{1,2},{2,1},{3,7},{4,0},{5,6},{6,5},{7,3},{8,12},{9,10},{10,... | collective-permute-start | bytes 786440 | tf_op jit(solution)/shard_map/ppermute | solution.py:31
  61.4 11.1 %collective-permute-start.31 = (bf16[128,1024]{1,0:T(8,128)(2,1)S(1)}, bf16[128,1024]{1,0:T(8,128)(2,1)S(1)}, u32[]{:S(2)}, u32[]{:S(2)}) collective-permute-start(bf16[128,1024]{1,0:T(8,128)(2,1)S(1)} %get-tuple-element.206), channel_id=1, source_target_pairs={{0,1},{1,0},{2,3},{3,2},{4,5},{5,4},{6,7},{7,6},{8,9},{9,8},{10,11... | collective-permute-start | bytes 786440 | tf_op jit(solution)/shard_map/ppermute | solution.py:21
  69.1 8.1 %collective-permute-start.28 = (bf16[128,1024]{1,0:T(8,128)(2,1)S(1)}, bf16[128,1024]{1,0:T(8,128)(2,1)S(1)}, u32[]{:S(2)}, u32[]{:S(2)}) collective-permute-start(bf16[128,1024]{1,0:T(8,128)(2,1)S(1)} %get-tuple-element.203), channel_id=1, source_target_pairs={{0,1},{1,0},{2,3},{3,2},{4,5},{5,4},{6,7},{7,6},{8,9},{9,8},{10,11... | collective-permute-start | bytes 786440 | tf_op jit(solution)/shard_map/ppermute | solution.py:21
  86.7 9.3 %collective-permute-start.40 = (bf16[128,1024]{1,0:T(8,128)(2,1)S(1)}, bf16[128,1024]{1,0:T(8,128)(2,1)S(1)}, u32[]{:S(2)}, u32[]{:S(2)}) collective-permute-start(bf16[128,1024]{1,0:T(8,128)(2,1)S(1)} %get-tuple-element.234), channel_id=1, source_target_pairs={{0,1},{1,0},{2,3},{3,2},{4,5},{5,4},{6,7},{7,6},{8,9},{9,8},{10,11... | collective-permute-start | bytes 786440 | tf_op jit(solution)/shard_map/ppermute | solution.py:21
  88.6 8.6 %collective-permute-start.39 = (bf16[128,1024]{1,0:T(8,128)(2,1)S(1)}, bf16[128,1024]{1,0:T(8,128)(2,1)S(1)}, u32[]{:S(2)}, u32[]{:S(2)}) collective-permute-start(bf16[128,1024]{1,0:T(8,128)(2,1)S(1)} %get-tuple-element.232), channel_id=1, source_target_pairs={{0,4},{1,2},{2,1},{3,7},{4,0},{5,6},{6,5},{7,3},{8,12},{9,10},{10,... | collective-permute-start | bytes 786440 | tf_op jit(solution)/shard_map/ppermute | solution.py:31
  88.7 7.3 %collective-permute-start.33 = (bf16[2,128,256]{2,1,0:T(8,128)(2,1)S(1)}, bf16[2,128,256]{2,1,0:T(8,128)(2,1)S(1)}, u32[]{:S(2)}, u32[]{:S(2)}) collective-permute-start(bf16[2,128,256]{2,1,0:T(8,128)(2,1)S(1)} %get-tuple-element.213), channel_id=1, source_target_pairs={{0,1},{1,0},{2,3},{3,2},{4,5},{5,4},{6,7},{7,6},{8,9},{9,8},{10,11... | collective-permute-start | bytes 393224 | tf_op jit(solution)/shard_map/ppermute | solution.py:21
  97.3 11.3 %collective-permute-start.43 = (bf16[128,1024]{1,0:T(8,128)(2,1)S(1)}, bf16[128,1024]{1,0:T(8,128)(2,1)S(1)}, u32[]{:S(2)}, u32[]{:S(2)}) collective-permute-start(bf16[128,1024]{1,0:T(8,128)(2,1)S(1)} %get-tuple-element.243), channel_id=1, source_target_pairs={{0,1},{1,0},{2,3},{3,2},{4,5},{5,4},{6,7},{7,6},{8,9},{9,8},{10,11... | collective-permute-start | bytes 786440 | tf_op jit(solution)/shard_map/ppermute | solution.py:21
  99.0 9.5 %collective-permute-start.38 = (bf16[2,128,256]{2,1,0:T(8,128)(2,1)S(1)}, bf16[2,128,256]{2,1,0:T(8,128)(2,1)S(1)}, u32[]{:S(2)}, u32[]{:S(2)}) collective-permute-start(bf16[2,128,256]{2,1,0:T(8,128)(2,1)S(1)} %get-tuple-element.230), channel_id=1, source_target_pairs={{0,1},{1,0},{2,3},{3,2},{4,5},{5,4},{6,7},{7,6},{8,9},{9,8},{10,11... | collective-permute-start | bytes 393224 | tf_op jit(solution)/shard_map/ppermute | solution.py:21
  99.4 13.6 %collective-permute-start.42 = (bf16[2,128,256]{2,1,0:T(8,128)(2,1)S(1)}, bf16[2,128,256]{2,1,0:T(8,128)(2,1)S(1)}, u32[]{:S(2)}, u32[]{:S(2)}) collective-permute-start(bf16[2,128,256]{2,1,0:T(8,128)(2,1)S(1)} %get-tuple-element.241), channel_id=1, source_target_pairs={{0,1},{1,0},{2,3},{3,2},{4,5},{5,4},{6,7},{7,6},{8,9},{9,8},{10,11... | collective-permute-start | bytes 393224 | tf_op jit(solution)/shard_map/ppermute | solution.py:21
  110.1 7.6 %collective-permute-start.37 = (bf16[1,128,256]{2,1,0:T(8,128)(2,1)S(1)}, bf16[1,128,256]{2,1,0:T(8,128)(2,1)S(1)}, u32[]{:S(2)}, u32[]{:S(2)}) collective-permute-start(bf16[1,128,256]{2,1,0:T(8,128)(2,1)S(1)} %get-tuple-element.228), channel_id=1, source_target_pairs={{0,2},{1,3},{2,0},{3,1},{4,6},{5,7},{6,4},{7,5},{8,10},{9,11},{10,... | collective-permute-start | bytes 196616 | tf_op jit(solution)/shard_map/ppermute | solution.py:21
  111.9 7.7 %collective-permute-start.41 = (bf16[1,128,256]{2,1,0:T(8,128)(2,1)S(1)}, bf16[1,128,256]{2,1,0:T(8,128)(2,1)S(1)}, u32[]{:S(2)}, u32[]{:S(2)}) collective-permute-start(bf16[1,128,256]{2,1,0:T(8,128)(2,1)S(1)} %get-tuple-element.239), channel_id=1, source_target_pairs={{0,2},{1,3},{2,0},{3,1},{4,6},{5,7},{6,4},{7,5},{8,10},{9,11},{10,... | collective-permute-start | bytes 196616 | tf_op jit(solution)/shard_map/ppermute | solution.py:21
  113.1 7.9 %collective-permute-start.44 = (bf16[1,128,256]{2,1,0:T(8,128)(2,1)S(1)}, bf16[1,128,256]{2,1,0:T(8,128)(2,1)S(1)}, u32[]{:S(2)}, u32[]{:S(2)}) collective-permute-start(bf16[1,128,256]{2,1,0:T(8,128)(2,1)S(1)} %get-tuple-element.247), channel_id=1, source_target_pairs={{0,2},{1,3},{2,0},{3,1},{4,6},{5,7},{6,4},{7,5},{8,10},{9,11},{10,... | collective-permute-start | bytes 196616 | tf_op jit(solution)/shard_map/ppermute | solution.py:21
  (32 other events, 179.3 us)

commit v4 on v3

--- a/solution.py
+++ b/solution.py
@@ -227,14 +227,14 @@
         part_ref[block, :] = dot(attended, weight_ref[0]).astype(part_ref.dtype)
 
 
-def mlp_kernel(
-    count, wide_ref, arrived_ref, gain_ref, gate_up_ref, down_ref, kept_ref, sent_ref, rows_ref, act_ref
-):
+def mlp_kernel(count, whole, wide_ref, arrived_ref, gain_ref, gate_up_ref, down_ref, *refs):
+    kept_ref, sent_ref, rows_ref, act_ref = refs
     choose(wide_ref, arrived_ref, rows_ref)
     index = lax.axis_index("hidden")
     hidden = act_ref.shape[1]
     step = min(hidden, 256)
-    width = kept_ref.shape[2]
+    width = down_ref.shape[2] // count
+    own = pl.ds(pl.multiple_of(index * width, width), width)
     for block in row_blocks(rows_ref.shape[0]):
         normed = normalize(rows_ref[block, :], gain_ref[0, 1:2, :]).astype(BF16)
         for start in range(0, hidden, step):
@@ -242,6 +242,12 @@
             gate_sum = dot(normed, gate_up_ref[0, 0, :, columns])
             upper_sum = dot(normed, gate_up_ref[0, 1, :, columns])
             act_ref[:, columns] = (jax.nn.silu(gate_sum) * upper_sum).astype(BF16)
+        if whole:
+            total = dot(act_ref[...], down_ref[0])
+            sent_ref[block, :] = total.astype(BF16)
+            kept_ref[block, :] = total
+            kept_ref[block, own] = kept_ref[block, own] + rows_ref[block, own]
+            continue
         for i in range(count // 2):
             owner = index ^ (2 * i)
             columns = pl.ds(pl.multiple_of((owner ^ 1) * width, width), width)
@@ -255,21 +261,58 @@
             kept_ref[i, block, :] = total
 
 
+def gather_kernel(mine_ref, arrived_ref, wide_ref, sent_ref):
+    index = lax.axis_index("hidden")
+    width = wide_ref.shape[2]
+    far = lax.axis_size("hidden") - 1 - index
+
+    def columns(owner):
+        return pl.ds(pl.multiple_of(owner * width, width), width)
+
+    def total(owner):
+        return mine_ref[:, columns(owner)] + arrived_ref[:, columns(owner)].astype(F32)
+
+    wide_ref[0] = total(index)
+    wide_ref[1] = mine_ref[:, columns(index ^ 1)]
+    sent_ref[0] = total(far).astype(BF16)
+    sent_ref[1] = total(far ^ 1).astype(BF16)
+
+
+def return_kernel(wide_ref, arrived_ref, own_ref, sent_ref):
+    own_ref[...] = wide_ref[0] + arrived_ref[0].astype(F32)
+    sent_ref[...] = (wide_ref[1] + arrived_ref[1].astype(F32)).astype(BF16)
+
+
 def halve_kernel(mine_ref, arrived_ref, wide_ref, sent_ref):
     kept = wide_ref.shape[0]
     wide_ref[...] = mine_ref[:kept] + arrived_ref[:kept].astype(F32)
     sent_ref[...] = (mine_ref[kept:] + arrived_ref[kept:].astype(F32)).astype(BF16)
 
 
-def final_kernel(count, *refs):
+def final_kernel(count, routes, *refs):
     *in_refs, out_ref, rows_ref, sems = refs
-    chunks = len(in_refs) // 2
+    chunks = rows_ref.shape[0]
     stride = out_ref.shape[1] // count
     size = stride // chunks
+    width = out_ref.shape[2]
+    index = lax.axis_index("hidden")
     copies = []
     for chunk in range(chunks):
-        wide_ref, arrived_ref = in_refs[2 * chunk : 2 * chunk + 2]
-        rows_ref[chunk] = wide_ref[0] + arrived_ref[0].astype(F32)
+        if routes[chunk]:
+            own_ref, mine_ref, arrived_ref, *in_refs = in_refs
+
+            @pl.when(is_middle())
+            def _():
+                rows_ref[chunk] = own_ref[...]
+
+            @pl.when(jnp.logical_not(is_middle()))
+            def _():
+                mine = mine_ref[:, pl.ds(pl.multiple_of(index * width, width), width)]
+                rows_ref[chunk] = mine + arrived_ref[...].astype(F32)
+
+        else:
+            wide_ref, arrived_ref, *in_refs = in_refs
+            rows_ref[chunk] = wide_ref[0] + arrived_ref[0].astype(F32)
         for i in range(count):
             source = rows_ref.at[chunk, pl.ds(i * size, size), :]
             target = out_ref.at[0, pl.ds(i * stride + chunk * size, size), :]
@@ -328,21 +371,30 @@
                 functools.partial(embed_kernel, c), "embed", [sent], [earlier, embed_table]
             )[0]
 
-    def mix(c, older, part, terms, names):
-        s, o = get(c), get(older)
-        if s is None and o is None:
+    def exchange(t):
+        giver = get(t) if get(t) is not None else get(t - 4)
+        name = "part"
+        if giver is None and get(t - 8) is not None and get(t - 6) is not None:
+            giver, name = get(t - 8), "sums_sent"
+        early = get(t - 2)
+        taker = early if early is not None else get(t - 6)
+        if giver is None and taker is None:
             return
-        args = [s[part]] if s is not None else []
-        given = [o[term] for term in terms] if o is not None else []
-        outs = [wide, sent] if given else [sent]
+        names = ["total", "far", "embedded"] if early is not None else ["x_zero", "total", "far"]
+        parts = [giver[name]] if giver is not None else []
+        terms = [taker[name] for name in names] if taker is not None else []
         *finished, out = step(
-            functools.partial(mix_kernel, len(given)), names[0], outs, [*args, *given]
+            functools.partial(mix_kernel, len(terms)),
+            "exchange",
+            [wide, sent] if terms else [sent],
+            [*parts, *terms],
         )
         arrived = swap(out, "hidden", pair_bit)
-        if s is not None:
-            s["arrived"] = arrived
-        if o is not None:
-            o[names[0]], o[names[1]] = finished[0], arrived
+        if giver is not None:
+            giver["arrived"] = arrived
+        if taker is not None:
+            done = "x_zero" if early is not None else "residual"
+            taker[done], taker[done + "_arrived"] = finished[0], arrived
 
     def pair_sum(c):
         if (s := get(c)) is not None:
@@ -355,7 +407,7 @@
                 qkv_kernel,
                 "qkv",
                 [((rows, local_width), BF16), ((2, rows, local_width), BF16)],
-                [s["x_zero"], s["x_arrived"], norm_gains, qkv_weight],
+                [s["x_zero"], s["x_zero_arrived"], norm_gains, qkv_weight],
                 [pltpu.VMEM((rows, width), F32)],
             )
             s["kvs"] = {0: kv} | {bit: swap(kv, "codebook", bit) for bit in code_bits}
@@ -376,30 +428,53 @@
                 [s["query"], *[s["kvs"][slot] for slot in range(code_count)], out_weight],
             )[0]
 
+    def rides(c):
+        return c + 8 < CHUNKS + 6
+
     def mlp(c):
         if (s := get(c)) is not None:
-            shape = (hidden_count // 2, rows, local_width)
-            s["sums"], out = step(
-                functools.partial(mlp_kernel, hidden_count),
+            shape = (rows, width) if rides(c) else (hidden_count // 2, rows, local_width)
+            s["sums"], s["sums_sent"] = step(
+                functools.partial(mlp_kernel, hidden_count, rides(c)),
                 "mlp",
                 [(shape, F32), (shape, BF16)],
                 [s["residual"], s["residual_arrived"], norm_gains, gate_up, down_weight],
                 [pltpu.VMEM((rows, width), F32), pltpu.VMEM((min(rows, 128), gate_up.shape[3]), BF16)],
             )
-            s["sums_arrived"] = swap(out, "hidden", pair_bit)
+            if not rides(c):
+                s["arrived"] = swap(s["sums_sent"], "hidden", pair_bit)
 
     def halve(c):
-        if (s := get(c)) is not None:
+        if (s := get(c)) is not None and not rides(c):
             shape = (hidden_count // 4, rows, local_width)
             s["wide"], out = step(
-                halve_kernel, "halve", [(shape, F32), (shape, BF16)], [s["sums"], s["sums_arrived"]]
+                halve_kernel, "halve", [(shape, F32), (shape, BF16)], [s["sums"], s["arrived"]]
             )
             s["last"] = swap(out, "hidden", far_bit)
 
+    def collect(c):
+        if (s := get(c)) is not None and rides(c):
+            shape = (2, rows, local_width)
+            s["wide"], out = step(
+                gather_kernel, "gather", [(shape, F32), (shape, BF16)], [s["sums"], s["arrived"]]
+            )
+            s["far"] = middle_swap(out)
+
+    def give_back(c):
+        if (s := get(c)) is not None and rides(c):
+            shape = (rows, local_width)
+            s["own"], out = step(
+                return_kernel, "return", [(shape, F32), (shape, BF16)], [s["wide"], s["far"]]
+            )
+            s["last"] = swap(out, "hidden", pair_bit)
+
     def final():
-        args = [s[name] for s in states for name in ("wide", "last")]
+        routes = [rides(c) for c in range(CHUNKS)]
+        args = []
+        for s, ridden in zip(states, routes):
+            args += [s[name] for name in (("own", "sums", "last") if ridden else ("wide", "last"))]
         return step(
-            functools.partial(final_kernel, code_count),
+            functools.partial(final_kernel, code_count, routes),
             "final",
             [((1, row_count, local_width), F32)],
             args,
@@ -411,16 +486,17 @@
     project(0)
     for t in range(CHUNKS + stages - 1):
         pair_sum(t - 1)
-        mix(t, t - 2, "part", ["total", "far", "embedded"], ["x_zero", "x_arrived"])
+        pair_sum(t - 5)
+        exchange(t)
         qkv(t - 3)
-        attend(t - 4)
         mlp(t - 7)
-        mix(t - 4, t - 6, "part", ["x_zero", "total", "far"], ["residual", "residual_arrived"])
-        pair_sum(t - 5)
+        collect(t - 9)
+        give_back(t - 10)
         halve(t - 8)
         project(t + 1)
         embed(t - 1)
         forward(t - 3)
+        attend(t - 3)
     return final()
 
 

time: 124 us -> 113 us (0.911)
  waiting for transfers between devices: 61.2 us -> 45.1 us
  starting transfers between devices: 40.5 us -> 46.1 us
    ppermute x38 -> x34, waiting for transfers between devices: 60.9 us -> 44.8 us  [swap(): return lax.ppermute(block, axis, [(i, i ^ distance) for i in range(count)])]
    ppermute x38 -> x34, starting transfers between devices: 37.2 us -> 43.5 us  [swap(): return lax.ppermute(block, axis, [(i, i ^ distance) for i in range(count)])]
  transfers between devices with their start and end apart: 47 -> 45, of which waited for: 23 -> 25; matrix products, arithmetic and copies ran while one was open for 0% -> 0% of each run, Pallas kernels for 13% -> 12%
where the time goes in v4:
time: 113 us
  starting transfers between devices  46.1 us (41%)
  waiting for transfers between devices  45.1 us (40%)
  Pallas kernels  18.1 us (16%)
  local copies, waits for them, and re-layouts  2.66 us (2%)
    ppermute x34, waiting for transfers between devices, swap(): return lax.ppermute(block, axis, [(i, i ^ distance) for i in range(count)])  44.8 us
    ppermute x34, starting transfers between devices, swap(): return lax.ppermute(block, axis, [(i, i ^ distance) for i in range(count)])  43.5 us
    pallas_call x49, Pallas kernels, __call__(): pl.pallas_call(with_token, name=name, out_shape=[jax.ShapeDtypeStruct(sha...  18.1 us
    ppermute x1, starting transfers between devices, shifted(): return lax.ppermute(block, axis, route)  2.4 us
  transfers between devices with their start and end apart: 45, of which 25 were waited for; matrix products, arithmetic and copies ran while one was open for 0% of the time, Pallas kernels for 12%

profile of v4, /device:TPU:0, one launch (start us, length us, event | category | flops | bytes accessed | tf_op | source)
XLA Modules:
  0.0 112.7 jit_solution(866843570899177065)
XLA Ops:
  1.0 3.0 %collective-permute-start.4 = (bf16[64,1024]{1,0:T(8,128)(2,1)S(1)}, bf16[64,1024]{1,0:T(8,128)(2,1)S(1)}, u32[]{:S(2)}, u32[]{:S(2)}) collective-permute-start(bf16[64,1024]{1,0:T(8,128)(2,1)S(1)} %get-tuple-element.259.refs_0_), channel_id=1, source_target_pairs={{0,8},{4,12},{8,0},{12,4},{1,9},{5,13},{9,1},{13,5},{2,10},{6,14},... | collective-permute-start | bytes 393224 | tf_op jit(solution)/shard_map/ppermute | solution.py:21
  4.0 3.5 %collective-permute-done.4.refs_2_ = bf16[64,1024]{1,0:T(8,128)(2,1)S(1)} collective-permute-done((bf16[64,1024]{1,0:T(8,128)(2,1)S(1)}, bf16[64,1024]{1,0:T(8,128)(2,1)S(1)}, u32[]{:S(2)}, u32[]{:S(2)}) %collective-permute-start.4) | collective-permute-done | bytes 131104 | tf_op jit(solution)/shard_map/ppermute | solution.py:21
  11.0 1.9 %collective-permute-start.6 = (bf16[128,1024]{1,0:T(8,128)(2,1)S(1)}, bf16[128,1024]{1,0:T(8,128)(2,1)S(1)}, u32[]{:S(2)}, u32[]{:S(2)}) collective-permute-start(bf16[128,1024]{1,0:T(8,128)(2,1)S(1)} %get-tuple-element.136), channel_id=1, source_target_pairs={{0,1},{1,0},{2,3},{3,2},{4,5},{5,4},{6,7},{7,6},{8,9},{9,8},{10,11... | collective-permute-start | bytes 786440 | tf_op jit(solution)/shard_map/ppermute | solution.py:21
  14.9 4.6 %collective-permute-done.6.refs_1_ = bf16[128,1024]{1,0:T(8,128)(2,1)S(1)} collective-permute-done((bf16[128,1024]{1,0:T(8,128)(2,1)S(1)}, bf16[128,1024]{1,0:T(8,128)(2,1)S(1)}, u32[]{:S(2)}, u32[]{:S(2)}) %collective-permute-start.6) | collective-permute-done | bytes 262176 | tf_op jit(solution)/shard_map/ppermute | solution.py:21
  19.6 1.8 %collective-permute-start.9 = (bf16[128,1024]{1,0:T(8,128)(2,1)S(1)}, bf16[128,1024]{1,0:T(8,128)(2,1)S(1)}, u32[]{:S(2)}, u32[]{:S(2)}) collective-permute-start(bf16[128,1024]{1,0:T(8,128)(2,1)S(1)} %get-tuple-element.145), channel_id=1, source_target_pairs={{0,1},{1,0},{2,3},{3,2},{4,5},{5,4},{6,7},{7,6},{8,9},{9,8},{10,11... | collective-permute-start | bytes 786440 | tf_op jit(solution)/shard_map/ppermute | solution.py:21
  22.0 2.4 %collective-permute-start.8 = (s32[4,128]{1,0:T(4,128)S(1)}, s32[4,128]{1,0:T(4,128)S(1)}, u32[]{:S(2)}, u32[]{:S(2)}) collective-permute-start(s32[4,128]{1,0:T(4,128)S(1)} %bitcast.1), channel_id=1, source_target_pairs={{0,4},{4,8},{8,12},{1,5},{5,9},{9,13},{2,6},{6,10},{10,14},{3,7},{... | collective-permute-start | bytes 6152 | tf_op jit(solution)/shard_map/ppermute | solution.py:47
  27.5 2.8 %collective-permute-start.10 = (bf16[128,1024]{1,0:T(8,128)(2,1)S(1)}, bf16[128,1024]{1,0:T(8,128)(2,1)S(1)}, u32[]{:S(2)}, u32[]{:S(2)}) collective-permute-start(bf16[128,1024]{1,0:T(8,128)(2,1)S(1)} %get-tuple-element.149), channel_id=1, source_target_pairs={{0,1},{1,0},{2,3},{3,2},{4,5},{5,4},{6,7},{7,6},{8,9},{9,8},{10,11... | collective-permute-start | bytes 786440 | tf_op jit(solution)/shard_map/ppermute | solution.py:21
  31.7 5.3 %collective-permute-done.10.refs_1_ = bf16[128,1024]{1,0:T(8,128)(2,1)S(1)} collective-permute-done((bf16[128,1024]{1,0:T(8,128)(2,1)S(1)}, bf16[128,1024]{1,0:T(8,128)(2,1)S(1)}, u32[]{:S(2)}, u32[]{:S(2)}) %collective-permute-start.10) | collective-permute-done | bytes 262176 | tf_op jit(solution)/shard_map/ppermute | solution.py:21
  38.0 1.8 %collective-permute-start.16 = (bf16[128,1024]{1,0:T(8,128)(2,1)S(1)}, bf16[128,1024]{1,0:T(8,128)(2,1)S(1)}, u32[]{:S(2)}, u32[]{:S(2)}) collective-permute-start(bf16[128,1024]{1,0:T(8,128)(2,1)S(1)} %get-tuple-element.169), channel_id=1, source_target_pairs={{0,1},{1,0},{2,3},{3,2},{4,5},{5,4},{6,7},{7,6},{8,9},{9,8},{10,11... | collective-permute-start | bytes 786440 | tf_op jit(solution)/shard_map/ppermute | solution.py:21
  46.4 1.7 %collective-permute-start.19 = (bf16[2,128,256]{2,1,0:T(8,128)(2,1)S(1)}, bf16[2,128,256]{2,1,0:T(8,128)(2,1)S(1)}, u32[]{:S(2)}, u32[]{:S(2)}) collective-permute-start(bf16[2,128,256]{2,1,0:T(8,128)(2,1)S(1)} %get-tuple-element.177.refs_1_), channel_id=1, source_target_pairs={{0,8},{4,12},{8,0},{12,4},{1,9},{5,13},{9,1},{13,5},{2,10},{6,14},... | collective-permute-start | bytes 393224 | tf_op jit(solution)/shard_map/ppermute | solution.py:21
  48.1 1.7 %collective-permute-start.17 = (bf16[128,1024]{1,0:T(8,128)(2,1)S(1)}, bf16[128,1024]{1,0:T(8,128)(2,1)S(1)}, u32[]{:S(2)}, u32[]{:S(2)}) collective-permute-start(bf16[128,1024]{1,0:T(8,128)(2,1)S(1)} %get-tuple-element.173), channel_id=1, source_target_pairs={{0,1},{1,0},{2,3},{3,2},{4,5},{5,4},{6,7},{7,6},{8,9},{9,8},{10,11... | collective-permute-start | bytes 786440 | tf_op jit(solution)/shard_map/ppermute | solution.py:21
  56.6 1.8 %collective-permute-start.26 = (bf16[128,1024]{1,0:T(8,128)(2,1)S(1)}, bf16[128,1024]{1,0:T(8,128)(2,1)S(1)}, u32[]{:S(2)}, u32[]{:S(2)}) collective-permute-start(bf16[128,1024]{1,0:T(8,128)(2,1)S(1)} %get-tuple-element.197), channel_id=1, source_target_pairs={{0,1},{1,0},{2,3},{3,2},{4,5},{5,4},{6,7},{7,6},{8,9},{9,8},{10,11... | collective-permute-start | bytes 786440 | tf_op jit(solution)/shard_map/ppermute | solution.py:21
  62.4 1.7 %collective-permute-done.26.refs_1_ = bf16[128,1024]{1,0:T(8,128)(2,1)S(1)} collective-permute-done((bf16[128,1024]{1,0:T(8,128)(2,1)S(1)}, bf16[128,1024]{1,0:T(8,128)(2,1)S(1)}, u32[]{:S(2)}, u32[]{:S(2)}) %collective-permute-start.26) | collective-permute-done | bytes 262176 | tf_op jit(solution)/shard_map/ppermute | solution.py:21
  65.4 1.8 %collective-permute-start.27 = (bf16[128,1024]{1,0:T(8,128)(2,1)S(1)}, bf16[128,1024]{1,0:T(8,128)(2,1)S(1)}, u32[]{:S(2)}, u32[]{:S(2)}) collective-permute-start(bf16[128,1024]{1,0:T(8,128)(2,1)S(1)} %get-tuple-element.201), channel_id=1, source_target_pairs={{0,1},{1,0},{2,3},{3,2},{4,5},{5,4},{6,7},{7,6},{8,9},{9,8},{10,11... | collective-permute-start | bytes 786440 | tf_op jit(solution)/shard_map/ppermute | solution.py:21
  67.7 2.3 %collective-permute-done.29.refs_3_ = bf16[2,128,256]{2,1,0:T(8,128)(2,1)S(1)} collective-permute-done((bf16[2,128,256]{2,1,0:T(8,128)(2,1)S(1)}, bf16[2,128,256]{2,1,0:T(8,128)(2,1)S(1)}, u32[]{:S(2)}, u32[]{:S(2)}) %collective-permute-start.29) | collective-permute-done | bytes 131104 | tf_op jit(solution)/shard_map/ppermute | solution.py:21
  73.0 1.9 %collective-permute-start.33 = (bf16[128,1024]{1,0:T(8,128)(2,1)S(1)}, bf16[128,1024]{1,0:T(8,128)(2,1)S(1)}, u32[]{:S(2)}, u32[]{:S(2)}) collective-permute-start(bf16[128,1024]{1,0:T(8,128)(2,1)S(1)} %get-tuple-element.219), channel_id=1, source_target_pairs={{0,1},{1,0},{2,3},{3,2},{4,5},{5,4},{6,7},{7,6},{8,9},{9,8},{10,11... | collective-permute-start | bytes 786440 | tf_op jit(solution)/shard_map/ppermute | solution.py:21
  76.1 4.8 %collective-permute-done.33.refs_1_ = bf16[128,1024]{1,0:T(8,128)(2,1)S(1)} collective-permute-done((bf16[128,1024]{1,0:T(8,128)(2,1)S(1)}, bf16[128,1024]{1,0:T(8,128)(2,1)S(1)}, u32[]{:S(2)}, u32[]{:S(2)}) %collective-permute-start.33) | collective-permute-done | bytes 262176 | tf_op jit(solution)/shard_map/ppermute | solution.py:21
  81.1 2.1 %collective-permute-start.34 = (bf16[128,1024]{1,0:T(8,128)(2,1)S(1)}, bf16[128,1024]{1,0:T(8,128)(2,1)S(1)}, u32[]{:S(2)}, u32[]{:S(2)}) collective-permute-start(bf16[128,1024]{1,0:T(8,128)(2,1)S(1)} %get-tuple-element.222), channel_id=1, source_target_pairs={{0,1},{1,0},{2,3},{3,2},{4,5},{5,4},{6,7},{7,6},{8,9},{9,8},{10,11... | collective-permute-start | bytes 786440 | tf_op jit(solution)/shard_map/ppermute | solution.py:21
  84.5 5.3 %collective-permute-start.37 = (bf16[128,1024]{1,0:T(8,128)(2,1)S(1)}, bf16[128,1024]{1,0:T(8,128)(2,1)S(1)}, u32[]{:S(2)}, u32[]{:S(2)}) collective-permute-start(bf16[128,1024]{1,0:T(8,128)(2,1)S(1)} %get-tuple-element.235), channel_id=1, source_target_pairs={{0,1},{1,0},{2,3},{3,2},{4,5},{5,4},{6,7},{7,6},{8,9},{9,8},{10,11... | collective-permute-start | bytes 786440 | tf_op jit(solution)/shard_map/ppermute | solution.py:21
  91.6 2.3 %collective-permute-start.40 = (bf16[2,128,256]{2,1,0:T(8,128)(2,1)S(1)}, bf16[2,128,256]{2,1,0:T(8,128)(2,1)S(1)}, u32[]{:S(2)}, u32[]{:S(2)}) collective-permute-start(bf16[2,128,256]{2,1,0:T(8,128)(2,1)S(1)} %get-tuple-element.245), channel_id=1, source_target_pairs={{0,1},{1,0},{2,3},{3,2},{4,5},{5,4},{6,7},{7,6},{8,9},{9,8},{10,11... | collective-permute-start | bytes 393224 | tf_op jit(solution)/shard_map/ppermute | solution.py:21
  93.9 2.3 %collective-permute-done.37.refs_1_ = bf16[128,1024]{1,0:T(8,128)(2,1)S(1)} collective-permute-done((bf16[128,1024]{1,0:T(8,128)(2,1)S(1)}, bf16[128,1024]{1,0:T(8,128)(2,1)S(1)}, u32[]{:S(2)}, u32[]{:S(2)}) %collective-permute-start.37) | collective-permute-done | bytes 262176 | tf_op jit(solution)/shard_map/ppermute | solution.py:21
  97.5 1.9 %collective-permute-start.43 = (bf16[2,128,256]{2,1,0:T(8,128)(2,1)S(1)}, bf16[2,128,256]{2,1,0:T(8,128)(2,1)S(1)}, u32[]{:S(2)}, u32[]{:S(2)}) collective-permute-start(bf16[2,128,256]{2,1,0:T(8,128)(2,1)S(1)} %get-tuple-element.253), channel_id=1, source_target_pairs={{0,1},{1,0},{2,3},{3,2},{4,5},{5,4},{6,7},{7,6},{8,9},{9,8},{10,11... | collective-permute-start | bytes 393224 | tf_op jit(solution)/shard_map/ppermute | solution.py:21
  99.7 2.5 %collective-permute-start.42 = (bf16[1,128,256]{2,1,0:T(8,128)(2,1)S(1)}, bf16[1,128,256]{2,1,0:T(8,128)(2,1)S(1)}, u32[]{:S(2)}, u32[]{:S(2)}) collective-permute-start(bf16[1,128,256]{2,1,0:T(8,128)(2,1)S(1)} %get-tuple-element.251), channel_id=1, source_target_pairs={{0,2},{1,3},{2,0},{3,1},{4,6},{5,7},{6,4},{7,5},{8,10},{9,11},{10,... | collective-permute-start | bytes 196616 | tf_op jit(solution)/shard_map/ppermute | solution.py:21
  107.8 3.2 %collective-permute-done.44.refs_9_ = bf16[1,128,256]{2,1,0:T(8,128)(2,1)S(1)} collective-permute-done((bf16[1,128,256]{2,1,0:T(8,128)(2,1)S(1)}, bf16[1,128,256]{2,1,0:T(8,128)(2,1)S(1)}, u32[]{:S(2)}, u32[]{:S(2)}) %collective-permute-start.44) | collective-permute-done | bytes 65568 | tf_op jit(solution)/shard_map/ppermute | solution.py:21
  (138 shorter events, 47.5 us)
Async XLA Ops:
  1.0 6.5 %collective-permute-start.4 = (bf16[64,1024]{1,0:T(8,128)(2,1)S(1)}, bf16[64,1024]{1,0:T(8,128)(2,1)S(1)}, u32[]{:S(2)}, u32[]{:S(2)}) collective-permute-start(bf16[64,1024]{1,0:T(8,128)(2,1)S(1)} %get-tuple-element.259.refs_0_), channel_id=1, source_target_pairs={{0,8},{4,12},{8,0},{12,4},{1,9},{5,13},{9,1},{13,5},{2,10},{6,14},... | collective-permute-start | bytes 393224 | tf_op jit(solution)/shard_map/ppermute | solution.py:21
  11.0 8.5 %collective-permute-start.6 = (bf16[128,1024]{1,0:T(8,128)(2,1)S(1)}, bf16[128,1024]{1,0:T(8,128)(2,1)S(1)}, u32[]{:S(2)}, u32[]{:S(2)}) collective-permute-start(bf16[128,1024]{1,0:T(8,128)(2,1)S(1)} %get-tuple-element.136), channel_id=1, source_target_pairs={{0,1},{1,0},{2,3},{3,2},{4,5},{5,4},{6,7},{7,6},{8,9},{9,8},{10,11... | collective-permute-start | bytes 786440 | tf_op jit(solution)/shard_map/ppermute | solution.py:21
  12.9 9.1 %collective-permute-start.1 = (bf16[64,1024]{1,0:T(8,128)(2,1)S(1)}, bf16[64,1024]{1,0:T(8,128)(2,1)S(1)}, u32[]{:S(2)}, u32[]{:S(2)}) collective-permute-start(bf16[64,1024]{1,0:T(8,128)(2,1)S(1)} %get-tuple-element.260.refs_0_), channel_id=1, source_target_pairs={{0,8},{4,12},{8,0},{12,4},{1,9},{5,13},{9,1},{13,5},{2,10},{6,14},... | collective-permute-start | bytes 393224 | tf_op jit(solution)/shard_map/ppermute | solution.py:21
  19.6 7.7 %collective-permute-start.9 = (bf16[128,1024]{1,0:T(8,128)(2,1)S(1)}, bf16[128,1024]{1,0:T(8,128)(2,1)S(1)}, u32[]{:S(2)}, u32[]{:S(2)}) collective-permute-start(bf16[128,1024]{1,0:T(8,128)(2,1)S(1)} %get-tuple-element.145), channel_id=1, source_target_pairs={{0,1},{1,0},{2,3},{3,2},{4,5},{5,4},{6,7},{7,6},{8,9},{9,8},{10,11... | collective-permute-start | bytes 786440 | tf_op jit(solution)/shard_map/ppermute | solution.py:21
  21.4 6.0 %collective-permute-start.7 = (bf16[128,1024]{1,0:T(8,128)(2,1)S(1)}, bf16[128,1024]{1,0:T(8,128)(2,1)S(1)}, u32[]{:S(2)}, u32[]{:S(2)}) collective-permute-start(bf16[128,1024]{1,0:T(8,128)(2,1)S(1)} %get-tuple-element.142), channel_id=1, source_target_pairs={{0,4},{1,2},{2,1},{3,7},{4,0},{5,6},{6,5},{7,3},{8,12},{9,10},{10,... | collective-permute-start | bytes 786440 | tf_op jit(solution)/shard_map/ppermute | solution.py:31
  27.5 9.5 %collective-permute-start.10 = (bf16[128,1024]{1,0:T(8,128)(2,1)S(1)}, bf16[128,1024]{1,0:T(8,128)(2,1)S(1)}, u32[]{:S(2)}, u32[]{:S(2)}) collective-permute-start(bf16[128,1024]{1,0:T(8,128)(2,1)S(1)} %get-tuple-element.149), channel_id=1, source_target_pairs={{0,1},{1,0},{2,3},{3,2},{4,5},{5,4},{6,7},{7,6},{8,9},{9,8},{10,11... | collective-permute-start | bytes 786440 | tf_op jit(solution)/shard_map/ppermute | solution.py:21
  30.3 6.8 %collective-permute-start.11 = (bf16[128,1024]{1,0:T(8,128)(2,1)S(1)}, bf16[128,1024]{1,0:T(8,128)(2,1)S(1)}, u32[]{:S(2)}, u32[]{:S(2)}) collective-permute-start(bf16[128,1024]{1,0:T(8,128)(2,1)S(1)} %get-tuple-element.153), channel_id=1, source_target_pairs={{0,4},{1,2},{2,1},{3,7},{4,0},{5,6},{6,5},{7,3},{8,12},{9,10},{10,... | collective-permute-start | bytes 786440 | tf_op jit(solution)/shard_map/ppermute | solution.py:31
  38.0 7.7 %collective-permute-start.16 = (bf16[128,1024]{1,0:T(8,128)(2,1)S(1)}, bf16[128,1024]{1,0:T(8,128)(2,1)S(1)}, u32[]{:S(2)}, u32[]{:S(2)}) collective-permute-start(bf16[128,1024]{1,0:T(8,128)(2,1)S(1)} %get-tuple-element.169), channel_id=1, source_target_pairs={{0,1},{1,0},{2,3},{3,2},{4,5},{5,4},{6,7},{7,6},{8,9},{9,8},{10,11... | collective-permute-start | bytes 786440 | tf_op jit(solution)/shard_map/ppermute | solution.py:21
  39.9 6.0 %collective-permute-start.15 = (bf16[128,1024]{1,0:T(8,128)(2,1)S(1)}, bf16[128,1024]{1,0:T(8,128)(2,1)S(1)}, u32[]{:S(2)}, u32[]{:S(2)}) collective-permute-start(bf16[128,1024]{1,0:T(8,128)(2,1)S(1)} %get-tuple-element.167), channel_id=1, source_target_pairs={{0,4},{1,2},{2,1},{3,7},{4,0},{5,6},{6,5},{7,3},{8,12},{9,10},{10,... | collective-permute-start | bytes 786440 | tf_op jit(solution)/shard_map/ppermute | solution.py:31
  48.1 6.4 %collective-permute-start.17 = (bf16[128,1024]{1,0:T(8,128)(2,1)S(1)}, bf16[128,1024]{1,0:T(8,128)(2,1)S(1)}, u32[]{:S(2)}, u32[]{:S(2)}) collective-permute-start(bf16[128,1024]{1,0:T(8,128)(2,1)S(1)} %get-tuple-element.173), channel_id=1, source_target_pairs={{0,1},{1,0},{2,3},{3,2},{4,5},{5,4},{6,7},{7,6},{8,9},{9,8},{10,11... | collective-permute-start | bytes 786440 | tf_op jit(solution)/shard_map/ppermute | solution.py:21
  56.6 7.5 %collective-permute-start.26 = (bf16[128,1024]{1,0:T(8,128)(2,1)S(1)}, bf16[128,1024]{1,0:T(8,128)(2,1)S(1)}, u32[]{:S(2)}, u32[]{:S(2)}) collective-permute-start(bf16[128,1024]{1,0:T(8,128)(2,1)S(1)} %get-tuple-element.197), channel_id=1, source_target_pairs={{0,1},{1,0},{2,3},{3,2},{4,5},{5,4},{6,7},{7,6},{8,9},{9,8},{10,11... | collective-permute-start | bytes 786440 | tf_op jit(solution)/shard_map/ppermute | solution.py:21
  58.4 5.8 %collective-permute-start.25 = (bf16[128,1024]{1,0:T(8,128)(2,1)S(1)}, bf16[128,1024]{1,0:T(8,128)(2,1)S(1)}, u32[]{:S(2)}, u32[]{:S(2)}) collective-permute-start(bf16[128,1024]{1,0:T(8,128)(2,1)S(1)} %get-tuple-element.196), channel_id=1, source_target_pairs={{0,4},{1,2},{2,1},{3,7},{4,0},{5,6},{6,5},{7,3},{8,12},{9,10},{10,... | collective-permute-start | bytes 786440 | tf_op jit(solution)/shard_map/ppermute | solution.py:31
  65.4 7.5 %collective-permute-start.27 = (bf16[128,1024]{1,0:T(8,128)(2,1)S(1)}, bf16[128,1024]{1,0:T(8,128)(2,1)S(1)}, u32[]{:S(2)}, u32[]{:S(2)}) collective-permute-start(bf16[128,1024]{1,0:T(8,128)(2,1)S(1)} %get-tuple-element.201), channel_id=1, source_target_pairs={{0,1},{1,0},{2,3},{3,2},{4,5},{5,4},{6,7},{7,6},{8,9},{9,8},{10,11... | collective-permute-start | bytes 786440 | tf_op jit(solution)/shard_map/ppermute | solution.py:21
  67.2 5.7 %collective-permute-start.31 = (bf16[128,1024]{1,0:T(8,128)(2,1)S(1)}, bf16[128,1024]{1,0:T(8,128)(2,1)S(1)}, u32[]{:S(2)}, u32[]{:S(2)}) collective-permute-start(bf16[128,1024]{1,0:T(8,128)(2,1)S(1)} %get-tuple-element.211), channel_id=1, source_target_pairs={{0,4},{1,2},{2,1},{3,7},{4,0},{5,6},{6,5},{7,3},{8,12},{9,10},{10,... | collective-permute-start | bytes 786440 | tf_op jit(solution)/shard_map/ppermute | solution.py:31
  73.0 7.9 %collective-permute-start.33 = (bf16[128,1024]{1,0:T(8,128)(2,1)S(1)}, bf16[128,1024]{1,0:T(8,128)(2,1)S(1)}, u32[]{:S(2)}, u32[]{:S(2)}) collective-permute-start(bf16[128,1024]{1,0:T(8,128)(2,1)S(1)} %get-tuple-element.219), channel_id=1, source_target_pairs={{0,1},{1,0},{2,3},{3,2},{4,5},{5,4},{6,7},{7,6},{8,9},{9,8},{10,11... | collective-permute-start | bytes 786440 | tf_op jit(solution)/shard_map/ppermute | solution.py:21
  74.9 6.2 %collective-permute-start.32 = (bf16[128,1024]{1,0:T(8,128)(2,1)S(1)}, bf16[128,1024]{1,0:T(8,128)(2,1)S(1)}, u32[]{:S(2)}, u32[]{:S(2)}) collective-permute-start(bf16[128,1024]{1,0:T(8,128)(2,1)S(1)} %get-tuple-element.218), channel_id=1, source_target_pairs={{0,4},{1,2},{2,1},{3,7},{4,0},{5,6},{6,5},{7,3},{8,12},{9,10},{10,... | collective-permute-start | bytes 786440 | tf_op jit(solution)/shard_map/ppermute | solution.py:31
  81.1 9.2 %collective-permute-start.34 = (bf16[128,1024]{1,0:T(8,128)(2,1)S(1)}, bf16[128,1024]{1,0:T(8,128)(2,1)S(1)}, u32[]{:S(2)}, u32[]{:S(2)}) collective-permute-start(bf16[128,1024]{1,0:T(8,128)(2,1)S(1)} %get-tuple-element.222), channel_id=1, source_target_pairs={{0,1},{1,0},{2,3},{3,2},{4,5},{5,4},{6,7},{7,6},{8,9},{9,8},{10,11... | collective-permute-start | bytes 786440 | tf_op jit(solution)/shard_map/ppermute | solution.py:21
  84.5 11.7 %collective-permute-start.37 = (bf16[128,1024]{1,0:T(8,128)(2,1)S(1)}, bf16[128,1024]{1,0:T(8,128)(2,1)S(1)}, u32[]{:S(2)}, u32[]{:S(2)}) collective-permute-start(bf16[128,1024]{1,0:T(8,128)(2,1)S(1)} %get-tuple-element.235), channel_id=1, source_target_pairs={{0,1},{1,0},{2,3},{3,2},{4,5},{5,4},{6,7},{7,6},{8,9},{9,8},{10,11... | collective-permute-start | bytes 786440 | tf_op jit(solution)/shard_map/ppermute | solution.py:21
  91.6 7.8 %collective-permute-start.36 = (bf16[2,128,256]{2,1,0:T(8,128)(2,1)S(1)}, bf16[2,128,256]{2,1,0:T(8,128)(2,1)S(1)}, u32[]{:S(2)}, u32[]{:S(2)}) collective-permute-start(bf16[2,128,256]{2,1,0:T(8,128)(2,1)S(1)} %get-tuple-element.233), channel_id=1, source_target_pairs={{0,4},{1,2},{2,1},{3,7},{4,0},{5,6},{6,5},{7,3},{8,12},{9,10},{10,... | collective-permute-start | bytes 393224 | tf_op jit(solution)/shard_map/ppermute | solution.py:31
  91.6 8.0 %collective-permute-start.40 = (bf16[2,128,256]{2,1,0:T(8,128)(2,1)S(1)}, bf16[2,128,256]{2,1,0:T(8,128)(2,1)S(1)}, u32[]{:S(2)}, u32[]{:S(2)}) collective-permute-start(bf16[2,128,256]{2,1,0:T(8,128)(2,1)S(1)} %get-tuple-element.245), channel_id=1, source_target_pairs={{0,1},{1,0},{2,3},{3,2},{4,5},{5,4},{6,7},{7,6},{8,9},{9,8},{10,11... | collective-permute-start | bytes 393224 | tf_op jit(solution)/shard_map/ppermute | solution.py:21
  97.5 7.8 %collective-permute-start.43 = (bf16[2,128,256]{2,1,0:T(8,128)(2,1)S(1)}, bf16[2,128,256]{2,1,0:T(8,128)(2,1)S(1)}, u32[]{:S(2)}, u32[]{:S(2)}) collective-permute-start(bf16[2,128,256]{2,1,0:T(8,128)(2,1)S(1)} %get-tuple-element.253), channel_id=1, source_target_pairs={{0,1},{1,0},{2,3},{3,2},{4,5},{5,4},{6,7},{7,6},{8,9},{9,8},{10,11... | collective-permute-start | bytes 393224 | tf_op jit(solution)/shard_map/ppermute | solution.py:21
  99.4 7.3 %collective-permute-start.38 = (bf16[128,256]{1,0:T(8,128)(2,1)S(1)}, bf16[128,256]{1,0:T(8,128)(2,1)S(1)}, u32[]{:S(2)}, u32[]{:S(2)}) collective-permute-start(bf16[128,256]{1,0:T(8,128)(2,1)S(1)} %get-tuple-element.241), channel_id=1, source_target_pairs={{0,1},{1,0},{2,3},{3,2},{4,5},{5,4},{6,7},{7,6},{8,9},{9,8},{10,11... | collective-permute-start | bytes 196616 | tf_op jit(solution)/shard_map/ppermute | solution.py:21
  99.7 6.9 %collective-permute-start.42 = (bf16[1,128,256]{2,1,0:T(8,128)(2,1)S(1)}, bf16[1,128,256]{2,1,0:T(8,128)(2,1)S(1)}, u32[]{:S(2)}, u32[]{:S(2)}) collective-permute-start(bf16[1,128,256]{2,1,0:T(8,128)(2,1)S(1)} %get-tuple-element.251), channel_id=1, source_target_pairs={{0,2},{1,3},{2,0},{3,1},{4,6},{5,7},{6,4},{7,5},{8,10},{9,11},{10,... | collective-permute-start | bytes 196616 | tf_op jit(solution)/shard_map/ppermute | solution.py:21
  105.3 5.7 %collective-permute-start.44 = (bf16[1,128,256]{2,1,0:T(8,128)(2,1)S(1)}, bf16[1,128,256]{2,1,0:T(8,128)(2,1)S(1)}, u32[]{:S(2)}, u32[]{:S(2)}) collective-permute-start(bf16[1,128,256]{2,1,0:T(8,128)(2,1)S(1)} %get-tuple-element.256), channel_id=1, source_target_pairs={{0,2},{1,3},{2,0},{3,1},{4,6},{5,7},{6,4},{7,5},{8,10},{9,11},{10,... | collective-permute-start | bytes 196616 | tf_op jit(solution)/shard_map/ppermute | solution.py:21
  (30 other events, 139.8 us)

commit v5 on v4

--- a/solution.py
+++ b/solution.py
@@ -10,7 +10,6 @@
 
 HEADS = 16
 CHUNKS = 4
-SPLITS = 2
 F32 = jnp.float32
 BF16 = jnp.bfloat16
 VMEM = pl.BlockSpec(memory_space=pltpu.VMEM)
@@ -91,6 +90,24 @@
             compiler_params=pltpu.CompilerParams(vmem_limit_bytes=size + (6 << 20)),
         )(*args, *tokens)
         return results
+
+
+def load(array):
+    def kernel(array_ref, out_ref, sem):
+        copy = pltpu.make_async_copy(array_ref, out_ref, sem)
+        copy.start()
+        copy.wait()
+
+    return pl.pallas_call(
+        kernel,
+        name="load",
+        out_shape=pltpu.VMEM(array.shape, array.dtype),
+        in_specs=[pl.BlockSpec(memory_space=pltpu.HBM)],
+        out_specs=VMEM,
+        scratch_shapes=[pltpu.SemaphoreType.DMA],
+        cost_estimate=pl.CostEstimate(flops=1000, bytes_accessed=1 << 24, transcendentals=0),
+        compiler_params=pltpu.CompilerParams(vmem_limit_bytes=math.prod(array.shape) * 2 + (6 << 20)),
+    )(array)
 
 
 def row_blocks(rows):
@@ -227,8 +244,9 @@
         part_ref[block, :] = dot(attended, weight_ref[0]).astype(part_ref.dtype)
 
 
-def mlp_kernel(count, whole, wide_ref, arrived_ref, gain_ref, gate_up_ref, down_ref, *refs):
-    kept_ref, sent_ref, rows_ref, act_ref = refs
+def mlp_kernel(count, form, wide_ref, arrived_ref, gain_ref, gate_up_ref, down_ref, *refs):
+    kept_ref, *sent_refs, rows_ref, act_ref = refs
+    sent_ref = sent_refs[0]
     choose(wide_ref, arrived_ref, rows_ref)
     index = lax.axis_index("hidden")
     hidden = act_ref.shape[1]
@@ -242,7 +260,17 @@
             gate_sum = dot(normed, gate_up_ref[0, 0, :, columns])
             upper_sum = dot(normed, gate_up_ref[0, 1, :, columns])
             act_ref[:, columns] = (jax.nn.silu(gate_sum) * upper_sum).astype(BF16)
-        if whole:
+        if form == "direct":
+            for i in reversed(range(count)):
+                owner = index ^ i
+                columns = pl.ds(pl.multiple_of(owner * width, width), width)
+                total = dot(act_ref[...], down_ref[0, :, columns])
+                if i:
+                    sent_refs[i - 1][block, :] = total.astype(BF16)
+                else:
+                    kept_ref[block, :] = total + rows_ref[block, columns]
+            continue
+        if form == "whole":
             total = dot(act_ref[...], down_ref[0])
             sent_ref[block, :] = total.astype(BF16)
             kept_ref[block, :] = total
@@ -289,7 +317,7 @@
     sent_ref[...] = (mine_ref[kept:] + arrived_ref[kept:].astype(F32)).astype(BF16)
 
 
-def final_kernel(count, routes, *refs):
+def final_kernel(count, forms, *refs):
     *in_refs, out_ref, rows_ref, sems = refs
     chunks = rows_ref.shape[0]
     stride = out_ref.shape[1] // count
@@ -298,7 +326,13 @@
     index = lax.axis_index("hidden")
     copies = []
     for chunk in range(chunks):
-        if routes[chunk]:
+        if forms[chunk] == "direct":
+            total_ref, *in_refs = in_refs
+            total = total_ref[...]
+            for arrived_ref in in_refs:
+                total = total + arrived_ref[...].astype(F32)
+            rows_ref[chunk] = total
+        elif forms[chunk] == "whole":
             own_ref, mine_ref, arrived_ref, *in_refs = in_refs
 
             @pl.when(is_middle())
@@ -345,8 +379,7 @@
     size = block_rows // CHUNKS
     rows = code_count * size
     row_count = code_count * block_rows
-    split = block_rows // SPLITS
-    pieces = [slots_of(temporal[i * split : (i + 1) * split], "codebook") for i in range(SPLITS)]
+    pieces = [slots_of(part, "codebook") for part in (temporal[:size], temporal[size:])]
     earlier = shifted(frame_ids.reshape(code_count, -1), "codebook", 1)
     step = Steps()
     wide, sent = ((rows, width), F32), ((rows, width), BF16)
@@ -358,10 +391,10 @@
     def project(c):
         if (s := get(c)) is not None:
             s["part"] = step(
-                functools.partial(proj_kernel, c * size % split),
+                functools.partial(proj_kernel, max(c - 1, 0) * size),
                 "project",
                 [wide],
-                [*pieces[c * size // split], proj_weight],
+                [*pieces[min(c, 1)], proj_weight],
                 [pltpu.VMEM((rows, temporal.shape[1]), BF16)],
             )[0]
 
@@ -428,24 +461,34 @@
                 [s["query"], *[s["kvs"][slot] for slot in range(code_count)], out_weight],
             )[0]
 
-    def rides(c):
-        return c + 8 < CHUNKS + 6
+    def form(c):
+        if c + 8 < CHUNKS + 6:
+            return "whole"
+        return "direct" if c == CHUNKS - 1 else "halves"
 
     def mlp(c):
         if (s := get(c)) is not None:
-            shape = (rows, width) if rides(c) else (hidden_count // 2, rows, local_width)
-            s["sums"], s["sums_sent"] = step(
-                functools.partial(mlp_kernel, hidden_count, rides(c)),
+            shape = {
+                "whole": (rows, width),
+                "halves": (hidden_count // 2, rows, local_width),
+                "direct": (rows, local_width),
+            }[form(c)]
+            messages = hidden_count - 1 if form(c) == "direct" else 1
+            s["sums"], s["sums_sent"], *others = step(
+                functools.partial(mlp_kernel, hidden_count, form(c)),
                 "mlp",
-                [(shape, F32), (shape, BF16)],
+                [(shape, F32)] + [(shape, BF16)] * messages,
                 [s["residual"], s["residual_arrived"], norm_gains, gate_up, down_weight],
                 [pltpu.VMEM((rows, width), F32), pltpu.VMEM((min(rows, 128), gate_up.shape[3]), BF16)],
             )
-            if not rides(c):
+            if form(c) == "halves":
                 s["arrived"] = swap(s["sums_sent"], "hidden", pair_bit)
+            if form(c) == "direct":
+                others = [s["sums_sent"], *others]
+                s["direct"] = [swap(out, "hidden", i + 1) for i, out in reversed(list(enumerate(others)))]
 
     def halve(c):
-        if (s := get(c)) is not None and not rides(c):
+        if (s := get(c)) is not None and form(c) == "halves":
             shape = (hidden_count // 4, rows, local_width)
             s["wide"], out = step(
                 halve_kernel, "halve", [(shape, F32), (shape, BF16)], [s["sums"], s["arrived"]]
@@ -453,7 +496,7 @@
             s["last"] = swap(out, "hidden", far_bit)
 
     def collect(c):
-        if (s := get(c)) is not None and rides(c):
+        if (s := get(c)) is not None and form(c) == "whole":
             shape = (2, rows, local_width)
             s["wide"], out = step(
                 gather_kernel, "gather", [(shape, F32), (shape, BF16)], [s["sums"], s["arrived"]]
@@ -461,7 +504,7 @@
             s["far"] = middle_swap(out)
 
     def give_back(c):
-        if (s := get(c)) is not None and rides(c):
+        if (s := get(c)) is not None and form(c) == "whole":
             shape = (rows, local_width)
             s["own"], out = step(
                 return_kernel, "return", [(shape, F32), (shape, BF16)], [s["wide"], s["far"]]
@@ -469,12 +512,13 @@
             s["last"] = swap(out, "hidden", pair_bit)
 
     def final():
-        routes = [rides(c) for c in range(CHUNKS)]
+        forms = [form(c) for c in range(CHUNKS)]
         args = []
-        for s, ridden in zip(states, routes):
-            args += [s[name] for name in (("own", "sums", "last") if ridden else ("wide", "last"))]
+        for s, kind in zip(states, forms):
+            names = {"whole": ("own", "sums", "last"), "halves": ("wide", "last"), "direct": ("sums",)}[kind]
+            args += [s[name] for name in names] + s.get("direct", [])
         return step(
-            functools.partial(final_kernel, code_count, routes),
+            functools.partial(final_kernel, code_count, forms),
             "final",
             [((1, row_count, local_width), F32)],
             args,
@@ -489,9 +533,9 @@
         pair_sum(t - 5)
         exchange(t)
         qkv(t - 3)
-        mlp(t - 7)
         collect(t - 9)
         give_back(t - 10)
+        mlp(t - 7)
         halve(t - 8)
         project(t + 1)
         embed(t - 1)

time: 113 us -> 111 us (0.982)
  waiting for transfers between devices: 45.1 us -> 42.6 us
    ppermute x34 -> x35, waiting for transfers between devices: 44.8 us -> 42.3 us  [swap(): return lax.ppermute(block, axis, [(i, i ^ distance) for i in range(count)])]
    ppermute x34 -> x35, starting transfers between devices: 43.5 us -> 43.3 us  [swap(): return lax.ppermute(block, axis, [(i, i ^ distance) for i in range(count)])]
    pallas_call x49 -> x48, Pallas kernels: 18.1 us -> 18.1 us  [__call__(): pl.pallas_call(with_token, name=name, out_shape=[jax.ShapeDtypeStruct(sha...]
  transfers between devices with their start and end apart: 45 -> 46, of which waited for: 25 -> 26; matrix products, arithmetic and copies ran while one was open for 0% -> 1% of each run, Pallas kernels for 12% -> 13%
where the time goes in v5:
time: 111 us
  starting transfers between devices  46 us (41%)
  waiting for transfers between devices  42.6 us (38%)
  Pallas kernels  18.1 us (16%)
  local copies, waits for them, and re-layouts  3.45 us (3%)
    ppermute x35, starting transfers between devices, swap(): return lax.ppermute(block, axis, [(i, i ^ distance) for i in range(count)])  43.3 us
    ppermute x35, waiting for transfers between devices, swap(): return lax.ppermute(block, axis, [(i, i ^ distance) for i in range(count)])  42.3 us
    pallas_call x48, Pallas kernels, __call__(): pl.pallas_call(with_token, name=name, out_shape=[jax.ShapeDtypeStruct(sha...  18.1 us
    ppermute x1, starting transfers between devices, shifted(): return lax.ppermute(block, axis, route)  2.4 us
  transfers between devices with their start and end apart: 46, of which 26 were waited for; matrix products, arithmetic and copies ran while one was open for 1% of the time, Pallas kernels for 13%

profile of v5, /device:TPU:0, one launch (start us, length us, event | category | flops | bytes accessed | tf_op | source)
XLA Modules:
  0.0 110.9 jit_solution(1964377212780900997)
XLA Ops:
  0.8 2.9 %collective-permute-start.4 = (bf16[32,1024]{1,0:T(8,128)(2,1)S(1)}, bf16[32,1024]{1,0:T(8,128)(2,1)S(1)}, u32[]{:S(2)}, u32[]{:S(2)}) collective-permute-start(bf16[32,1024]{1,0:T(8,128)(2,1)S(1)} %slice.7.refs_0_), channel_id=1, source_target_pairs={{0,8},{4,12},{8,0},{12,4},{1,9},{5,13},{9,1},{13,5},{2,10},{6,14},... | collective-permute-start | bytes 196616 | tf_op jit(solution)/shard_map/ppermute | solution.py:20
  9.7 1.9 %collective-permute-start.6 = (bf16[128,1024]{1,0:T(8,128)(2,1)S(1)}, bf16[128,1024]{1,0:T(8,128)(2,1)S(1)}, u32[]{:S(2)}, u32[]{:S(2)}) collective-permute-start(bf16[128,1024]{1,0:T(8,128)(2,1)S(1)} %get-tuple-element.135), channel_id=1, source_target_pairs={{0,1},{1,0},{2,3},{3,2},{4,5},{5,4},{6,7},{7,6},{8,9},{9,8},{10,11... | collective-permute-start | bytes 786440 | tf_op jit(solution)/shard_map/ppermute | solution.py:20
  13.8 4.4 %collective-permute-done.6.refs_1_ = bf16[128,1024]{1,0:T(8,128)(2,1)S(1)} collective-permute-done((bf16[128,1024]{1,0:T(8,128)(2,1)S(1)}, bf16[128,1024]{1,0:T(8,128)(2,1)S(1)}, u32[]{:S(2)}, u32[]{:S(2)}) %collective-permute-start.6) | collective-permute-done | bytes 262176 | tf_op jit(solution)/shard_map/ppermute | solution.py:20
  18.3 1.8 %collective-permute-start.9 = (bf16[128,1024]{1,0:T(8,128)(2,1)S(1)}, bf16[128,1024]{1,0:T(8,128)(2,1)S(1)}, u32[]{:S(2)}, u32[]{:S(2)}) collective-permute-start(bf16[128,1024]{1,0:T(8,128)(2,1)S(1)} %get-tuple-element.144), channel_id=1, source_target_pairs={{0,1},{1,0},{2,3},{3,2},{4,5},{5,4},{6,7},{7,6},{8,9},{9,8},{10,11... | collective-permute-start | bytes 786440 | tf_op jit(solution)/shard_map/ppermute | solution.py:20
  20.2 2.4 %collective-permute-start.8 = (s32[4,128]{1,0:T(4,128)S(1)}, s32[4,128]{1,0:T(4,128)S(1)}, u32[]{:S(2)}, u32[]{:S(2)}) collective-permute-start(s32[4,128]{1,0:T(4,128)S(1)} %bitcast.1), channel_id=1, source_target_pairs={{0,4},{4,8},{8,12},{1,5},{5,9},{9,13},{2,6},{6,10},{10,14},{3,7},{... | collective-permute-start | bytes 6152 | tf_op jit(solution)/shard_map/ppermute | solution.py:46
  24.2 1.9 %collective-permute-done.9.refs_1_ = bf16[128,1024]{1,0:T(8,128)(2,1)S(1)} collective-permute-done((bf16[128,1024]{1,0:T(8,128)(2,1)S(1)}, bf16[128,1024]{1,0:T(8,128)(2,1)S(1)}, u32[]{:S(2)}, u32[]{:S(2)}) %collective-permute-start.9) | collective-permute-done | bytes 262176 | tf_op jit(solution)/shard_map/ppermute | solution.py:20
  26.2 2.8 %collective-permute-start.10 = (bf16[128,1024]{1,0:T(8,128)(2,1)S(1)}, bf16[128,1024]{1,0:T(8,128)(2,1)S(1)}, u32[]{:S(2)}, u32[]{:S(2)}) collective-permute-start(bf16[128,1024]{1,0:T(8,128)(2,1)S(1)} %get-tuple-element.148), channel_id=1, source_target_pairs={{0,1},{1,0},{2,3},{3,2},{4,5},{5,4},{6,7},{7,6},{8,9},{9,8},{10,11... | collective-permute-start | bytes 786440 | tf_op jit(solution)/shard_map/ppermute | solution.py:20
  30.4 5.3 %collective-permute-done.10.refs_1_ = bf16[128,1024]{1,0:T(8,128)(2,1)S(1)} collective-permute-done((bf16[128,1024]{1,0:T(8,128)(2,1)S(1)}, bf16[128,1024]{1,0:T(8,128)(2,1)S(1)}, u32[]{:S(2)}, u32[]{:S(2)}) %collective-permute-start.10) | collective-permute-done | bytes 262176 | tf_op jit(solution)/shard_map/ppermute | solution.py:20
  36.8 1.8 %collective-permute-start.16 = (bf16[128,1024]{1,0:T(8,128)(2,1)S(1)}, bf16[128,1024]{1,0:T(8,128)(2,1)S(1)}, u32[]{:S(2)}, u32[]{:S(2)}) collective-permute-start(bf16[128,1024]{1,0:T(8,128)(2,1)S(1)} %get-tuple-element.168), channel_id=1, source_target_pairs={{0,1},{1,0},{2,3},{3,2},{4,5},{5,4},{6,7},{7,6},{8,9},{9,8},{10,11... | collective-permute-start | bytes 786440 | tf_op jit(solution)/shard_map/ppermute | solution.py:20
  45.2 1.7 %collective-permute-start.19 = (bf16[2,128,256]{2,1,0:T(8,128)(2,1)S(1)}, bf16[2,128,256]{2,1,0:T(8,128)(2,1)S(1)}, u32[]{:S(2)}, u32[]{:S(2)}) collective-permute-start(bf16[2,128,256]{2,1,0:T(8,128)(2,1)S(1)} %get-tuple-element.176.refs_1_), channel_id=1, source_target_pairs={{0,8},{4,12},{8,0},{12,4},{1,9},{5,13},{9,1},{13,5},{2,10},{6,14},... | collective-permute-start | bytes 393224 | tf_op jit(solution)/shard_map/ppermute | solution.py:20
  46.9 1.7 %collective-permute-start.17 = (bf16[128,1024]{1,0:T(8,128)(2,1)S(1)}, bf16[128,1024]{1,0:T(8,128)(2,1)S(1)}, u32[]{:S(2)}, u32[]{:S(2)}) collective-permute-start(bf16[128,1024]{1,0:T(8,128)(2,1)S(1)} %get-tuple-element.172), channel_id=1, source_target_pairs={{0,1},{1,0},{2,3},{3,2},{4,5},{5,4},{6,7},{7,6},{8,9},{9,8},{10,11... | collective-permute-start | bytes 786440 | tf_op jit(solution)/shard_map/ppermute | solution.py:20
  55.4 1.8 %collective-permute-start.26 = (bf16[128,1024]{1,0:T(8,128)(2,1)S(1)}, bf16[128,1024]{1,0:T(8,128)(2,1)S(1)}, u32[]{:S(2)}, u32[]{:S(2)}) collective-permute-start(bf16[128,1024]{1,0:T(8,128)(2,1)S(1)} %get-tuple-element.196), channel_id=1, source_target_pairs={{0,1},{1,0},{2,3},{3,2},{4,5},{5,4},{6,7},{7,6},{8,9},{9,8},{10,11... | collective-permute-start | bytes 786440 | tf_op jit(solution)/shard_map/ppermute | solution.py:20
  64.2 1.8 %collective-permute-start.27 = (bf16[128,1024]{1,0:T(8,128)(2,1)S(1)}, bf16[128,1024]{1,0:T(8,128)(2,1)S(1)}, u32[]{:S(2)}, u32[]{:S(2)}) collective-permute-start(bf16[128,1024]{1,0:T(8,128)(2,1)S(1)} %get-tuple-element.200), channel_id=1, source_target_pairs={{0,1},{1,0},{2,3},{3,2},{4,5},{5,4},{6,7},{7,6},{8,9},{9,8},{10,11... | collective-permute-start | bytes 786440 | tf_op jit(solution)/shard_map/ppermute | solution.py:20
  66.5 2.3 %collective-permute-done.29.refs_3_ = bf16[2,128,256]{2,1,0:T(8,128)(2,1)S(1)} collective-permute-done((bf16[2,128,256]{2,1,0:T(8,128)(2,1)S(1)}, bf16[2,128,256]{2,1,0:T(8,128)(2,1)S(1)}, u32[]{:S(2)}, u32[]{:S(2)}) %collective-permute-start.29) | collective-permute-done | bytes 131104 | tf_op jit(solution)/shard_map/ppermute | solution.py:20
  71.8 1.9 %collective-permute-start.33 = (bf16[128,1024]{1,0:T(8,128)(2,1)S(1)}, bf16[128,1024]{1,0:T(8,128)(2,1)S(1)}, u32[]{:S(2)}, u32[]{:S(2)}) collective-permute-start(bf16[128,1024]{1,0:T(8,128)(2,1)S(1)} %get-tuple-element.218), channel_id=1, source_target_pairs={{0,1},{1,0},{2,3},{3,2},{4,5},{5,4},{6,7},{7,6},{8,9},{9,8},{10,11... | collective-permute-start | bytes 786440 | tf_op jit(solution)/shard_map/ppermute | solution.py:20
  74.8 4.8 %collective-permute-done.33.refs_1_ = bf16[128,1024]{1,0:T(8,128)(2,1)S(1)} collective-permute-done((bf16[128,1024]{1,0:T(8,128)(2,1)S(1)}, bf16[128,1024]{1,0:T(8,128)(2,1)S(1)}, u32[]{:S(2)}, u32[]{:S(2)}) %collective-permute-start.33) | collective-permute-done | bytes 262176 | tf_op jit(solution)/shard_map/ppermute | solution.py:20
  79.9 2.1 %collective-permute-start.34 = (bf16[128,1024]{1,0:T(8,128)(2,1)S(1)}, bf16[128,1024]{1,0:T(8,128)(2,1)S(1)}, u32[]{:S(2)}, u32[]{:S(2)}) collective-permute-start(bf16[128,1024]{1,0:T(8,128)(2,1)S(1)} %get-tuple-element.221), channel_id=1, source_target_pairs={{0,1},{1,0},{2,3},{3,2},{4,5},{5,4},{6,7},{7,6},{8,9},{9,8},{10,11... | collective-permute-start | bytes 786440 | tf_op jit(solution)/shard_map/ppermute | solution.py:20
  83.2 5.4 %collective-permute-start.37 = (bf16[128,1024]{1,0:T(8,128)(2,1)S(1)}, bf16[128,1024]{1,0:T(8,128)(2,1)S(1)}, u32[]{:S(2)}, u32[]{:S(2)}) collective-permute-start(bf16[128,1024]{1,0:T(8,128)(2,1)S(1)} %get-tuple-element.232), channel_id=1, source_target_pairs={{0,1},{1,0},{2,3},{3,2},{4,5},{5,4},{6,7},{7,6},{8,9},{9,8},{10,11... | collective-permute-start | bytes 786440 | tf_op jit(solution)/shard_map/ppermute | solution.py:20
  90.4 2.4 %collective-permute-start.40 = (bf16[2,128,256]{2,1,0:T(8,128)(2,1)S(1)}, bf16[2,128,256]{2,1,0:T(8,128)(2,1)S(1)}, u32[]{:S(2)}, u32[]{:S(2)}) collective-permute-start(bf16[2,128,256]{2,1,0:T(8,128)(2,1)S(1)} %get-tuple-element.242), channel_id=1, source_target_pairs={{0,1},{1,0},{2,3},{3,2},{4,5},{5,4},{6,7},{7,6},{8,9},{9,8},{10,11... | collective-permute-start | bytes 393224 | tf_op jit(solution)/shard_map/ppermute | solution.py:20
  92.8 2.2 %collective-permute-done.37.refs_1_ = bf16[128,1024]{1,0:T(8,128)(2,1)S(1)} collective-permute-done((bf16[128,1024]{1,0:T(8,128)(2,1)S(1)}, bf16[128,1024]{1,0:T(8,128)(2,1)S(1)}, u32[]{:S(2)}, u32[]{:S(2)}) %collective-permute-start.37) | collective-permute-done | bytes 262176 | tf_op jit(solution)/shard_map/ppermute | solution.py:20
  95.1 2.0 %collective-permute-start.38 = (bf16[128,256]{1,0:T(8,128)(2,1)S(1)}, bf16[128,256]{1,0:T(8,128)(2,1)S(1)}, u32[]{:S(2)}, u32[]{:S(2)}) collective-permute-start(bf16[128,256]{1,0:T(8,128)(2,1)S(1)} %get-tuple-element.238), channel_id=1, source_target_pairs={{0,1},{1,0},{2,3},{3,2},{4,5},{5,4},{6,7},{7,6},{8,9},{9,8},{10,11... | collective-permute-start | bytes 196616 | tf_op jit(solution)/shard_map/ppermute | solution.py:20
  99.0 1.8 %collective-permute-start.43 = (bf16[128,256]{1,0:T(8,128)(2,1)S(1)}, bf16[128,256]{1,0:T(8,128)(2,1)S(1)}, u32[]{:S(2)}, u32[]{:S(2)}) collective-permute-start(bf16[128,256]{1,0:T(8,128)(2,1)S(1)} %get-tuple-element.252), channel_id=1, source_target_pairs={{0,3},{1,2},{2,1},{3,0},{4,7},{5,6},{6,5},{7,4},{8,11},{9,10},{10,... | collective-permute-start | bytes 196616 | tf_op jit(solution)/shard_map/ppermute | solution.py:20
  104.6 2.8 %collective-permute-done.42.refs_7_ = bf16[1,128,256]{2,1,0:T(8,128)(2,1)S(1)} collective-permute-done((bf16[1,128,256]{2,1,0:T(8,128)(2,1)S(1)}, bf16[1,128,256]{2,1,0:T(8,128)(2,1)S(1)}, u32[]{:S(2)}, u32[]{:S(2)}) %collective-permute-start.42) | collective-permute-done | bytes 65568 | tf_op jit(solution)/shard_map/ppermute | solution.py:20
  107.4 1.7 %collective-permute-done.44.refs_10_ = bf16[128,256]{1,0:T(8,128)(2,1)S(1)} collective-permute-done((bf16[128,256]{1,0:T(8,128)(2,1)S(1)}, bf16[128,256]{1,0:T(8,128)(2,1)S(1)}, u32[]{:S(2)}, u32[]{:S(2)}) %collective-permute-start.44) | collective-permute-done | bytes 65568 | tf_op jit(solution)/shard_map/ppermute | solution.py:20
  (140 shorter events, 48.6 us)
Async XLA Ops:
  4.7 6.9 %collective-permute-start.1 = (bf16[96,1024]{1,0:T(8,128)(2,1)S(1)}, bf16[96,1024]{1,0:T(8,128)(2,1)S(1)}, u32[]{:S(2)}, u32[]{:S(2)}) collective-permute-start(bf16[96,1024]{1,0:T(8,128)(2,1)S(1)} %slice.6.refs_0_), channel_id=1, source_target_pairs={{0,8},{4,12},{8,0},{12,4},{1,9},{5,13},{9,1},{13,5},{2,10},{6,14},... | collective-permute-start | bytes 589832 | tf_op jit(solution)/shard_map/ppermute | solution.py:20
  9.7 8.6 %collective-permute-start.6 = (bf16[128,1024]{1,0:T(8,128)(2,1)S(1)}, bf16[128,1024]{1,0:T(8,128)(2,1)S(1)}, u32[]{:S(2)}, u32[]{:S(2)}) collective-permute-start(bf16[128,1024]{1,0:T(8,128)(2,1)S(1)} %get-tuple-element.135), channel_id=1, source_target_pairs={{0,1},{1,0},{2,3},{3,2},{4,5},{5,4},{6,7},{7,6},{8,9},{9,8},{10,11... | collective-permute-start | bytes 786440 | tf_op jit(solution)/shard_map/ppermute | solution.py:20
  18.3 7.7 %collective-permute-start.9 = (bf16[128,1024]{1,0:T(8,128)(2,1)S(1)}, bf16[128,1024]{1,0:T(8,128)(2,1)S(1)}, u32[]{:S(2)}, u32[]{:S(2)}) collective-permute-start(bf16[128,1024]{1,0:T(8,128)(2,1)S(1)} %get-tuple-element.144), channel_id=1, source_target_pairs={{0,1},{1,0},{2,3},{3,2},{4,5},{5,4},{6,7},{7,6},{8,9},{9,8},{10,11... | collective-permute-start | bytes 786440 | tf_op jit(solution)/shard_map/ppermute | solution.py:20
  20.1 6.0 %collective-permute-start.7 = (bf16[128,1024]{1,0:T(8,128)(2,1)S(1)}, bf16[128,1024]{1,0:T(8,128)(2,1)S(1)}, u32[]{:S(2)}, u32[]{:S(2)}) collective-permute-start(bf16[128,1024]{1,0:T(8,128)(2,1)S(1)} %get-tuple-element.141), channel_id=1, source_target_pairs={{0,4},{1,2},{2,1},{3,7},{4,0},{5,6},{6,5},{7,3},{8,12},{9,10},{10,... | collective-permute-start | bytes 786440 | tf_op jit(solution)/shard_map/ppermute | solution.py:30
  26.2 9.5 %collective-permute-start.10 = (bf16[128,1024]{1,0:T(8,128)(2,1)S(1)}, bf16[128,1024]{1,0:T(8,128)(2,1)S(1)}, u32[]{:S(2)}, u32[]{:S(2)}) collective-permute-start(bf16[128,1024]{1,0:T(8,128)(2,1)S(1)} %get-tuple-element.148), channel_id=1, source_target_pairs={{0,1},{1,0},{2,3},{3,2},{4,5},{5,4},{6,7},{7,6},{8,9},{9,8},{10,11... | collective-permute-start | bytes 786440 | tf_op jit(solution)/shard_map/ppermute | solution.py:20
  29.0 6.8 %collective-permute-start.11 = (bf16[128,1024]{1,0:T(8,128)(2,1)S(1)}, bf16[128,1024]{1,0:T(8,128)(2,1)S(1)}, u32[]{:S(2)}, u32[]{:S(2)}) collective-permute-start(bf16[128,1024]{1,0:T(8,128)(2,1)S(1)} %get-tuple-element.152), channel_id=1, source_target_pairs={{0,4},{1,2},{2,1},{3,7},{4,0},{5,6},{6,5},{7,3},{8,12},{9,10},{10,... | collective-permute-start | bytes 786440 | tf_op jit(solution)/shard_map/ppermute | solution.py:30
  36.8 7.7 %collective-permute-start.16 = (bf16[128,1024]{1,0:T(8,128)(2,1)S(1)}, bf16[128,1024]{1,0:T(8,128)(2,1)S(1)}, u32[]{:S(2)}, u32[]{:S(2)}) collective-permute-start(bf16[128,1024]{1,0:T(8,128)(2,1)S(1)} %get-tuple-element.168), channel_id=1, source_target_pairs={{0,1},{1,0},{2,3},{3,2},{4,5},{5,4},{6,7},{7,6},{8,9},{9,8},{10,11... | collective-permute-start | bytes 786440 | tf_op jit(solution)/shard_map/ppermute | solution.py:20
  38.6 6.0 %collective-permute-start.15 = (bf16[128,1024]{1,0:T(8,128)(2,1)S(1)}, bf16[128,1024]{1,0:T(8,128)(2,1)S(1)}, u32[]{:S(2)}, u32[]{:S(2)}) collective-permute-start(bf16[128,1024]{1,0:T(8,128)(2,1)S(1)} %get-tuple-element.166), channel_id=1, source_target_pairs={{0,4},{1,2},{2,1},{3,7},{4,0},{5,6},{6,5},{7,3},{8,12},{9,10},{10,... | collective-permute-start | bytes 786440 | tf_op jit(solution)/shard_map/ppermute | solution.py:30
  46.9 6.5 %collective-permute-start.17 = (bf16[128,1024]{1,0:T(8,128)(2,1)S(1)}, bf16[128,1024]{1,0:T(8,128)(2,1)S(1)}, u32[]{:S(2)}, u32[]{:S(2)}) collective-permute-start(bf16[128,1024]{1,0:T(8,128)(2,1)S(1)} %get-tuple-element.172), channel_id=1, source_target_pairs={{0,1},{1,0},{2,3},{3,2},{4,5},{5,4},{6,7},{7,6},{8,9},{9,8},{10,11... | collective-permute-start | bytes 786440 | tf_op jit(solution)/shard_map/ppermute | solution.py:20
  55.4 7.5 %collective-permute-start.26 = (bf16[128,1024]{1,0:T(8,128)(2,1)S(1)}, bf16[128,1024]{1,0:T(8,128)(2,1)S(1)}, u32[]{:S(2)}, u32[]{:S(2)}) collective-permute-start(bf16[128,1024]{1,0:T(8,128)(2,1)S(1)} %get-tuple-element.196), channel_id=1, source_target_pairs={{0,1},{1,0},{2,3},{3,2},{4,5},{5,4},{6,7},{7,6},{8,9},{9,8},{10,11... | collective-permute-start | bytes 786440 | tf_op jit(solution)/shard_map/ppermute | solution.py:20
  57.1 5.9 %collective-permute-start.25 = (bf16[128,1024]{1,0:T(8,128)(2,1)S(1)}, bf16[128,1024]{1,0:T(8,128)(2,1)S(1)}, u32[]{:S(2)}, u32[]{:S(2)}) collective-permute-start(bf16[128,1024]{1,0:T(8,128)(2,1)S(1)} %get-tuple-element.195), channel_id=1, source_target_pairs={{0,4},{1,2},{2,1},{3,7},{4,0},{5,6},{6,5},{7,3},{8,12},{9,10},{10,... | collective-permute-start | bytes 786440 | tf_op jit(solution)/shard_map/ppermute | solution.py:30
  64.2 7.4 %collective-permute-start.27 = (bf16[128,1024]{1,0:T(8,128)(2,1)S(1)}, bf16[128,1024]{1,0:T(8,128)(2,1)S(1)}, u32[]{:S(2)}, u32[]{:S(2)}) collective-permute-start(bf16[128,1024]{1,0:T(8,128)(2,1)S(1)} %get-tuple-element.200), channel_id=1, source_target_pairs={{0,1},{1,0},{2,3},{3,2},{4,5},{5,4},{6,7},{7,6},{8,9},{9,8},{10,11... | collective-permute-start | bytes 786440 | tf_op jit(solution)/shard_map/ppermute | solution.py:20
  71.8 7.9 %collective-permute-start.33 = (bf16[128,1024]{1,0:T(8,128)(2,1)S(1)}, bf16[128,1024]{1,0:T(8,128)(2,1)S(1)}, u32[]{:S(2)}, u32[]{:S(2)}) collective-permute-start(bf16[128,1024]{1,0:T(8,128)(2,1)S(1)} %get-tuple-element.218), channel_id=1, source_target_pairs={{0,1},{1,0},{2,3},{3,2},{4,5},{5,4},{6,7},{7,6},{8,9},{9,8},{10,11... | collective-permute-start | bytes 786440 | tf_op jit(solution)/shard_map/ppermute | solution.py:20
  73.6 6.2 %collective-permute-start.32 = (bf16[128,1024]{1,0:T(8,128)(2,1)S(1)}, bf16[128,1024]{1,0:T(8,128)(2,1)S(1)}, u32[]{:S(2)}, u32[]{:S(2)}) collective-permute-start(bf16[128,1024]{1,0:T(8,128)(2,1)S(1)} %get-tuple-element.217), channel_id=1, source_target_pairs={{0,4},{1,2},{2,1},{3,7},{4,0},{5,6},{6,5},{7,3},{8,12},{9,10},{10,... | collective-permute-start | bytes 786440 | tf_op jit(solution)/shard_map/ppermute | solution.py:30
  79.9 9.2 %collective-permute-start.34 = (bf16[128,1024]{1,0:T(8,128)(2,1)S(1)}, bf16[128,1024]{1,0:T(8,128)(2,1)S(1)}, u32[]{:S(2)}, u32[]{:S(2)}) collective-permute-start(bf16[128,1024]{1,0:T(8,128)(2,1)S(1)} %get-tuple-element.221), channel_id=1, source_target_pairs={{0,1},{1,0},{2,3},{3,2},{4,5},{5,4},{6,7},{7,6},{8,9},{9,8},{10,11... | collective-permute-start | bytes 786440 | tf_op jit(solution)/shard_map/ppermute | solution.py:20
  83.2 11.7 %collective-permute-start.37 = (bf16[128,1024]{1,0:T(8,128)(2,1)S(1)}, bf16[128,1024]{1,0:T(8,128)(2,1)S(1)}, u32[]{:S(2)}, u32[]{:S(2)}) collective-permute-start(bf16[128,1024]{1,0:T(8,128)(2,1)S(1)} %get-tuple-element.232), channel_id=1, source_target_pairs={{0,1},{1,0},{2,3},{3,2},{4,5},{5,4},{6,7},{7,6},{8,9},{9,8},{10,11... | collective-permute-start | bytes 786440 | tf_op jit(solution)/shard_map/ppermute | solution.py:20
  89.2 5.9 %collective-permute-start.36 = (bf16[2,128,256]{2,1,0:T(8,128)(2,1)S(1)}, bf16[2,128,256]{2,1,0:T(8,128)(2,1)S(1)}, u32[]{:S(2)}, u32[]{:S(2)}) collective-permute-start(bf16[2,128,256]{2,1,0:T(8,128)(2,1)S(1)} %get-tuple-element.230), channel_id=1, source_target_pairs={{0,4},{1,2},{2,1},{3,7},{4,0},{5,6},{6,5},{7,3},{8,12},{9,10},{10,... | collective-permute-start | bytes 393224 | tf_op jit(solution)/shard_map/ppermute | solution.py:30
  90.4 7.9 %collective-permute-start.40 = (bf16[2,128,256]{2,1,0:T(8,128)(2,1)S(1)}, bf16[2,128,256]{2,1,0:T(8,128)(2,1)S(1)}, u32[]{:S(2)}, u32[]{:S(2)}) collective-permute-start(bf16[2,128,256]{2,1,0:T(8,128)(2,1)S(1)} %get-tuple-element.242), channel_id=1, source_target_pairs={{0,1},{1,0},{2,3},{3,2},{4,5},{5,4},{6,7},{7,6},{8,9},{9,8},{10,11... | collective-permute-start | bytes 393224 | tf_op jit(solution)/shard_map/ppermute | solution.py:20
  95.0 7.5 %collective-permute-start.39 = (bf16[2,128,256]{2,1,0:T(8,128)(2,1)S(1)}, bf16[2,128,256]{2,1,0:T(8,128)(2,1)S(1)}, u32[]{:S(2)}, u32[]{:S(2)}) collective-permute-start(bf16[2,128,256]{2,1,0:T(8,128)(2,1)S(1)} %get-tuple-element.240), channel_id=1, source_target_pairs={{0,4},{1,2},{2,1},{3,7},{4,0},{5,6},{6,5},{7,3},{8,12},{9,10},{10,... | collective-permute-start | bytes 393224 | tf_op jit(solution)/shard_map/ppermute | solution.py:30
  95.1 8.3 %collective-permute-start.38 = (bf16[128,256]{1,0:T(8,128)(2,1)S(1)}, bf16[128,256]{1,0:T(8,128)(2,1)S(1)}, u32[]{:S(2)}, u32[]{:S(2)}) collective-permute-start(bf16[128,256]{1,0:T(8,128)(2,1)S(1)} %get-tuple-element.238), channel_id=1, source_target_pairs={{0,1},{1,0},{2,3},{3,2},{4,5},{5,4},{6,7},{7,6},{8,9},{9,8},{10,11... | collective-permute-start | bytes 196616 | tf_op jit(solution)/shard_map/ppermute | solution.py:20
  98.3 9.1 %collective-permute-start.42 = (bf16[1,128,256]{2,1,0:T(8,128)(2,1)S(1)}, bf16[1,128,256]{2,1,0:T(8,128)(2,1)S(1)}, u32[]{:S(2)}, u32[]{:S(2)}) collective-permute-start(bf16[1,128,256]{2,1,0:T(8,128)(2,1)S(1)} %get-tuple-element.250), channel_id=1, source_target_pairs={{0,2},{1,3},{2,0},{3,1},{4,6},{5,7},{6,4},{7,5},{8,10},{9,11},{10,... | collective-permute-start | bytes 196616 | tf_op jit(solution)/shard_map/ppermute | solution.py:20
  99.0 8.4 %collective-permute-start.43 = (bf16[128,256]{1,0:T(8,128)(2,1)S(1)}, bf16[128,256]{1,0:T(8,128)(2,1)S(1)}, u32[]{:S(2)}, u32[]{:S(2)}) collective-permute-start(bf16[128,256]{1,0:T(8,128)(2,1)S(1)} %get-tuple-element.252), channel_id=1, source_target_pairs={{0,3},{1,2},{2,1},{3,0},{4,7},{5,6},{6,5},{7,4},{8,11},{9,10},{10,... | collective-permute-start | bytes 196616 | tf_op jit(solution)/shard_map/ppermute | solution.py:20
  100.8 8.3 %collective-permute-start.44 = (bf16[128,256]{1,0:T(8,128)(2,1)S(1)}, bf16[128,256]{1,0:T(8,128)(2,1)S(1)}, u32[]{:S(2)}, u32[]{:S(2)}) collective-permute-start(bf16[128,256]{1,0:T(8,128)(2,1)S(1)} %get-tuple-element.253), channel_id=1, source_target_pairs={{0,2},{1,3},{2,0},{3,1},{4,6},{5,7},{6,4},{7,5},{8,10},{9,11},{10,... | collective-permute-start | bytes 196616 | tf_op jit(solution)/shard_map/ppermute | solution.py:20
  102.5 6.6 %collective-permute-start.45 = (bf16[128,256]{1,0:T(8,128)(2,1)S(1)}, bf16[128,256]{1,0:T(8,128)(2,1)S(1)}, u32[]{:S(2)}, u32[]{:S(2)}) collective-permute-start(bf16[128,256]{1,0:T(8,128)(2,1)S(1)} %get-tuple-element.254), channel_id=1, source_target_pairs={{0,1},{1,0},{2,3},{3,2},{4,5},{5,4},{6,7},{7,6},{8,9},{9,8},{10,11... | collective-permute-start | bytes 196616 | tf_op jit(solution)/shard_map/ppermute | solution.py:20
  (31 other events, 123.2 us)

commit v6 on v5

--- a/solution.py
+++ b/solution.py
@@ -189,20 +189,14 @@
         pl.when(jnp.logical_not(is_middle()))(send_part)
 
 
-def choose(wide_ref, arrived_ref, rows_ref):
-    @pl.when(is_middle())
-    def _():
-        rows_ref[...] = wide_ref[...]
-
-    @pl.when(jnp.logical_not(is_middle()))
-    def _():
-        rows_ref[...] = arrived_ref[...].astype(F32)
-
-
-def qkv_kernel(wide_ref, arrived_ref, gain_ref, weight_ref, query_ref, kv_ref, rows_ref):
-    choose(wide_ref, arrived_ref, rows_ref)
-    for block in row_blocks(rows_ref.shape[0]):
-        normed = normalize(rows_ref[block, :].astype(F32), gain_ref[0, 0:1, :]).astype(BF16)
+def choose(wide_ref, arrived_ref, block):
+    return jnp.where(is_middle(), wide_ref[block, :], arrived_ref[block, :].astype(F32))
+
+
+def qkv_kernel(wide_ref, arrived_ref, gain_ref, weight_ref, query_ref, kv_ref):
+    for block in row_blocks(wide_ref.shape[0]):
+        rows = choose(wide_ref, arrived_ref, block)
+        normed = normalize(rows, gain_ref[0, 0:1, :]).astype(BF16)
         query_ref[block, :] = dot(normed, weight_ref[0, 0]).astype(BF16)
         kv_ref[0, block, :] = dot(normed, weight_ref[0, 1]).astype(BF16)
         kv_ref[1, block, :] = dot(normed, weight_ref[0, 2]).astype(BF16)
@@ -245,16 +239,16 @@
 
 
 def mlp_kernel(count, form, wide_ref, arrived_ref, gain_ref, gate_up_ref, down_ref, *refs):
-    kept_ref, *sent_refs, rows_ref, act_ref = refs
+    kept_ref, *sent_refs, act_ref = refs
     sent_ref = sent_refs[0]
-    choose(wide_ref, arrived_ref, rows_ref)
     index = lax.axis_index("hidden")
     hidden = act_ref.shape[1]
     step = min(hidden, 256)
     width = down_ref.shape[2] // count
     own = pl.ds(pl.multiple_of(index * width, width), width)
-    for block in row_blocks(rows_ref.shape[0]):
-        normed = normalize(rows_ref[block, :], gain_ref[0, 1:2, :]).astype(BF16)
+    for block in row_blocks(wide_ref.shape[0]):
+        normed = normalize(choose(wide_ref, arrived_ref, block), gain_ref[0, 1:2, :]).astype(BF16)
+        residual = jnp.where(is_middle(), wide_ref[block, own], arrived_ref[block, own].astype(F32))
         for start in range(0, hidden, step):
             columns = pl.ds(start, step)
             gate_sum = dot(normed, gate_up_ref[0, 0, :, columns])
@@ -268,13 +262,14 @@
                 if i:
                     sent_refs[i - 1][block, :] = total.astype(BF16)
                 else:
-                    kept_ref[block, :] = total + rows_ref[block, columns]
+                    kept_ref[block, :] = total + residual
             continue
         if form == "whole":
             total = dot(act_ref[...], down_ref[0])
             sent_ref[block, :] = total.astype(BF16)
             kept_ref[block, :] = total
-            kept_ref[block, own] = kept_ref[block, own] + rows_ref[block, own]
+            kept_ref[block, own] = kept_ref[block, own] + residual
+            sent_refs[1][block, :] = kept_ref[block, own]
             continue
         for i in range(count // 2):
             owner = index ^ (2 * i)
@@ -285,7 +280,7 @@
             columns = pl.ds(pl.multiple_of(owner * width, width), width)
             total = dot(act_ref[...], down_ref[0, :, columns])
             if i == 0:
-                total = total + rows_ref[block, columns]
+                total = total + residual
             kept_ref[i, block, :] = total
 
 
@@ -317,13 +312,10 @@
     sent_ref[...] = (mine_ref[kept:] + arrived_ref[kept:].astype(F32)).astype(BF16)
 
 
-def final_kernel(count, forms, *refs):
+def final_kernel(forms, *refs):
     *in_refs, out_ref, rows_ref, sems = refs
-    chunks = rows_ref.shape[0]
-    stride = out_ref.shape[1] // count
-    size = stride // chunks
-    width = out_ref.shape[2]
-    index = lax.axis_index("hidden")
+    chunks, count, size, width = rows_ref.shape
+    shape = (count, size, width)
     copies = []
     for chunk in range(chunks):
         if forms[chunk] == "direct":
@@ -331,27 +323,24 @@
             total = total_ref[...]
             for arrived_ref in in_refs:
                 total = total + arrived_ref[...].astype(F32)
-            rows_ref[chunk] = total
+            rows_ref[chunk] = total.reshape(shape)
         elif forms[chunk] == "whole":
             own_ref, mine_ref, arrived_ref, *in_refs = in_refs
 
             @pl.when(is_middle())
             def _():
-                rows_ref[chunk] = own_ref[...]
+                rows_ref[chunk] = own_ref[...].reshape(shape)
 
             @pl.when(jnp.logical_not(is_middle()))
             def _():
-                mine = mine_ref[:, pl.ds(pl.multiple_of(index * width, width), width)]
-                rows_ref[chunk] = mine + arrived_ref[...].astype(F32)
+                rows_ref[chunk] = (mine_ref[...] + arrived_ref[...].astype(F32)).reshape(shape)
 
         else:
             wide_ref, arrived_ref, *in_refs = in_refs
-            rows_ref[chunk] = wide_ref[0] + arrived_ref[0].astype(F32)
-        for i in range(count):
-            source = rows_ref.at[chunk, pl.ds(i * size, size), :]
-            target = out_ref.at[0, pl.ds(i * stride + chunk * size, size), :]
-            copies.append(pltpu.make_async_copy(source, target, sems.at[chunk, i]))
-            copies[-1].start()
+            rows_ref[chunk] = (wide_ref[0] + arrived_ref[0].astype(F32)).reshape(shape)
+        target = out_ref.at[0, :, pl.ds(chunk * size, size), :]
+        copies.append(pltpu.make_async_copy(rows_ref.at[chunk], target, sems.at[chunk]))
+        copies[-1].start()
     for copy in copies:
         copy.wait()
 
@@ -441,7 +430,6 @@
                 "qkv",
                 [((rows, local_width), BF16), ((2, rows, local_width), BF16)],
                 [s["x_zero"], s["x_zero_arrived"], norm_gains, qkv_weight],
-                [pltpu.VMEM((rows, width), F32)],
             )
             s["kvs"] = {0: kv} | {bit: swap(kv, "codebook", bit) for bit in code_bits}
 
@@ -450,7 +438,7 @@
             for bit in code_bits:
                 for slot in [slot for slot in s["kvs"] if slot > bit and not slot & (2 * bit - 1)]:
                     (kv,) = step(pass_kernel, "pass", [((2, rows, local_width), BF16)], [s["kvs"][slot]], aliases={0: 0})
-                    s["kvs"][slot ^ bit] = swap(kv, "codebook", bit)
+                    s["kvs"][slot], s["kvs"][slot ^ bit] = kv, swap(kv, "codebook", bit)
 
     def attend(c):
         if (s := get(c)) is not None:
@@ -473,14 +461,16 @@
                 "halves": (hidden_count // 2, rows, local_width),
                 "direct": (rows, local_width),
             }[form(c)]
-            messages = hidden_count - 1 if form(c) == "direct" else 1
+            more = {"whole": [F32], "halves": [], "direct": [BF16] * (hidden_count - 2)}[form(c)]
             s["sums"], s["sums_sent"], *others = step(
                 functools.partial(mlp_kernel, hidden_count, form(c)),
                 "mlp",
-                [(shape, F32)] + [(shape, BF16)] * messages,
+                [(shape, F32), (shape, BF16)] + [((rows, local_width), dtype) for dtype in more],
                 [s["residual"], s["residual_arrived"], norm_gains, gate_up, down_weight],
-                [pltpu.VMEM((rows, width), F32), pltpu.VMEM((min(rows, 128), gate_up.shape[3]), BF16)],
+                [pltpu.VMEM((min(rows, 128), gate_up.shape[3]), BF16)],
             )
+            if form(c) == "whole":
+                s["mine"] = others[0]
             if form(c) == "halves":
                 s["arrived"] = swap(s["sums_sent"], "hidden", pair_bit)
             if form(c) == "direct":
@@ -515,27 +505,35 @@
         forms = [form(c) for c in range(CHUNKS)]
         args = []
         for s, kind in zip(states, forms):
-            names = {"whole": ("own", "sums", "last"), "halves": ("wide", "last"), "direct": ("sums",)}[kind]
+            names = {"whole": ("own", "mine", "last"), "halves": ("wide", "last"), "direct": ("sums",)}[kind]
             args += [s[name] for name in names] + s.get("direct", [])
-        return step(
-            functools.partial(final_kernel, code_count, forms),
+        out = step(
+            functools.partial(final_kernel, forms),
             "final",
-            [((1, row_count, local_width), F32)],
+            [((1, code_count, block_rows, local_width), F32)],
             args,
-            [pltpu.VMEM((CHUNKS, rows, local_width), F32), pltpu.SemaphoreType.DMA((CHUNKS, code_count))],
+            [
+                pltpu.VMEM((CHUNKS, code_count, size, local_width), F32),
+                pltpu.SemaphoreType.DMA((CHUNKS,)),
+            ],
             out_space=pl.ANY,
         )[0]
+        return out.reshape(1, row_count, local_width)
 
     stages = 9
     project(0)
     for t in range(CHUNKS + stages - 1):
-        pair_sum(t - 1)
-        pair_sum(t - 5)
-        exchange(t)
-        qkv(t - 3)
+        if t < 3:
+            exchange(t)
+            pair_sum(t - 1)
+        else:
+            qkv(t - 3)
+            pair_sum(t - 1)
+            pair_sum(t - 5)
+            exchange(t)
         collect(t - 9)
+        mlp(t - 7)
         give_back(t - 10)
-        mlp(t - 7)
         halve(t - 8)
         project(t + 1)
         embed(t - 1)

time: 111 us -> 110 us (level)
  starting transfers between devices: 46 us -> 41.5 us
  waiting for transfers between devices: 42.6 us -> 46.2 us
    ppermute x35, waiting for transfers between devices: 42.3 us -> 45.9 us  [swap(): return lax.ppermute(block, axis, [(i, i ^ distance) for i in range(count)])]
    ppermute x35, starting transfers between devices: 43.3 us -> 39.8 us  [swap(): return lax.ppermute(block, axis, [(i, i ^ distance) for i in range(count)])]
    ppermute x1, starting transfers between devices: 2.4 us -> 1.28 us  [shifted(): return lax.ppermute(block, axis, route)]
  transfers between devices with their start and end apart: 46 -> 46, of which waited for: 26 -> 25; matrix products, arithmetic and copies ran while one was open for 1% -> 1% of each run, Pallas kernels for 13% -> 15%
where the time goes in v6:
time: 110 us
  waiting for transfers between devices  46.2 us (42%)
  starting transfers between devices  41.5 us (38%)
  Pallas kernels  17.9 us (16%)
  local copies, waits for them, and re-layouts  3.41 us (3%)
    ppermute x35, waiting for transfers between devices, swap(): return lax.ppermute(block, axis, [(i, i ^ distance) for i in range(count)])  45.9 us
    ppermute x35, starting transfers between devices, swap(): return lax.ppermute(block, axis, [(i, i ^ distance) for i in range(count)])  39.8 us
    pallas_call x48, Pallas kernels, __call__(): pl.pallas_call(with_token, name=name, out_shape=[jax.ShapeDtypeStruct(sha...  17.9 us
  transfers between devices with their start and end apart: 46, of which 25 were waited for; matrix products, arithmetic and copies ran while one was open for 1% of the time, Pallas kernels for 15%

profile of v6, /device:TPU:0, one launch (start us, length us, event | category | flops | bytes accessed | tf_op | source)
XLA Modules:
  0.0 109.6 jit_solution(15606165041120578271)
XLA Ops:
  0.8 2.9 %collective-permute-start.4 = (bf16[32,1024]{1,0:T(8,128)(2,1)S(1)}, bf16[32,1024]{1,0:T(8,128)(2,1)S(1)}, u32[]{:S(2)}, u32[]{:S(2)}) collective-permute-start(bf16[32,1024]{1,0:T(8,128)(2,1)S(1)} %slice.7.refs_0_), channel_id=1, source_target_pairs={{0,8},{4,12},{8,0},{12,4},{1,9},{5,13},{9,1},{13,5},{2,10},{6,14},... | collective-permute-start | bytes 196616 | tf_op jit(solution)/shard_map/ppermute | solution.py:20
  7.5 1.6 %copy-done.2 = bf16[1,1024,1024]{2,1,0:T(8,128)(2,1)S(1)} copy-done((bf16[1,1024,1024]{2,1,0:T(8,128)(2,1)S(1)}, bf16[1,1024,1024]{2,1,0:T(8,128)(2,1)}, u32[]{:S(2)}) %copy-start.2) | copy-done | bytes 2097176
  9.7 1.9 %collective-permute-start.6 = (bf16[128,1024]{1,0:T(8,128)(2,1)S(1)}, bf16[128,1024]{1,0:T(8,128)(2,1)S(1)}, u32[]{:S(2)}, u32[]{:S(2)}) collective-permute-start(bf16[128,1024]{1,0:T(8,128)(2,1)S(1)} %get-tuple-element.135), channel_id=1, source_target_pairs={{0,1},{1,0},{2,3},{3,2},{4,5},{5,4},{6,7},{7,6},{8,9},{9,8},{10,11... | collective-permute-start | bytes 786440 | tf_op jit(solution)/shard_map/ppermute | solution.py:20
  13.9 4.3 %collective-permute-done.6.refs_1_ = bf16[128,1024]{1,0:T(8,128)(2,1)S(1)} collective-permute-done((bf16[128,1024]{1,0:T(8,128)(2,1)S(1)}, bf16[128,1024]{1,0:T(8,128)(2,1)S(1)}, u32[]{:S(2)}, u32[]{:S(2)}) %collective-permute-start.6) | collective-permute-done | bytes 262176 | tf_op jit(solution)/shard_map/ppermute | solution.py:20
  18.4 3.3 %collective-permute-start.10 = (bf16[128,1024]{1,0:T(8,128)(2,1)S(1)}, bf16[128,1024]{1,0:T(8,128)(2,1)S(1)}, u32[]{:S(2)}, u32[]{:S(2)}) collective-permute-start(bf16[128,1024]{1,0:T(8,128)(2,1)S(1)} %get-tuple-element.149), channel_id=1, source_target_pairs={{0,1},{1,0},{2,3},{3,2},{4,5},{5,4},{6,7},{7,6},{8,9},{9,8},{10,11... | collective-permute-start | bytes 786440 | tf_op jit(solution)/shard_map/ppermute | solution.py:20
  24.7 3.1 %collective-permute-start.9 = (bf16[128,1024]{1,0:T(8,128)(2,1)S(1)}, bf16[128,1024]{1,0:T(8,128)(2,1)S(1)}, u32[]{:S(2)}, u32[]{:S(2)}) collective-permute-start(bf16[128,1024]{1,0:T(8,128)(2,1)S(1)} %get-tuple-element.148), channel_id=1, source_target_pairs={{0,1},{1,0},{2,3},{3,2},{4,5},{5,4},{6,7},{7,6},{8,9},{9,8},{10,11... | collective-permute-start | bytes 786440 | tf_op jit(solution)/shard_map/ppermute | solution.py:20
  29.5 4.9 %collective-permute-done.9.refs_1_ = bf16[128,1024]{1,0:T(8,128)(2,1)S(1)} collective-permute-done((bf16[128,1024]{1,0:T(8,128)(2,1)S(1)}, bf16[128,1024]{1,0:T(8,128)(2,1)S(1)}, u32[]{:S(2)}, u32[]{:S(2)}) %collective-permute-start.9) | collective-permute-done | bytes 262176 | tf_op jit(solution)/shard_map/ppermute | solution.py:20
  34.9 1.7 %collective-permute-start.12 = (bf16[2,128,256]{2,1,0:T(8,128)(2,1)S(1)}, bf16[2,128,256]{2,1,0:T(8,128)(2,1)S(1)}, u32[]{:S(2)}, u32[]{:S(2)}) collective-permute-start(bf16[2,128,256]{2,1,0:T(8,128)(2,1)S(1)} %get-tuple-element.155.refs_1_), channel_id=1, source_target_pairs={{0,8},{4,12},{8,0},{12,4},{1,9},{5,13},{9,1},{13,5},{2,10},{6,14},... | collective-permute-start | bytes 393224 | tf_op jit(solution)/shard_map/ppermute | solution.py:20
  39.1 1.6 %collective-permute-done.12.refs_0_ = bf16[2,128,256]{2,1,0:T(8,128)(2,1)S(1)} collective-permute-done((bf16[2,128,256]{2,1,0:T(8,128)(2,1)S(1)}, bf16[2,128,256]{2,1,0:T(8,128)(2,1)S(1)}, u32[]{:S(2)}, u32[]{:S(2)}) %collective-permute-start.12) | collective-permute-done | bytes 131104 | tf_op jit(solution)/shard_map/ppermute | solution.py:20
  44.3 1.8 %collective-permute-start.19 = (bf16[2,128,256]{2,1,0:T(8,128)(2,1)S(1)}, bf16[2,128,256]{2,1,0:T(8,128)(2,1)S(1)}, u32[]{:S(2)}, u32[]{:S(2)}) collective-permute-start(bf16[2,128,256]{2,1,0:T(8,128)(2,1)S(1)} %get-tuple-element.178.refs_1_), channel_id=1, source_target_pairs={{0,8},{4,12},{8,0},{12,4},{1,9},{5,13},{9,1},{13,5},{2,10},{6,14},... | collective-permute-start | bytes 393224 | tf_op jit(solution)/shard_map/ppermute | solution.py:20
  51.4 2.2 %collective-permute-done.17.refs_1_ = bf16[128,1024]{1,0:T(8,128)(2,1)S(1)} collective-permute-done((bf16[128,1024]{1,0:T(8,128)(2,1)S(1)}, bf16[128,1024]{1,0:T(8,128)(2,1)S(1)}, u32[]{:S(2)}, u32[]{:S(2)}) %collective-permute-start.17) | collective-permute-done | bytes 262176 | tf_op jit(solution)/shard_map/ppermute | solution.py:20
  56.1 3.0 %collective-permute-done.22.refs_0_ = bf16[2,128,256]{2,1,0:T(8,128)(2,1)S(1)} collective-permute-done((bf16[2,128,256]{2,1,0:T(8,128)(2,1)S(1)}, bf16[2,128,256]{2,1,0:T(8,128)(2,1)S(1)}, u32[]{:S(2)}, u32[]{:S(2)}) %collective-permute-start.22) | collective-permute-done | bytes 131104 | tf_op jit(solution)/shard_map/ppermute | solution.py:20
  65.4 2.2 %collective-permute-done.29.refs_0_ = bf16[2,128,256]{2,1,0:T(8,128)(2,1)S(1)} collective-permute-done((bf16[2,128,256]{2,1,0:T(8,128)(2,1)S(1)}, bf16[2,128,256]{2,1,0:T(8,128)(2,1)S(1)}, u32[]{:S(2)}, u32[]{:S(2)}) %collective-permute-start.29) | collective-permute-done | bytes 131104 | tf_op jit(solution)/shard_map/ppermute | solution.py:20
  70.7 1.6 %collective-permute-start.33 = (bf16[128,1024]{1,0:T(8,128)(2,1)S(1)}, bf16[128,1024]{1,0:T(8,128)(2,1)S(1)}, u32[]{:S(2)}, u32[]{:S(2)}) collective-permute-start(bf16[128,1024]{1,0:T(8,128)(2,1)S(1)} %get-tuple-element.220), channel_id=1, source_target_pairs={{0,1},{1,0},{2,3},{3,2},{4,5},{5,4},{6,7},{7,6},{8,9},{9,8},{10,11... | collective-permute-start | bytes 786440 | tf_op jit(solution)/shard_map/ppermute | solution.py:20
  73.5 4.9 %collective-permute-done.33.refs_1_ = bf16[128,1024]{1,0:T(8,128)(2,1)S(1)} collective-permute-done((bf16[128,1024]{1,0:T(8,128)(2,1)S(1)}, bf16[128,1024]{1,0:T(8,128)(2,1)S(1)}, u32[]{:S(2)}, u32[]{:S(2)}) %collective-permute-start.33) | collective-permute-done | bytes 262176 | tf_op jit(solution)/shard_map/ppermute | solution.py:20
  78.6 2.6 %collective-permute-start.34 = (bf16[128,1024]{1,0:T(8,128)(2,1)S(1)}, bf16[128,1024]{1,0:T(8,128)(2,1)S(1)}, u32[]{:S(2)}, u32[]{:S(2)}) collective-permute-start(bf16[128,1024]{1,0:T(8,128)(2,1)S(1)} %get-tuple-element.223), channel_id=1, source_target_pairs={{0,1},{1,0},{2,3},{3,2},{4,5},{5,4},{6,7},{7,6},{8,9},{9,8},{10,11... | collective-permute-start | bytes 786440 | tf_op jit(solution)/shard_map/ppermute | solution.py:20
  82.5 3.5 %collective-permute-start.37 = (bf16[128,1024]{1,0:T(8,128)(2,1)S(1)}, bf16[128,1024]{1,0:T(8,128)(2,1)S(1)}, u32[]{:S(2)}, u32[]{:S(2)}) collective-permute-start(bf16[128,1024]{1,0:T(8,128)(2,1)S(1)} %get-tuple-element.234), channel_id=1, source_target_pairs={{0,1},{1,0},{2,3},{3,2},{4,5},{5,4},{6,7},{7,6},{8,9},{9,8},{10,11... | collective-permute-start | bytes 786440 | tf_op jit(solution)/shard_map/ppermute | solution.py:20
  86.0 2.4 %collective-permute-done.34.refs_1_ = bf16[128,1024]{1,0:T(8,128)(2,1)S(1)} collective-permute-done((bf16[128,1024]{1,0:T(8,128)(2,1)S(1)}, bf16[128,1024]{1,0:T(8,128)(2,1)S(1)}, u32[]{:S(2)}, u32[]{:S(2)}) %collective-permute-start.34) | collective-permute-done | bytes 262176 | tf_op jit(solution)/shard_map/ppermute | solution.py:20
  89.7 2.0 %collective-permute-start.40 = (bf16[2,128,256]{2,1,0:T(8,128)(2,1)S(1)}, bf16[2,128,256]{2,1,0:T(8,128)(2,1)S(1)}, u32[]{:S(2)}, u32[]{:S(2)}) collective-permute-start(bf16[2,128,256]{2,1,0:T(8,128)(2,1)S(1)} %get-tuple-element.247), channel_id=1, source_target_pairs={{0,1},{1,0},{2,3},{3,2},{4,5},{5,4},{6,7},{7,6},{8,9},{9,8},{10,11... | collective-permute-start | bytes 393224 | tf_op jit(solution)/shard_map/ppermute | solution.py:20
  94.4 1.8 %collective-permute-start.38 = (bf16[128,256]{1,0:T(8,128)(2,1)S(1)}, bf16[128,256]{1,0:T(8,128)(2,1)S(1)}, u32[]{:S(2)}, u32[]{:S(2)}) collective-permute-start(bf16[128,256]{1,0:T(8,128)(2,1)S(1)} %get-tuple-element.243), channel_id=1, source_target_pairs={{0,1},{1,0},{2,3},{3,2},{4,5},{5,4},{6,7},{7,6},{8,9},{9,8},{10,11... | collective-permute-start | bytes 196616 | tf_op jit(solution)/shard_map/ppermute | solution.py:20
  97.5 1.6 %collective-permute-start.43 = (bf16[128,256]{1,0:T(8,128)(2,1)S(1)}, bf16[128,256]{1,0:T(8,128)(2,1)S(1)}, u32[]{:S(2)}, u32[]{:S(2)}) collective-permute-start(bf16[128,256]{1,0:T(8,128)(2,1)S(1)} %get-tuple-element.256), channel_id=1, source_target_pairs={{0,3},{1,2},{2,1},{3,0},{4,7},{5,6},{6,5},{7,4},{8,11},{9,10},{10,... | collective-permute-start | bytes 196616 | tf_op jit(solution)/shard_map/ppermute | solution.py:20
  99.9 2.0 %collective-permute-start.45 = (bf16[128,256]{1,0:T(8,128)(2,1)S(1)}, bf16[128,256]{1,0:T(8,128)(2,1)S(1)}, u32[]{:S(2)}, u32[]{:S(2)}) collective-permute-start(bf16[128,256]{1,0:T(8,128)(2,1)S(1)} %get-tuple-element.258), channel_id=1, source_target_pairs={{0,1},{1,0},{2,3},{3,2},{4,5},{5,4},{6,7},{7,6},{8,9},{9,8},{10,11... | collective-permute-start | bytes 196616 | tf_op jit(solution)/shard_map/ppermute | solution.py:20
  102.1 3.6 %collective-permute-done.42.refs_7_ = bf16[1,128,256]{2,1,0:T(8,128)(2,1)S(1)} collective-permute-done((bf16[1,128,256]{2,1,0:T(8,128)(2,1)S(1)}, bf16[1,128,256]{2,1,0:T(8,128)(2,1)S(1)}, u32[]{:S(2)}, u32[]{:S(2)}) %collective-permute-start.42) | collective-permute-done | bytes 65568 | tf_op jit(solution)/shard_map/ppermute | solution.py:20
  105.6 2.0 %collective-permute-done.44.refs_10_ = bf16[128,256]{1,0:T(8,128)(2,1)S(1)} collective-permute-done((bf16[128,256]{1,0:T(8,128)(2,1)S(1)}, bf16[128,256]{1,0:T(8,128)(2,1)S(1)}, u32[]{:S(2)}, u32[]{:S(2)}) %collective-permute-start.44) | collective-permute-done | bytes 65568 | tf_op jit(solution)/shard_map/ppermute | solution.py:20
  (136 shorter events, 46.3 us)
Async XLA Ops:
  4.7 6.9 %collective-permute-start.1 = (bf16[96,1024]{1,0:T(8,128)(2,1)S(1)}, bf16[96,1024]{1,0:T(8,128)(2,1)S(1)}, u32[]{:S(2)}, u32[]{:S(2)}) collective-permute-start(bf16[96,1024]{1,0:T(8,128)(2,1)S(1)} %slice.6.refs_0_), channel_id=1, source_target_pairs={{0,8},{4,12},{8,0},{12,4},{1,9},{5,13},{9,1},{13,5},{2,10},{6,14},... | collective-permute-start | bytes 589832 | tf_op jit(solution)/shard_map/ppermute | solution.py:20
  9.7 8.6 %collective-permute-start.6 = (bf16[128,1024]{1,0:T(8,128)(2,1)S(1)}, bf16[128,1024]{1,0:T(8,128)(2,1)S(1)}, u32[]{:S(2)}, u32[]{:S(2)}) collective-permute-start(bf16[128,1024]{1,0:T(8,128)(2,1)S(1)} %get-tuple-element.135), channel_id=1, source_target_pairs={{0,1},{1,0},{2,3},{3,2},{4,5},{5,4},{6,7},{7,6},{8,9},{9,8},{10,11... | collective-permute-start | bytes 786440 | tf_op jit(solution)/shard_map/ppermute | solution.py:20
  18.3 6.3 %collective-permute-start.7 = (bf16[128,1024]{1,0:T(8,128)(2,1)S(1)}, bf16[128,1024]{1,0:T(8,128)(2,1)S(1)}, u32[]{:S(2)}, u32[]{:S(2)}) collective-permute-start(bf16[128,1024]{1,0:T(8,128)(2,1)S(1)} %get-tuple-element.143), channel_id=1, source_target_pairs={{0,4},{1,2},{2,1},{3,7},{4,0},{5,6},{6,5},{7,3},{8,12},{9,10},{10,... | collective-permute-start | bytes 786440 | tf_op jit(solution)/shard_map/ppermute | solution.py:30
  18.4 9.5 %collective-permute-start.10 = (bf16[128,1024]{1,0:T(8,128)(2,1)S(1)}, bf16[128,1024]{1,0:T(8,128)(2,1)S(1)}, u32[]{:S(2)}, u32[]{:S(2)}) collective-permute-start(bf16[128,1024]{1,0:T(8,128)(2,1)S(1)} %get-tuple-element.149), channel_id=1, source_target_pairs={{0,1},{1,0},{2,3},{3,2},{4,5},{5,4},{6,7},{7,6},{8,9},{9,8},{10,11... | collective-permute-start | bytes 786440 | tf_op jit(solution)/shard_map/ppermute | solution.py:20
  24.7 9.7 %collective-permute-start.9 = (bf16[128,1024]{1,0:T(8,128)(2,1)S(1)}, bf16[128,1024]{1,0:T(8,128)(2,1)S(1)}, u32[]{:S(2)}, u32[]{:S(2)}) collective-permute-start(bf16[128,1024]{1,0:T(8,128)(2,1)S(1)} %get-tuple-element.148), channel_id=1, source_target_pairs={{0,1},{1,0},{2,3},{3,2},{4,5},{5,4},{6,7},{7,6},{8,9},{9,8},{10,11... | collective-permute-start | bytes 786440 | tf_op jit(solution)/shard_map/ppermute | solution.py:20
  27.9 8.7 %collective-permute-start.13 = (bf16[128,1024]{1,0:T(8,128)(2,1)S(1)}, bf16[128,1024]{1,0:T(8,128)(2,1)S(1)}, u32[]{:S(2)}, u32[]{:S(2)}) collective-permute-start(bf16[128,1024]{1,0:T(8,128)(2,1)S(1)} %get-tuple-element.158), channel_id=1, source_target_pairs={{0,4},{1,2},{2,1},{3,7},{4,0},{5,6},{6,5},{7,3},{8,12},{9,10},{10,... | collective-permute-start | bytes 786440 | tf_op jit(solution)/shard_map/ppermute | solution.py:30
  36.7 7.1 %collective-permute-start.16 = (bf16[128,1024]{1,0:T(8,128)(2,1)S(1)}, bf16[128,1024]{1,0:T(8,128)(2,1)S(1)}, u32[]{:S(2)}, u32[]{:S(2)}) collective-permute-start(bf16[128,1024]{1,0:T(8,128)(2,1)S(1)} %get-tuple-element.170), channel_id=1, source_target_pairs={{0,1},{1,0},{2,3},{3,2},{4,5},{5,4},{6,7},{7,6},{8,9},{9,8},{10,11... | collective-permute-start | bytes 786440 | tf_op jit(solution)/shard_map/ppermute | solution.py:20
  37.8 8.4 %collective-permute-start.15 = (bf16[128,1024]{1,0:T(8,128)(2,1)S(1)}, bf16[128,1024]{1,0:T(8,128)(2,1)S(1)}, u32[]{:S(2)}, u32[]{:S(2)}) collective-permute-start(bf16[128,1024]{1,0:T(8,128)(2,1)S(1)} %get-tuple-element.168), channel_id=1, source_target_pairs={{0,4},{1,2},{2,1},{3,7},{4,0},{5,6},{6,5},{7,3},{8,12},{9,10},{10,... | collective-permute-start | bytes 786440 | tf_op jit(solution)/shard_map/ppermute | solution.py:30
  46.2 7.4 %collective-permute-start.17 = (bf16[128,1024]{1,0:T(8,128)(2,1)S(1)}, bf16[128,1024]{1,0:T(8,128)(2,1)S(1)}, u32[]{:S(2)}, u32[]{:S(2)}) collective-permute-start(bf16[128,1024]{1,0:T(8,128)(2,1)S(1)} %get-tuple-element.176), channel_id=1, source_target_pairs={{0,1},{1,0},{2,3},{3,2},{4,5},{5,4},{6,7},{7,6},{8,9},{9,8},{10,11... | collective-permute-start | bytes 786440 | tf_op jit(solution)/shard_map/ppermute | solution.py:20
  46.7 7.9 %collective-permute-start.23 = (bf16[128,1024]{1,0:T(8,128)(2,1)S(1)}, bf16[128,1024]{1,0:T(8,128)(2,1)S(1)}, u32[]{:S(2)}, u32[]{:S(2)}) collective-permute-start(bf16[128,1024]{1,0:T(8,128)(2,1)S(1)} %get-tuple-element.188), channel_id=1, source_target_pairs={{0,4},{1,2},{2,1},{3,7},{4,0},{5,6},{6,5},{7,3},{8,12},{9,10},{10,... | collective-permute-start | bytes 786440 | tf_op jit(solution)/shard_map/ppermute | solution.py:30
  54.6 7.4 %collective-permute-start.26 = (bf16[128,1024]{1,0:T(8,128)(2,1)S(1)}, bf16[128,1024]{1,0:T(8,128)(2,1)S(1)}, u32[]{:S(2)}, u32[]{:S(2)}) collective-permute-start(bf16[128,1024]{1,0:T(8,128)(2,1)S(1)} %get-tuple-element.198), channel_id=1, source_target_pairs={{0,1},{1,0},{2,3},{3,2},{4,5},{5,4},{6,7},{7,6},{8,9},{9,8},{10,11... | collective-permute-start | bytes 786440 | tf_op jit(solution)/shard_map/ppermute | solution.py:20
  55.6 7.8 %collective-permute-start.25 = (bf16[128,1024]{1,0:T(8,128)(2,1)S(1)}, bf16[128,1024]{1,0:T(8,128)(2,1)S(1)}, u32[]{:S(2)}, u32[]{:S(2)}) collective-permute-start(bf16[128,1024]{1,0:T(8,128)(2,1)S(1)} %get-tuple-element.197), channel_id=1, source_target_pairs={{0,4},{1,2},{2,1},{3,7},{4,0},{5,6},{6,5},{7,3},{8,12},{9,10},{10,... | collective-permute-start | bytes 786440 | tf_op jit(solution)/shard_map/ppermute | solution.py:30
  63.5 6.9 %collective-permute-start.27 = (bf16[128,1024]{1,0:T(8,128)(2,1)S(1)}, bf16[128,1024]{1,0:T(8,128)(2,1)S(1)}, u32[]{:S(2)}, u32[]{:S(2)}) collective-permute-start(bf16[128,1024]{1,0:T(8,128)(2,1)S(1)} %get-tuple-element.204), channel_id=1, source_target_pairs={{0,1},{1,0},{2,3},{3,2},{4,5},{5,4},{6,7},{7,6},{8,9},{9,8},{10,11... | collective-permute-start | bytes 786440 | tf_op jit(solution)/shard_map/ppermute | solution.py:20
  70.7 7.7 %collective-permute-start.33 = (bf16[128,1024]{1,0:T(8,128)(2,1)S(1)}, bf16[128,1024]{1,0:T(8,128)(2,1)S(1)}, u32[]{:S(2)}, u32[]{:S(2)}) collective-permute-start(bf16[128,1024]{1,0:T(8,128)(2,1)S(1)} %get-tuple-element.220), channel_id=1, source_target_pairs={{0,1},{1,0},{2,3},{3,2},{4,5},{5,4},{6,7},{7,6},{8,9},{9,8},{10,11... | collective-permute-start | bytes 786440 | tf_op jit(solution)/shard_map/ppermute | solution.py:20
  72.3 6.3 %collective-permute-start.32 = (bf16[128,1024]{1,0:T(8,128)(2,1)S(1)}, bf16[128,1024]{1,0:T(8,128)(2,1)S(1)}, u32[]{:S(2)}, u32[]{:S(2)}) collective-permute-start(bf16[128,1024]{1,0:T(8,128)(2,1)S(1)} %get-tuple-element.219), channel_id=1, source_target_pairs={{0,4},{1,2},{2,1},{3,7},{4,0},{5,6},{6,5},{7,3},{8,12},{9,10},{10,... | collective-permute-start | bytes 786440 | tf_op jit(solution)/shard_map/ppermute | solution.py:30
  78.6 9.8 %collective-permute-start.34 = (bf16[128,1024]{1,0:T(8,128)(2,1)S(1)}, bf16[128,1024]{1,0:T(8,128)(2,1)S(1)}, u32[]{:S(2)}, u32[]{:S(2)}) collective-permute-start(bf16[128,1024]{1,0:T(8,128)(2,1)S(1)} %get-tuple-element.223), channel_id=1, source_target_pairs={{0,1},{1,0},{2,3},{3,2},{4,5},{5,4},{6,7},{7,6},{8,9},{9,8},{10,11... | collective-permute-start | bytes 786440 | tf_op jit(solution)/shard_map/ppermute | solution.py:20
  82.5 10.6 %collective-permute-start.37 = (bf16[128,1024]{1,0:T(8,128)(2,1)S(1)}, bf16[128,1024]{1,0:T(8,128)(2,1)S(1)}, u32[]{:S(2)}, u32[]{:S(2)}) collective-permute-start(bf16[128,1024]{1,0:T(8,128)(2,1)S(1)} %get-tuple-element.234), channel_id=1, source_target_pairs={{0,1},{1,0},{2,3},{3,2},{4,5},{5,4},{6,7},{7,6},{8,9},{9,8},{10,11... | collective-permute-start | bytes 786440 | tf_op jit(solution)/shard_map/ppermute | solution.py:20
  89.7 6.6 %collective-permute-start.40 = (bf16[2,128,256]{2,1,0:T(8,128)(2,1)S(1)}, bf16[2,128,256]{2,1,0:T(8,128)(2,1)S(1)}, u32[]{:S(2)}, u32[]{:S(2)}) collective-permute-start(bf16[2,128,256]{2,1,0:T(8,128)(2,1)S(1)} %get-tuple-element.247), channel_id=1, source_target_pairs={{0,1},{1,0},{2,3},{3,2},{4,5},{5,4},{6,7},{7,6},{8,9},{9,8},{10,11... | collective-permute-start | bytes 393224 | tf_op jit(solution)/shard_map/ppermute | solution.py:20
  93.2 6.7 %collective-permute-start.39 = (bf16[2,128,256]{2,1,0:T(8,128)(2,1)S(1)}, bf16[2,128,256]{2,1,0:T(8,128)(2,1)S(1)}, u32[]{:S(2)}, u32[]{:S(2)}) collective-permute-start(bf16[2,128,256]{2,1,0:T(8,128)(2,1)S(1)} %get-tuple-element.245), channel_id=1, source_target_pairs={{0,4},{1,2},{2,1},{3,7},{4,0},{5,6},{6,5},{7,3},{8,12},{9,10},{10,... | collective-permute-start | bytes 393224 | tf_op jit(solution)/shard_map/ppermute | solution.py:30
  94.4 7.5 %collective-permute-start.38 = (bf16[128,256]{1,0:T(8,128)(2,1)S(1)}, bf16[128,256]{1,0:T(8,128)(2,1)S(1)}, u32[]{:S(2)}, u32[]{:S(2)}) collective-permute-start(bf16[128,256]{1,0:T(8,128)(2,1)S(1)} %get-tuple-element.243), channel_id=1, source_target_pairs={{0,1},{1,0},{2,3},{3,2},{4,5},{5,4},{6,7},{7,6},{8,9},{9,8},{10,11... | collective-permute-start | bytes 196616 | tf_op jit(solution)/shard_map/ppermute | solution.py:20
  96.3 9.4 %collective-permute-start.42 = (bf16[1,128,256]{2,1,0:T(8,128)(2,1)S(1)}, bf16[1,128,256]{2,1,0:T(8,128)(2,1)S(1)}, u32[]{:S(2)}, u32[]{:S(2)}) collective-permute-start(bf16[1,128,256]{2,1,0:T(8,128)(2,1)S(1)} %get-tuple-element.254), channel_id=1, source_target_pairs={{0,2},{1,3},{2,0},{3,1},{4,6},{5,7},{6,4},{7,5},{8,10},{9,11},{10,... | collective-permute-start | bytes 196616 | tf_op jit(solution)/shard_map/ppermute | solution.py:20
  97.5 8.1 %collective-permute-start.43 = (bf16[128,256]{1,0:T(8,128)(2,1)S(1)}, bf16[128,256]{1,0:T(8,128)(2,1)S(1)}, u32[]{:S(2)}, u32[]{:S(2)}) collective-permute-start(bf16[128,256]{1,0:T(8,128)(2,1)S(1)} %get-tuple-element.256), channel_id=1, source_target_pairs={{0,3},{1,2},{2,1},{3,0},{4,7},{5,6},{6,5},{7,4},{8,11},{9,10},{10,... | collective-permute-start | bytes 196616 | tf_op jit(solution)/shard_map/ppermute | solution.py:20
  99.1 8.6 %collective-permute-start.44 = (bf16[128,256]{1,0:T(8,128)(2,1)S(1)}, bf16[128,256]{1,0:T(8,128)(2,1)S(1)}, u32[]{:S(2)}, u32[]{:S(2)}) collective-permute-start(bf16[128,256]{1,0:T(8,128)(2,1)S(1)} %get-tuple-element.257), channel_id=1, source_target_pairs={{0,2},{1,3},{2,0},{3,1},{4,6},{5,7},{6,4},{7,5},{8,10},{9,11},{10,... | collective-permute-start | bytes 196616 | tf_op jit(solution)/shard_map/ppermute | solution.py:20
  99.9 7.8 %collective-permute-start.45 = (bf16[128,256]{1,0:T(8,128)(2,1)S(1)}, bf16[128,256]{1,0:T(8,128)(2,1)S(1)}, u32[]{:S(2)}, u32[]{:S(2)}) collective-permute-start(bf16[128,256]{1,0:T(8,128)(2,1)S(1)} %get-tuple-element.258), channel_id=1, source_target_pairs={{0,1},{1,0},{2,3},{3,2},{4,5},{5,4},{6,7},{7,6},{8,9},{9,8},{10,11... | collective-permute-start | bytes 196616 | tf_op jit(solution)/shard_map/ppermute | solution.py:20
  (31 other events, 130.7 us)

commit v7 on v6

--- a/solution.py
+++ b/solution.py
@@ -202,14 +202,36 @@
         kv_ref[1, block, :] = dot(normed, weight_ref[0, 2]).astype(BF16)
 
 
-def attend_kernel(head_size, query_ref, *refs):
+def per_head(width, lanes, head_size):
+    column = lax.broadcasted_iota(jnp.int32, (width, lanes), 0) // head_size
+    head = lax.broadcasted_iota(jnp.int32, (width, lanes), 1)
+    return (column == head).astype(F32).astype(BF16)
+
+
+def score(slot, head_size, query, keys):
+    product = query * keys.astype(F32)
+    high = product.astype(BF16)
+    low = (product - high.astype(F32)).astype(BF16)
+    gather = per_head(query.shape[1], 128, head_size)
+    result = (dot(high, gather) + dot(low, gather)) * head_size ** (-0.5)
+    if slot:
+        code = lax.axis_index("codebook")
+        result = jnp.where((code ^ slot) <= code, result, -1e30)
+    return result
+
+
+def score_kernel(slots, head_size, query_ref, *refs):
+    *kv_refs, scores_ref = refs
+    for block in row_blocks(query_ref.shape[0]):
+        query = query_ref[block, :].astype(F32)
+        for i, (slot, kv_ref) in enumerate(zip(slots, kv_refs)):
+            scores_ref[i, block, :] = score(slot, head_size, query, kv_ref[0, block, :])
+
+
+def attend_kernel(early, head_size, query_ref, scores_ref, *refs):
     *kv_refs, weight_ref, part_ref = refs
-    code = lax.axis_index("codebook")
     width = query_ref.shape[-1]
     lanes = 128
-    column = lax.broadcasted_iota(jnp.int32, (width, lanes), 0) // head_size
-    head = lax.broadcasted_iota(jnp.int32, (width, lanes), 1)
-    gather = (column == head).astype(F32).astype(BF16)
     head_t = lax.broadcasted_iota(jnp.int32, (lanes, width), 0)
     column_t = lax.broadcasted_iota(jnp.int32, (lanes, width), 1) // head_size
     spread = (column_t == head_t).astype(F32).astype(BF16)
@@ -217,15 +239,12 @@
         query = query_ref[block, :].astype(F32)
         scores = []
         for slot, kv_ref in enumerate(kv_refs):
-            product = query * kv_ref[0, block, :].astype(F32)
-            high = product.astype(BF16)
-            low = (product - high.astype(F32)).astype(BF16)
-            score = (dot(high, gather) + dot(low, gather)) * head_size ** (-0.5)
-            if slot:
-                score = jnp.where((code ^ slot) <= code, score, -1e30)
-            scores.append(score)
+            if slot in early:
+                scores.append(scores_ref[early.index(slot), block, :])
+            else:
+                scores.append(score(slot, head_size, query, kv_ref[0, block, :]))
         highest = functools.reduce(jnp.maximum, scores)
-        weights = [jnp.exp(score - highest) for score in scores]
+        weights = [jnp.exp(one - highest) for one in scores]
         running = functools.reduce(jnp.add, weights)
         summed = None
         for kv_ref, weight in zip(kv_refs, weights):
@@ -442,11 +461,18 @@
 
     def attend(c):
         if (s := get(c)) is not None:
+            early = (0, *code_bits)
+            (scores,) = step(
+                functools.partial(score_kernel, early, head_size),
+                "score",
+                [((len(early), rows, 128), F32)],
+                [s["query"], *[s["kvs"][slot] for slot in early]],
+            )
             s["part"] = step(
-                functools.partial(attend_kernel, head_size),
+                functools.partial(attend_kernel, early, head_size),
                 "attend",
                 [wide],
-                [s["query"], *[s["kvs"][slot] for slot in range(code_count)], out_weight],
+                [s["query"], scores, *[s["kvs"][slot] for slot in range(code_count)], out_weight],
             )[0]
 
     def form(c):
@@ -527,9 +553,9 @@
             exchange(t)
             pair_sum(t - 1)
         else:
-            qkv(t - 3)
             pair_sum(t - 1)
             pair_sum(t - 5)
+            qkv(t - 3)
             exchange(t)
         collect(t - 9)
         mlp(t - 7)

time: 110 us -> 109 us (level)
  waiting for transfers between devices: 46.2 us -> 44.9 us
    ppermute x35, waiting for transfers between devices: 45.9 us -> 44.7 us  [swap(): return lax.ppermute(block, axis, [(i, i ^ distance) for i in range(count)])]
    pallas_call x48 -> x52, Pallas kernels: 17.9 us -> 18.5 us  [__call__(): pl.pallas_call(with_token, name=name, out_shape=[jax.ShapeDtypeStruct(sha...]
  transfers between devices with their start and end apart: 46 -> 46, of which waited for: 25 -> 25; matrix products, arithmetic and copies ran while one was open for 1% -> 1% of each run, Pallas kernels for 15% -> 16%
where the time goes in v7:
time: 109 us
  waiting for transfers between devices  44.9 us (41%)
  starting transfers between devices  41.6 us (38%)
  Pallas kernels  18.5 us (17%)
  local copies, waits for them, and re-layouts  3.41 us (3%)
    ppermute x35, waiting for transfers between devices, swap(): return lax.ppermute(block, axis, [(i, i ^ distance) for i in range(count)])  44.7 us
    ppermute x35, starting transfers between devices, swap(): return lax.ppermute(block, axis, [(i, i ^ distance) for i in range(count)])  40 us
    pallas_call x52, Pallas kernels, __call__(): pl.pallas_call(with_token, name=name, out_shape=[jax.ShapeDtypeStruct(sha...  18.5 us
  transfers between devices with their start and end apart: 46, of which 25 were waited for; matrix products, arithmetic and copies ran while one was open for 1% of the time, Pallas kernels for 16%

profile of v7, /device:TPU:0, one launch (start us, length us, event | category | flops | bytes accessed | tf_op | source)
XLA Modules:
  0.0 109.2 jit_solution(13015569098145618603)
XLA Ops:
  0.8 2.9 %collective-permute-start.4 = (bf16[32,1024]{1,0:T(8,128)(2,1)S(1)}, bf16[32,1024]{1,0:T(8,128)(2,1)S(1)}, u32[]{:S(2)}, u32[]{:S(2)}) collective-permute-start(bf16[32,1024]{1,0:T(8,128)(2,1)S(1)} %slice.7.refs_0_), channel_id=1, source_target_pairs={{0,8},{4,12},{8,0},{12,4},{1,9},{5,13},{9,1},{13,5},{2,10},{6,14},... | collective-permute-start | bytes 196616 | tf_op jit(solution)/shard_map/ppermute | solution.py:20
  7.5 1.6 %copy-done.2 = bf16[1,1024,1024]{2,1,0:T(8,128)(2,1)S(1)} copy-done((bf16[1,1024,1024]{2,1,0:T(8,128)(2,1)S(1)}, bf16[1,1024,1024]{2,1,0:T(8,128)(2,1)}, u32[]{:S(2)}) %copy-start.2) | copy-done | bytes 2097176
  9.7 1.9 %collective-permute-start.6 = (bf16[128,1024]{1,0:T(8,128)(2,1)S(1)}, bf16[128,1024]{1,0:T(8,128)(2,1)S(1)}, u32[]{:S(2)}, u32[]{:S(2)}) collective-permute-start(bf16[128,1024]{1,0:T(8,128)(2,1)S(1)} %get-tuple-element.143), channel_id=1, source_target_pairs={{0,1},{1,0},{2,3},{3,2},{4,5},{5,4},{6,7},{7,6},{8,9},{9,8},{10,11... | collective-permute-start | bytes 786440 | tf_op jit(solution)/shard_map/ppermute | solution.py:20
  13.9 4.3 %collective-permute-done.6.refs_1_ = bf16[128,1024]{1,0:T(8,128)(2,1)S(1)} collective-permute-done((bf16[128,1024]{1,0:T(8,128)(2,1)S(1)}, bf16[128,1024]{1,0:T(8,128)(2,1)S(1)}, u32[]{:S(2)}, u32[]{:S(2)}) %collective-permute-start.6) | collective-permute-done | bytes 262176 | tf_op jit(solution)/shard_map/ppermute | solution.py:20
  18.4 3.3 %collective-permute-start.10 = (bf16[128,1024]{1,0:T(8,128)(2,1)S(1)}, bf16[128,1024]{1,0:T(8,128)(2,1)S(1)}, u32[]{:S(2)}, u32[]{:S(2)}) collective-permute-start(bf16[128,1024]{1,0:T(8,128)(2,1)S(1)} %get-tuple-element.157), channel_id=1, source_target_pairs={{0,1},{1,0},{2,3},{3,2},{4,5},{5,4},{6,7},{7,6},{8,9},{9,8},{10,11... | collective-permute-start | bytes 786440 | tf_op jit(solution)/shard_map/ppermute | solution.py:20
  24.7 3.1 %collective-permute-start.9 = (bf16[128,1024]{1,0:T(8,128)(2,1)S(1)}, bf16[128,1024]{1,0:T(8,128)(2,1)S(1)}, u32[]{:S(2)}, u32[]{:S(2)}) collective-permute-start(bf16[128,1024]{1,0:T(8,128)(2,1)S(1)} %get-tuple-element.156), channel_id=1, source_target_pairs={{0,1},{1,0},{2,3},{3,2},{4,5},{5,4},{6,7},{7,6},{8,9},{9,8},{10,11... | collective-permute-start | bytes 786440 | tf_op jit(solution)/shard_map/ppermute | solution.py:20
  29.5 4.9 %collective-permute-done.9.refs_1_ = bf16[128,1024]{1,0:T(8,128)(2,1)S(1)} collective-permute-done((bf16[128,1024]{1,0:T(8,128)(2,1)S(1)}, bf16[128,1024]{1,0:T(8,128)(2,1)S(1)}, u32[]{:S(2)}, u32[]{:S(2)}) %collective-permute-start.9) | collective-permute-done | bytes 262176 | tf_op jit(solution)/shard_map/ppermute | solution.py:20
  35.0 1.7 %collective-permute-start.11 = (bf16[2,128,256]{2,1,0:T(8,128)(2,1)S(1)}, bf16[2,128,256]{2,1,0:T(8,128)(2,1)S(1)}, u32[]{:S(2)}, u32[]{:S(2)}) collective-permute-start(bf16[2,128,256]{2,1,0:T(8,128)(2,1)S(1)} %get-tuple-element.164.refs_1_.refs_2_), channel_id=1, source_target_pairs={{0,8},{4,12},{8,0},{12,4},{1,9},{5,13},{9,1},{13,5},{2,10},{6,14},... | collective-permute-start | bytes 393224 | tf_op jit(solution)/shard_map/ppermute | solution.py:20
  39.1 1.7 %collective-permute-done.11.refs_0_ = bf16[2,128,256]{2,1,0:T(8,128)(2,1)S(1)} collective-permute-done((bf16[2,128,256]{2,1,0:T(8,128)(2,1)S(1)}, bf16[2,128,256]{2,1,0:T(8,128)(2,1)S(1)}, u32[]{:S(2)}, u32[]{:S(2)}) %collective-permute-start.11) | collective-permute-done | bytes 131104 | tf_op jit(solution)/shard_map/ppermute | solution.py:20
  44.4 1.8 %collective-permute-start.18 = (bf16[2,128,256]{2,1,0:T(8,128)(2,1)S(1)}, bf16[2,128,256]{2,1,0:T(8,128)(2,1)S(1)}, u32[]{:S(2)}, u32[]{:S(2)}) collective-permute-start(bf16[2,128,256]{2,1,0:T(8,128)(2,1)S(1)} %get-tuple-element.188.refs_1_.refs_2_), channel_id=1, source_target_pairs={{0,8},{4,12},{8,0},{12,4},{1,9},{5,13},{9,1},{13,5},{2,10},{6,14},... | collective-permute-start | bytes 393224 | tf_op jit(solution)/shard_map/ppermute | solution.py:20
  51.4 2.1 %collective-permute-done.17.refs_1_ = bf16[128,1024]{1,0:T(8,128)(2,1)S(1)} collective-permute-done((bf16[128,1024]{1,0:T(8,128)(2,1)S(1)}, bf16[128,1024]{1,0:T(8,128)(2,1)S(1)}, u32[]{:S(2)}, u32[]{:S(2)}) %collective-permute-start.17) | collective-permute-done | bytes 262176 | tf_op jit(solution)/shard_map/ppermute | solution.py:20
  56.1 3.1 %collective-permute-done.21.refs_0_ = bf16[2,128,256]{2,1,0:T(8,128)(2,1)S(1)} collective-permute-done((bf16[2,128,256]{2,1,0:T(8,128)(2,1)S(1)}, bf16[2,128,256]{2,1,0:T(8,128)(2,1)S(1)}, u32[]{:S(2)}, u32[]{:S(2)}) %collective-permute-start.21) | collective-permute-done | bytes 131104 | tf_op jit(solution)/shard_map/ppermute | solution.py:20
  65.5 2.1 %collective-permute-done.28.refs_0_ = bf16[2,128,256]{2,1,0:T(8,128)(2,1)S(1)} collective-permute-done((bf16[2,128,256]{2,1,0:T(8,128)(2,1)S(1)}, bf16[2,128,256]{2,1,0:T(8,128)(2,1)S(1)}, u32[]{:S(2)}, u32[]{:S(2)}) %collective-permute-start.28) | collective-permute-done | bytes 131104 | tf_op jit(solution)/shard_map/ppermute | solution.py:20
  70.7 1.8 %collective-permute-start.33 = (bf16[128,1024]{1,0:T(8,128)(2,1)S(1)}, bf16[128,1024]{1,0:T(8,128)(2,1)S(1)}, u32[]{:S(2)}, u32[]{:S(2)}) collective-permute-start(bf16[128,1024]{1,0:T(8,128)(2,1)S(1)} %get-tuple-element.236), channel_id=1, source_target_pairs={{0,1},{1,0},{2,3},{3,2},{4,5},{5,4},{6,7},{7,6},{8,9},{9,8},{10,11... | collective-permute-start | bytes 786440 | tf_op jit(solution)/shard_map/ppermute | solution.py:20
  73.7 4.5 %collective-permute-done.33.refs_1_ = bf16[128,1024]{1,0:T(8,128)(2,1)S(1)} collective-permute-done((bf16[128,1024]{1,0:T(8,128)(2,1)S(1)}, bf16[128,1024]{1,0:T(8,128)(2,1)S(1)}, u32[]{:S(2)}, u32[]{:S(2)}) %collective-permute-start.33) | collective-permute-done | bytes 262176 | tf_op jit(solution)/shard_map/ppermute | solution.py:20
  78.4 2.8 %collective-permute-start.34 = (bf16[128,1024]{1,0:T(8,128)(2,1)S(1)}, bf16[128,1024]{1,0:T(8,128)(2,1)S(1)}, u32[]{:S(2)}, u32[]{:S(2)}) collective-permute-start(bf16[128,1024]{1,0:T(8,128)(2,1)S(1)} %get-tuple-element.239), channel_id=1, source_target_pairs={{0,1},{1,0},{2,3},{3,2},{4,5},{5,4},{6,7},{7,6},{8,9},{9,8},{10,11... | collective-permute-start | bytes 786440 | tf_op jit(solution)/shard_map/ppermute | solution.py:20
  82.4 3.3 %collective-permute-start.37 = (bf16[128,1024]{1,0:T(8,128)(2,1)S(1)}, bf16[128,1024]{1,0:T(8,128)(2,1)S(1)}, u32[]{:S(2)}, u32[]{:S(2)}) collective-permute-start(bf16[128,1024]{1,0:T(8,128)(2,1)S(1)} %get-tuple-element.250), channel_id=1, source_target_pairs={{0,1},{1,0},{2,3},{3,2},{4,5},{5,4},{6,7},{7,6},{8,9},{9,8},{10,11... | collective-permute-start | bytes 786440 | tf_op jit(solution)/shard_map/ppermute | solution.py:20
  85.7 2.7 %collective-permute-done.34.refs_1_ = bf16[128,1024]{1,0:T(8,128)(2,1)S(1)} collective-permute-done((bf16[128,1024]{1,0:T(8,128)(2,1)S(1)}, bf16[128,1024]{1,0:T(8,128)(2,1)S(1)}, u32[]{:S(2)}, u32[]{:S(2)}) %collective-permute-start.34) | collective-permute-done | bytes 262176 | tf_op jit(solution)/shard_map/ppermute | solution.py:20
  89.7 1.9 %collective-permute-start.40 = (bf16[2,128,256]{2,1,0:T(8,128)(2,1)S(1)}, bf16[2,128,256]{2,1,0:T(8,128)(2,1)S(1)}, u32[]{:S(2)}, u32[]{:S(2)}) collective-permute-start(bf16[2,128,256]{2,1,0:T(8,128)(2,1)S(1)} %get-tuple-element.263), channel_id=1, source_target_pairs={{0,1},{1,0},{2,3},{3,2},{4,5},{5,4},{6,7},{7,6},{8,9},{9,8},{10,11... | collective-permute-start | bytes 393224 | tf_op jit(solution)/shard_map/ppermute | solution.py:20
  95.7 1.6 %collective-permute-start.42 = (bf16[1,128,256]{2,1,0:T(8,128)(2,1)S(1)}, bf16[1,128,256]{2,1,0:T(8,128)(2,1)S(1)}, u32[]{:S(2)}, u32[]{:S(2)}) collective-permute-start(bf16[1,128,256]{2,1,0:T(8,128)(2,1)S(1)} %get-tuple-element.270), channel_id=1, source_target_pairs={{0,2},{1,3},{2,0},{3,1},{4,6},{5,7},{6,4},{7,5},{8,10},{9,11},{10,... | collective-permute-start | bytes 196616 | tf_op jit(solution)/shard_map/ppermute | solution.py:20
  97.3 1.7 %collective-permute-start.43 = (bf16[128,256]{1,0:T(8,128)(2,1)S(1)}, bf16[128,256]{1,0:T(8,128)(2,1)S(1)}, u32[]{:S(2)}, u32[]{:S(2)}) collective-permute-start(bf16[128,256]{1,0:T(8,128)(2,1)S(1)} %get-tuple-element.272), channel_id=1, source_target_pairs={{0,3},{1,2},{2,1},{3,0},{4,7},{5,6},{6,5},{7,4},{8,11},{9,10},{10,... | collective-permute-start | bytes 196616 | tf_op jit(solution)/shard_map/ppermute | solution.py:20
  99.7 2.0 %collective-permute-start.45 = (bf16[128,256]{1,0:T(8,128)(2,1)S(1)}, bf16[128,256]{1,0:T(8,128)(2,1)S(1)}, u32[]{:S(2)}, u32[]{:S(2)}) collective-permute-start(bf16[128,256]{1,0:T(8,128)(2,1)S(1)} %get-tuple-element.274), channel_id=1, source_target_pairs={{0,1},{1,0},{2,3},{3,2},{4,5},{5,4},{6,7},{7,6},{8,9},{9,8},{10,11... | collective-permute-start | bytes 196616 | tf_op jit(solution)/shard_map/ppermute | solution.py:20
  101.8 3.6 %collective-permute-done.42.refs_7_ = bf16[1,128,256]{2,1,0:T(8,128)(2,1)S(1)} collective-permute-done((bf16[1,128,256]{2,1,0:T(8,128)(2,1)S(1)}, bf16[1,128,256]{2,1,0:T(8,128)(2,1)S(1)}, u32[]{:S(2)}, u32[]{:S(2)}) %collective-permute-start.42) | collective-permute-done | bytes 65568 | tf_op jit(solution)/shard_map/ppermute | solution.py:20
  105.4 2.0 %collective-permute-done.44.refs_10_ = bf16[128,256]{1,0:T(8,128)(2,1)S(1)} collective-permute-done((bf16[128,256]{1,0:T(8,128)(2,1)S(1)}, bf16[128,256]{1,0:T(8,128)(2,1)S(1)}, u32[]{:S(2)}, u32[]{:S(2)}) %collective-permute-start.44) | collective-permute-done | bytes 65568 | tf_op jit(solution)/shard_map/ppermute | solution.py:20
  (140 shorter events, 46.0 us)
Async XLA Ops:
  4.7 6.9 %collective-permute-start.1 = (bf16[96,1024]{1,0:T(8,128)(2,1)S(1)}, bf16[96,1024]{1,0:T(8,128)(2,1)S(1)}, u32[]{:S(2)}, u32[]{:S(2)}) collective-permute-start(bf16[96,1024]{1,0:T(8,128)(2,1)S(1)} %slice.6.refs_0_), channel_id=1, source_target_pairs={{0,8},{4,12},{8,0},{12,4},{1,9},{5,13},{9,1},{13,5},{2,10},{6,14},... | collective-permute-start | bytes 589832 | tf_op jit(solution)/shard_map/ppermute | solution.py:20
  9.7 8.6 %collective-permute-start.6 = (bf16[128,1024]{1,0:T(8,128)(2,1)S(1)}, bf16[128,1024]{1,0:T(8,128)(2,1)S(1)}, u32[]{:S(2)}, u32[]{:S(2)}) collective-permute-start(bf16[128,1024]{1,0:T(8,128)(2,1)S(1)} %get-tuple-element.143), channel_id=1, source_target_pairs={{0,1},{1,0},{2,3},{3,2},{4,5},{5,4},{6,7},{7,6},{8,9},{9,8},{10,11... | collective-permute-start | bytes 786440 | tf_op jit(solution)/shard_map/ppermute | solution.py:20
  18.3 6.3 %collective-permute-start.7 = (bf16[128,1024]{1,0:T(8,128)(2,1)S(1)}, bf16[128,1024]{1,0:T(8,128)(2,1)S(1)}, u32[]{:S(2)}, u32[]{:S(2)}) collective-permute-start(bf16[128,1024]{1,0:T(8,128)(2,1)S(1)} %get-tuple-element.151), channel_id=1, source_target_pairs={{0,4},{1,2},{2,1},{3,7},{4,0},{5,6},{6,5},{7,3},{8,12},{9,10},{10,... | collective-permute-start | bytes 786440 | tf_op jit(solution)/shard_map/ppermute | solution.py:30
  18.4 9.5 %collective-permute-start.10 = (bf16[128,1024]{1,0:T(8,128)(2,1)S(1)}, bf16[128,1024]{1,0:T(8,128)(2,1)S(1)}, u32[]{:S(2)}, u32[]{:S(2)}) collective-permute-start(bf16[128,1024]{1,0:T(8,128)(2,1)S(1)} %get-tuple-element.157), channel_id=1, source_target_pairs={{0,1},{1,0},{2,3},{3,2},{4,5},{5,4},{6,7},{7,6},{8,9},{9,8},{10,11... | collective-permute-start | bytes 786440 | tf_op jit(solution)/shard_map/ppermute | solution.py:20
  24.7 9.7 %collective-permute-start.9 = (bf16[128,1024]{1,0:T(8,128)(2,1)S(1)}, bf16[128,1024]{1,0:T(8,128)(2,1)S(1)}, u32[]{:S(2)}, u32[]{:S(2)}) collective-permute-start(bf16[128,1024]{1,0:T(8,128)(2,1)S(1)} %get-tuple-element.156), channel_id=1, source_target_pairs={{0,1},{1,0},{2,3},{3,2},{4,5},{5,4},{6,7},{7,6},{8,9},{9,8},{10,11... | collective-permute-start | bytes 786440 | tf_op jit(solution)/shard_map/ppermute | solution.py:20
  27.9 8.7 %collective-permute-start.12 = (bf16[128,1024]{1,0:T(8,128)(2,1)S(1)}, bf16[128,1024]{1,0:T(8,128)(2,1)S(1)}, u32[]{:S(2)}, u32[]{:S(2)}) collective-permute-start(bf16[128,1024]{1,0:T(8,128)(2,1)S(1)} %get-tuple-element.167), channel_id=1, source_target_pairs={{0,4},{1,2},{2,1},{3,7},{4,0},{5,6},{6,5},{7,3},{8,12},{9,10},{10,... | collective-permute-start | bytes 786440 | tf_op jit(solution)/shard_map/ppermute | solution.py:30
  35.0 5.9 %collective-permute-start.11 = (bf16[2,128,256]{2,1,0:T(8,128)(2,1)S(1)}, bf16[2,128,256]{2,1,0:T(8,128)(2,1)S(1)}, u32[]{:S(2)}, u32[]{:S(2)}) collective-permute-start(bf16[2,128,256]{2,1,0:T(8,128)(2,1)S(1)} %get-tuple-element.164.refs_1_.refs_2_), channel_id=1, source_target_pairs={{0,8},{4,12},{8,0},{12,4},{1,9},{5,13},{9,1},{13,5},{2,10},{6,14},... | collective-permute-start | bytes 393224 | tf_op jit(solution)/shard_map/ppermute | solution.py:20
  36.7 7.1 %collective-permute-start.16 = (bf16[128,1024]{1,0:T(8,128)(2,1)S(1)}, bf16[128,1024]{1,0:T(8,128)(2,1)S(1)}, u32[]{:S(2)}, u32[]{:S(2)}) collective-permute-start(bf16[128,1024]{1,0:T(8,128)(2,1)S(1)} %get-tuple-element.181), channel_id=1, source_target_pairs={{0,1},{1,0},{2,3},{3,2},{4,5},{5,4},{6,7},{7,6},{8,9},{9,8},{10,11... | collective-permute-start | bytes 786440 | tf_op jit(solution)/shard_map/ppermute | solution.py:20
  37.8 8.4 %collective-permute-start.15 = (bf16[128,1024]{1,0:T(8,128)(2,1)S(1)}, bf16[128,1024]{1,0:T(8,128)(2,1)S(1)}, u32[]{:S(2)}, u32[]{:S(2)}) collective-permute-start(bf16[128,1024]{1,0:T(8,128)(2,1)S(1)} %get-tuple-element.178), channel_id=1, source_target_pairs={{0,4},{1,2},{2,1},{3,7},{4,0},{5,6},{6,5},{7,3},{8,12},{9,10},{10,... | collective-permute-start | bytes 786440 | tf_op jit(solution)/shard_map/ppermute | solution.py:30
  46.2 7.4 %collective-permute-start.17 = (bf16[128,1024]{1,0:T(8,128)(2,1)S(1)}, bf16[128,1024]{1,0:T(8,128)(2,1)S(1)}, u32[]{:S(2)}, u32[]{:S(2)}) collective-permute-start(bf16[128,1024]{1,0:T(8,128)(2,1)S(1)} %get-tuple-element.186), channel_id=1, source_target_pairs={{0,1},{1,0},{2,3},{3,2},{4,5},{5,4},{6,7},{7,6},{8,9},{9,8},{10,11... | collective-permute-start | bytes 786440 | tf_op jit(solution)/shard_map/ppermute | solution.py:20
  46.6 7.9 %collective-permute-start.22 = (bf16[128,1024]{1,0:T(8,128)(2,1)S(1)}, bf16[128,1024]{1,0:T(8,128)(2,1)S(1)}, u32[]{:S(2)}, u32[]{:S(2)}) collective-permute-start(bf16[128,1024]{1,0:T(8,128)(2,1)S(1)} %get-tuple-element.201), channel_id=1, source_target_pairs={{0,4},{1,2},{2,1},{3,7},{4,0},{5,6},{6,5},{7,3},{8,12},{9,10},{10,... | collective-permute-start | bytes 786440 | tf_op jit(solution)/shard_map/ppermute | solution.py:30
  54.6 7.4 %collective-permute-start.26 = (bf16[128,1024]{1,0:T(8,128)(2,1)S(1)}, bf16[128,1024]{1,0:T(8,128)(2,1)S(1)}, u32[]{:S(2)}, u32[]{:S(2)}) collective-permute-start(bf16[128,1024]{1,0:T(8,128)(2,1)S(1)} %get-tuple-element.213), channel_id=1, source_target_pairs={{0,1},{1,0},{2,3},{3,2},{4,5},{5,4},{6,7},{7,6},{8,9},{9,8},{10,11... | collective-permute-start | bytes 786440 | tf_op jit(solution)/shard_map/ppermute | solution.py:20
  55.6 7.8 %collective-permute-start.25 = (bf16[128,1024]{1,0:T(8,128)(2,1)S(1)}, bf16[128,1024]{1,0:T(8,128)(2,1)S(1)}, u32[]{:S(2)}, u32[]{:S(2)}) collective-permute-start(bf16[128,1024]{1,0:T(8,128)(2,1)S(1)} %get-tuple-element.211), channel_id=1, source_target_pairs={{0,4},{1,2},{2,1},{3,7},{4,0},{5,6},{6,5},{7,3},{8,12},{9,10},{10,... | collective-permute-start | bytes 786440 | tf_op jit(solution)/shard_map/ppermute | solution.py:30
  63.6 6.9 %collective-permute-start.27 = (bf16[128,1024]{1,0:T(8,128)(2,1)S(1)}, bf16[128,1024]{1,0:T(8,128)(2,1)S(1)}, u32[]{:S(2)}, u32[]{:S(2)}) collective-permute-start(bf16[128,1024]{1,0:T(8,128)(2,1)S(1)} %get-tuple-element.218), channel_id=1, source_target_pairs={{0,1},{1,0},{2,3},{3,2},{4,5},{5,4},{6,7},{7,6},{8,9},{9,8},{10,11... | collective-permute-start | bytes 786440 | tf_op jit(solution)/shard_map/ppermute | solution.py:20
  70.7 7.5 %collective-permute-start.33 = (bf16[128,1024]{1,0:T(8,128)(2,1)S(1)}, bf16[128,1024]{1,0:T(8,128)(2,1)S(1)}, u32[]{:S(2)}, u32[]{:S(2)}) collective-permute-start(bf16[128,1024]{1,0:T(8,128)(2,1)S(1)} %get-tuple-element.236), channel_id=1, source_target_pairs={{0,1},{1,0},{2,3},{3,2},{4,5},{5,4},{6,7},{7,6},{8,9},{9,8},{10,11... | collective-permute-start | bytes 786440 | tf_op jit(solution)/shard_map/ppermute | solution.py:20
  78.4 10.0 %collective-permute-start.34 = (bf16[128,1024]{1,0:T(8,128)(2,1)S(1)}, bf16[128,1024]{1,0:T(8,128)(2,1)S(1)}, u32[]{:S(2)}, u32[]{:S(2)}) collective-permute-start(bf16[128,1024]{1,0:T(8,128)(2,1)S(1)} %get-tuple-element.239), channel_id=1, source_target_pairs={{0,1},{1,0},{2,3},{3,2},{4,5},{5,4},{6,7},{7,6},{8,9},{9,8},{10,11... | collective-permute-start | bytes 786440 | tf_op jit(solution)/shard_map/ppermute | solution.py:20
  82.4 10.3 %collective-permute-start.37 = (bf16[128,1024]{1,0:T(8,128)(2,1)S(1)}, bf16[128,1024]{1,0:T(8,128)(2,1)S(1)}, u32[]{:S(2)}, u32[]{:S(2)}) collective-permute-start(bf16[128,1024]{1,0:T(8,128)(2,1)S(1)} %get-tuple-element.250), channel_id=1, source_target_pairs={{0,1},{1,0},{2,3},{3,2},{4,5},{5,4},{6,7},{7,6},{8,9},{9,8},{10,11... | collective-permute-start | bytes 786440 | tf_op jit(solution)/shard_map/ppermute | solution.py:20
  89.7 6.0 %collective-permute-start.40 = (bf16[2,128,256]{2,1,0:T(8,128)(2,1)S(1)}, bf16[2,128,256]{2,1,0:T(8,128)(2,1)S(1)}, u32[]{:S(2)}, u32[]{:S(2)}) collective-permute-start(bf16[2,128,256]{2,1,0:T(8,128)(2,1)S(1)} %get-tuple-element.263), channel_id=1, source_target_pairs={{0,1},{1,0},{2,3},{3,2},{4,5},{5,4},{6,7},{7,6},{8,9},{9,8},{10,11... | collective-permute-start | bytes 393224 | tf_op jit(solution)/shard_map/ppermute | solution.py:20
  92.8 6.8 %collective-permute-start.39 = (bf16[2,128,256]{2,1,0:T(8,128)(2,1)S(1)}, bf16[2,128,256]{2,1,0:T(8,128)(2,1)S(1)}, u32[]{:S(2)}, u32[]{:S(2)}) collective-permute-start(bf16[2,128,256]{2,1,0:T(8,128)(2,1)S(1)} %get-tuple-element.261), channel_id=1, source_target_pairs={{0,4},{1,2},{2,1},{3,7},{4,0},{5,6},{6,5},{7,3},{8,12},{9,10},{10,... | collective-permute-start | bytes 393224 | tf_op jit(solution)/shard_map/ppermute | solution.py:30
  94.1 7.6 %collective-permute-start.38 = (bf16[128,256]{1,0:T(8,128)(2,1)S(1)}, bf16[128,256]{1,0:T(8,128)(2,1)S(1)}, u32[]{:S(2)}, u32[]{:S(2)}) collective-permute-start(bf16[128,256]{1,0:T(8,128)(2,1)S(1)} %get-tuple-element.259), channel_id=1, source_target_pairs={{0,1},{1,0},{2,3},{3,2},{4,5},{5,4},{6,7},{7,6},{8,9},{9,8},{10,11... | collective-permute-start | bytes 196616 | tf_op jit(solution)/shard_map/ppermute | solution.py:20
  95.7 9.7 %collective-permute-start.42 = (bf16[1,128,256]{2,1,0:T(8,128)(2,1)S(1)}, bf16[1,128,256]{2,1,0:T(8,128)(2,1)S(1)}, u32[]{:S(2)}, u32[]{:S(2)}) collective-permute-start(bf16[1,128,256]{2,1,0:T(8,128)(2,1)S(1)} %get-tuple-element.270), channel_id=1, source_target_pairs={{0,2},{1,3},{2,0},{3,1},{4,6},{5,7},{6,4},{7,5},{8,10},{9,11},{10,... | collective-permute-start | bytes 196616 | tf_op jit(solution)/shard_map/ppermute | solution.py:20
  97.3 8.1 %collective-permute-start.43 = (bf16[128,256]{1,0:T(8,128)(2,1)S(1)}, bf16[128,256]{1,0:T(8,128)(2,1)S(1)}, u32[]{:S(2)}, u32[]{:S(2)}) collective-permute-start(bf16[128,256]{1,0:T(8,128)(2,1)S(1)} %get-tuple-element.272), channel_id=1, source_target_pairs={{0,3},{1,2},{2,1},{3,0},{4,7},{5,6},{6,5},{7,4},{8,11},{9,10},{10,... | collective-permute-start | bytes 196616 | tf_op jit(solution)/shard_map/ppermute | solution.py:20
  99.0 8.4 %collective-permute-start.44 = (bf16[128,256]{1,0:T(8,128)(2,1)S(1)}, bf16[128,256]{1,0:T(8,128)(2,1)S(1)}, u32[]{:S(2)}, u32[]{:S(2)}) collective-permute-start(bf16[128,256]{1,0:T(8,128)(2,1)S(1)} %get-tuple-element.273), channel_id=1, source_target_pairs={{0,2},{1,3},{2,0},{3,1},{4,6},{5,7},{6,4},{7,5},{8,10},{9,11},{10,... | collective-permute-start | bytes 196616 | tf_op jit(solution)/shard_map/ppermute | solution.py:20
  99.7 7.8 %collective-permute-start.45 = (bf16[128,256]{1,0:T(8,128)(2,1)S(1)}, bf16[128,256]{1,0:T(8,128)(2,1)S(1)}, u32[]{:S(2)}, u32[]{:S(2)}) collective-permute-start(bf16[128,256]{1,0:T(8,128)(2,1)S(1)} %get-tuple-element.274), channel_id=1, source_target_pairs={{0,1},{1,0},{2,3},{3,2},{4,5},{5,4},{6,7},{7,6},{8,9},{9,8},{10,11... | collective-permute-start | bytes 196616 | tf_op jit(solution)/shard_map/ppermute | solution.py:20
  (31 other events, 126.9 us)

commit v8 on v7

--- a/solution.py
+++ b/solution.py
@@ -561,9 +561,9 @@
         mlp(t - 7)
         give_back(t - 10)
         halve(t - 8)
-        project(t + 1)
         embed(t - 1)
         forward(t - 3)
+        project(t + 1)
         attend(t - 3)
     return final()
 

time: 109 us -> 110 us (level)
  starting transfers between devices: 41.6 us -> 47.7 us
  waiting for transfers between devices: 44.9 us -> 39.8 us
    ppermute x35, starting transfers between devices: 40 us -> 45.9 us  [swap(): return lax.ppermute(block, axis, [(i, i ^ distance) for i in range(count)])]
    ppermute x35, waiting for transfers between devices: 44.7 us -> 39 us  [swap(): return lax.ppermute(block, axis, [(i, i ^ distance) for i in range(count)])]
  transfers between devices with their start and end apart: 46 -> 46, of which waited for: 25 -> 26; matrix products, arithmetic and copies ran while one was open for 1% -> 1% of each run, Pallas kernels for 16% -> 15%
where the time goes in v8:
time: 110 us
  starting transfers between devices  47.7 us (43%)
  waiting for transfers between devices  39.8 us (36%)
  Pallas kernels  18.5 us (17%)
  local copies, waits for them, and re-layouts  3.41 us (3%)
    ppermute x35, starting transfers between devices, swap(): return lax.ppermute(block, axis, [(i, i ^ distance) for i in range(count)])  45.9 us
    ppermute x35, waiting for transfers between devices, swap(): return lax.ppermute(block, axis, [(i, i ^ distance) for i in range(count)])  39 us
    pallas_call x52, Pallas kernels, __call__(): pl.pallas_call(with_token, name=name, out_shape=[jax.ShapeDtypeStruct(sha...  18.5 us
  transfers between devices with their start and end apart: 46, of which 26 were waited for; matrix products, arithmetic and copies ran while one was open for 1% of the time, Pallas kernels for 15%

profile of v8, /device:TPU:0, one launch (start us, length us, event | category | flops | bytes accessed | tf_op | source)
XLA Modules:
  0.0 110.1 jit_solution(5449944776407155024)
XLA Ops:
  0.8 2.9 %collective-permute-start.5 = (bf16[32,1024]{1,0:T(8,128)(2,1)S(1)}, bf16[32,1024]{1,0:T(8,128)(2,1)S(1)}, u32[]{:S(2)}, u32[]{:S(2)}) collective-permute-start(bf16[32,1024]{1,0:T(8,128)(2,1)S(1)} %slice.7.refs_0_), channel_id=1, source_target_pairs={{0,8},{4,12},{8,0},{12,4},{1,9},{5,13},{9,1},{13,5},{2,10},{6,14},... | collective-permute-start | bytes 196616 | tf_op jit(solution)/shard_map/ppermute | solution.py:20
  7.5 1.6 %copy-done.2 = bf16[1,1024,1024]{2,1,0:T(8,128)(2,1)S(1)} copy-done((bf16[1,1024,1024]{2,1,0:T(8,128)(2,1)S(1)}, bf16[1,1024,1024]{2,1,0:T(8,128)(2,1)}, u32[]{:S(2)}) %copy-start.2) | copy-done | bytes 2097176
  9.7 1.9 %collective-permute-start.7 = (bf16[128,1024]{1,0:T(8,128)(2,1)S(1)}, bf16[128,1024]{1,0:T(8,128)(2,1)S(1)}, u32[]{:S(2)}, u32[]{:S(2)}) collective-permute-start(bf16[128,1024]{1,0:T(8,128)(2,1)S(1)} %get-tuple-element.143), channel_id=1, source_target_pairs={{0,1},{1,0},{2,3},{3,2},{4,5},{5,4},{6,7},{7,6},{8,9},{9,8},{10,11... | collective-permute-start | bytes 786440 | tf_op jit(solution)/shard_map/ppermute | solution.py:20
  13.9 4.3 %collective-permute-done.7.refs_1_ = bf16[128,1024]{1,0:T(8,128)(2,1)S(1)} collective-permute-done((bf16[128,1024]{1,0:T(8,128)(2,1)S(1)}, bf16[128,1024]{1,0:T(8,128)(2,1)S(1)}, u32[]{:S(2)}, u32[]{:S(2)}) %collective-permute-start.7) | collective-permute-done | bytes 262176 | tf_op jit(solution)/shard_map/ppermute | solution.py:20
  18.4 3.3 %collective-permute-start.10 = (bf16[128,1024]{1,0:T(8,128)(2,1)S(1)}, bf16[128,1024]{1,0:T(8,128)(2,1)S(1)}, u32[]{:S(2)}, u32[]{:S(2)}) collective-permute-start(bf16[128,1024]{1,0:T(8,128)(2,1)S(1)} %get-tuple-element.157), channel_id=1, source_target_pairs={{0,1},{1,0},{2,3},{3,2},{4,5},{5,4},{6,7},{7,6},{8,9},{9,8},{10,11... | collective-permute-start | bytes 786440 | tf_op jit(solution)/shard_map/ppermute | solution.py:20
  25.3 2.6 %collective-permute-start.9 = (bf16[128,1024]{1,0:T(8,128)(2,1)S(1)}, bf16[128,1024]{1,0:T(8,128)(2,1)S(1)}, u32[]{:S(2)}, u32[]{:S(2)}) collective-permute-start(bf16[128,1024]{1,0:T(8,128)(2,1)S(1)} %get-tuple-element.156), channel_id=1, source_target_pairs={{0,1},{1,0},{2,3},{3,2},{4,5},{5,4},{6,7},{7,6},{8,9},{9,8},{10,11... | collective-permute-start | bytes 786440 | tf_op jit(solution)/shard_map/ppermute | solution.py:20
  29.6 4.4 %collective-permute-done.9.refs_1_ = bf16[128,1024]{1,0:T(8,128)(2,1)S(1)} collective-permute-done((bf16[128,1024]{1,0:T(8,128)(2,1)S(1)}, bf16[128,1024]{1,0:T(8,128)(2,1)S(1)}, u32[]{:S(2)}, u32[]{:S(2)}) %collective-permute-start.9) | collective-permute-done | bytes 262176 | tf_op jit(solution)/shard_map/ppermute | solution.py:20
  34.6 2.6 %collective-permute-start.11 = (bf16[2,128,256]{2,1,0:T(8,128)(2,1)S(1)}, bf16[2,128,256]{2,1,0:T(8,128)(2,1)S(1)}, u32[]{:S(2)}, u32[]{:S(2)}) collective-permute-start(bf16[2,128,256]{2,1,0:T(8,128)(2,1)S(1)} %get-tuple-element.164.refs_1_.refs_2_), channel_id=1, source_target_pairs={{0,8},{4,12},{8,0},{12,4},{1,9},{5,13},{9,1},{13,5},{2,10},{6,14},... | collective-permute-start | bytes 393224 | tf_op jit(solution)/shard_map/ppermute | solution.py:20
  42.9 1.8 %collective-permute-done.16.refs_1_ = bf16[128,1024]{1,0:T(8,128)(2,1)S(1)} collective-permute-done((bf16[128,1024]{1,0:T(8,128)(2,1)S(1)}, bf16[128,1024]{1,0:T(8,128)(2,1)S(1)}, u32[]{:S(2)}, u32[]{:S(2)}) %collective-permute-start.16) | collective-permute-done | bytes 262176 | tf_op jit(solution)/shard_map/ppermute | solution.py:20
  46.2 1.6 %collective-permute-start.17 = (bf16[128,1024]{1,0:T(8,128)(2,1)S(1)}, bf16[128,1024]{1,0:T(8,128)(2,1)S(1)}, u32[]{:S(2)}, u32[]{:S(2)}) collective-permute-start(bf16[128,1024]{1,0:T(8,128)(2,1)S(1)} %get-tuple-element.186), channel_id=1, source_target_pairs={{0,1},{1,0},{2,3},{3,2},{4,5},{5,4},{6,7},{7,6},{8,9},{9,8},{10,11... | collective-permute-start | bytes 786440 | tf_op jit(solution)/shard_map/ppermute | solution.py:20
  55.3 1.9 %collective-permute-start.26 = (bf16[128,1024]{1,0:T(8,128)(2,1)S(1)}, bf16[128,1024]{1,0:T(8,128)(2,1)S(1)}, u32[]{:S(2)}, u32[]{:S(2)}) collective-permute-start(bf16[128,1024]{1,0:T(8,128)(2,1)S(1)} %get-tuple-element.213), channel_id=1, source_target_pairs={{0,1},{1,0},{2,3},{3,2},{4,5},{5,4},{6,7},{7,6},{8,9},{9,8},{10,11... | collective-permute-start | bytes 786440 | tf_op jit(solution)/shard_map/ppermute | solution.py:20
  64.1 1.9 %collective-permute-start.27 = (bf16[128,1024]{1,0:T(8,128)(2,1)S(1)}, bf16[128,1024]{1,0:T(8,128)(2,1)S(1)}, u32[]{:S(2)}, u32[]{:S(2)}) collective-permute-start(bf16[128,1024]{1,0:T(8,128)(2,1)S(1)} %get-tuple-element.218), channel_id=1, source_target_pairs={{0,1},{1,0},{2,3},{3,2},{4,5},{5,4},{6,7},{7,6},{8,9},{9,8},{10,11... | collective-permute-start | bytes 786440 | tf_op jit(solution)/shard_map/ppermute | solution.py:20
  69.6 1.7 %collective-permute-done.27.refs_1_ = bf16[128,1024]{1,0:T(8,128)(2,1)S(1)} collective-permute-done((bf16[128,1024]{1,0:T(8,128)(2,1)S(1)}, bf16[128,1024]{1,0:T(8,128)(2,1)S(1)}, u32[]{:S(2)}, u32[]{:S(2)}) %collective-permute-start.27) | collective-permute-done | bytes 262176 | tf_op jit(solution)/shard_map/ppermute | solution.py:20
  71.5 1.9 %collective-permute-start.33 = (bf16[128,1024]{1,0:T(8,128)(2,1)S(1)}, bf16[128,1024]{1,0:T(8,128)(2,1)S(1)}, u32[]{:S(2)}, u32[]{:S(2)}) collective-permute-start(bf16[128,1024]{1,0:T(8,128)(2,1)S(1)} %get-tuple-element.236), channel_id=1, source_target_pairs={{0,1},{1,0},{2,3},{3,2},{4,5},{5,4},{6,7},{7,6},{8,9},{9,8},{10,11... | collective-permute-start | bytes 786440 | tf_op jit(solution)/shard_map/ppermute | solution.py:20
  74.5 3.7 %collective-permute-done.33.refs_1_ = bf16[128,1024]{1,0:T(8,128)(2,1)S(1)} collective-permute-done((bf16[128,1024]{1,0:T(8,128)(2,1)S(1)}, bf16[128,1024]{1,0:T(8,128)(2,1)S(1)}, u32[]{:S(2)}, u32[]{:S(2)}) %collective-permute-start.33) | collective-permute-done | bytes 262176 | tf_op jit(solution)/shard_map/ppermute | solution.py:20
  78.4 3.0 %collective-permute-start.34 = (bf16[128,1024]{1,0:T(8,128)(2,1)S(1)}, bf16[128,1024]{1,0:T(8,128)(2,1)S(1)}, u32[]{:S(2)}, u32[]{:S(2)}) collective-permute-start(bf16[128,1024]{1,0:T(8,128)(2,1)S(1)} %get-tuple-element.239), channel_id=1, source_target_pairs={{0,1},{1,0},{2,3},{3,2},{4,5},{5,4},{6,7},{7,6},{8,9},{9,8},{10,11... | collective-permute-start | bytes 786440 | tf_op jit(solution)/shard_map/ppermute | solution.py:20
  82.7 3.9 %collective-permute-start.37 = (bf16[128,1024]{1,0:T(8,128)(2,1)S(1)}, bf16[128,1024]{1,0:T(8,128)(2,1)S(1)}, u32[]{:S(2)}, u32[]{:S(2)}) collective-permute-start(bf16[128,1024]{1,0:T(8,128)(2,1)S(1)} %get-tuple-element.250), channel_id=1, source_target_pairs={{0,1},{1,0},{2,3},{3,2},{4,5},{5,4},{6,7},{7,6},{8,9},{9,8},{10,11... | collective-permute-start | bytes 786440 | tf_op jit(solution)/shard_map/ppermute | solution.py:20
  86.6 2.1 %collective-permute-done.34.refs_1_ = bf16[128,1024]{1,0:T(8,128)(2,1)S(1)} collective-permute-done((bf16[128,1024]{1,0:T(8,128)(2,1)S(1)}, bf16[128,1024]{1,0:T(8,128)(2,1)S(1)}, u32[]{:S(2)}, u32[]{:S(2)}) %collective-permute-start.34) | collective-permute-done | bytes 262176 | tf_op jit(solution)/shard_map/ppermute | solution.py:20
  90.0 2.7 %collective-permute-start.40 = (bf16[2,128,256]{2,1,0:T(8,128)(2,1)S(1)}, bf16[2,128,256]{2,1,0:T(8,128)(2,1)S(1)}, u32[]{:S(2)}, u32[]{:S(2)}) collective-permute-start(bf16[2,128,256]{2,1,0:T(8,128)(2,1)S(1)} %get-tuple-element.263), channel_id=1, source_target_pairs={{0,1},{1,0},{2,3},{3,2},{4,5},{5,4},{6,7},{7,6},{8,9},{9,8},{10,11... | collective-permute-start | bytes 393224 | tf_op jit(solution)/shard_map/ppermute | solution.py:20
  94.1 2.8 %collective-permute-start.38 = (bf16[128,256]{1,0:T(8,128)(2,1)S(1)}, bf16[128,256]{1,0:T(8,128)(2,1)S(1)}, u32[]{:S(2)}, u32[]{:S(2)}) collective-permute-start(bf16[128,256]{1,0:T(8,128)(2,1)S(1)} %get-tuple-element.259), channel_id=1, source_target_pairs={{0,1},{1,0},{2,3},{3,2},{4,5},{5,4},{6,7},{7,6},{8,9},{9,8},{10,11... | collective-permute-start | bytes 196616 | tf_op jit(solution)/shard_map/ppermute | solution.py:20
  98.2 1.8 %collective-permute-start.43 = (bf16[128,256]{1,0:T(8,128)(2,1)S(1)}, bf16[128,256]{1,0:T(8,128)(2,1)S(1)}, u32[]{:S(2)}, u32[]{:S(2)}) collective-permute-start(bf16[128,256]{1,0:T(8,128)(2,1)S(1)} %get-tuple-element.272), channel_id=1, source_target_pairs={{0,3},{1,2},{2,1},{3,0},{4,7},{5,6},{6,5},{7,4},{8,11},{9,10},{10,... | collective-permute-start | bytes 196616 | tf_op jit(solution)/shard_map/ppermute | solution.py:20
  100.4 2.2 %collective-permute-start.45 = (bf16[128,256]{1,0:T(8,128)(2,1)S(1)}, bf16[128,256]{1,0:T(8,128)(2,1)S(1)}, u32[]{:S(2)}, u32[]{:S(2)}) collective-permute-start(bf16[128,256]{1,0:T(8,128)(2,1)S(1)} %get-tuple-element.274), channel_id=1, source_target_pairs={{0,1},{1,0},{2,3},{3,2},{4,5},{5,4},{6,7},{7,6},{8,9},{9,8},{10,11... | collective-permute-start | bytes 196616 | tf_op jit(solution)/shard_map/ppermute | solution.py:20
  102.7 3.3 %collective-permute-done.42.refs_7_ = bf16[1,128,256]{2,1,0:T(8,128)(2,1)S(1)} collective-permute-done((bf16[1,128,256]{2,1,0:T(8,128)(2,1)S(1)}, bf16[1,128,256]{2,1,0:T(8,128)(2,1)S(1)}, u32[]{:S(2)}, u32[]{:S(2)}) %collective-permute-start.42) | collective-permute-done | bytes 65568 | tf_op jit(solution)/shard_map/ppermute | solution.py:20
  106.0 1.9 %collective-permute-done.44.refs_10_ = bf16[128,256]{1,0:T(8,128)(2,1)S(1)} collective-permute-done((bf16[128,256]{1,0:T(8,128)(2,1)S(1)}, bf16[128,256]{1,0:T(8,128)(2,1)S(1)}, u32[]{:S(2)}, u32[]{:S(2)}) %collective-permute-start.44) | collective-permute-done | bytes 65568 | tf_op jit(solution)/shard_map/ppermute | solution.py:20
  (140 shorter events, 47.7 us)
Async XLA Ops:
  4.7 6.9 %collective-permute-start.1 = (bf16[96,1024]{1,0:T(8,128)(2,1)S(1)}, bf16[96,1024]{1,0:T(8,128)(2,1)S(1)}, u32[]{:S(2)}, u32[]{:S(2)}) collective-permute-start(bf16[96,1024]{1,0:T(8,128)(2,1)S(1)} %slice.6.refs_0_), channel_id=1, source_target_pairs={{0,8},{4,12},{8,0},{12,4},{1,9},{5,13},{9,1},{13,5},{2,10},{6,14},... | collective-permute-start | bytes 589832 | tf_op jit(solution)/shard_map/ppermute | solution.py:20
  9.7 8.6 %collective-permute-start.7 = (bf16[128,1024]{1,0:T(8,128)(2,1)S(1)}, bf16[128,1024]{1,0:T(8,128)(2,1)S(1)}, u32[]{:S(2)}, u32[]{:S(2)}) collective-permute-start(bf16[128,1024]{1,0:T(8,128)(2,1)S(1)} %get-tuple-element.143), channel_id=1, source_target_pairs={{0,1},{1,0},{2,3},{3,2},{4,5},{5,4},{6,7},{7,6},{8,9},{9,8},{10,11... | collective-permute-start | bytes 786440 | tf_op jit(solution)/shard_map/ppermute | solution.py:20
  18.3 6.9 %collective-permute-start.8 = (bf16[128,1024]{1,0:T(8,128)(2,1)S(1)}, bf16[128,1024]{1,0:T(8,128)(2,1)S(1)}, u32[]{:S(2)}, u32[]{:S(2)}) collective-permute-start(bf16[128,1024]{1,0:T(8,128)(2,1)S(1)} %get-tuple-element.152), channel_id=1, source_target_pairs={{0,4},{1,2},{2,1},{3,7},{4,0},{5,6},{6,5},{7,3},{8,12},{9,10},{10,... | collective-permute-start | bytes 786440 | tf_op jit(solution)/shard_map/ppermute | solution.py:30
  18.4 9.5 %collective-permute-start.10 = (bf16[128,1024]{1,0:T(8,128)(2,1)S(1)}, bf16[128,1024]{1,0:T(8,128)(2,1)S(1)}, u32[]{:S(2)}, u32[]{:S(2)}) collective-permute-start(bf16[128,1024]{1,0:T(8,128)(2,1)S(1)} %get-tuple-element.157), channel_id=1, source_target_pairs={{0,1},{1,0},{2,3},{3,2},{4,5},{5,4},{6,7},{7,6},{8,9},{9,8},{10,11... | collective-permute-start | bytes 786440 | tf_op jit(solution)/shard_map/ppermute | solution.py:20
  25.3 8.8 %collective-permute-start.9 = (bf16[128,1024]{1,0:T(8,128)(2,1)S(1)}, bf16[128,1024]{1,0:T(8,128)(2,1)S(1)}, u32[]{:S(2)}, u32[]{:S(2)}) collective-permute-start(bf16[128,1024]{1,0:T(8,128)(2,1)S(1)} %get-tuple-element.156), channel_id=1, source_target_pairs={{0,1},{1,0},{2,3},{3,2},{4,5},{5,4},{6,7},{7,6},{8,9},{9,8},{10,11... | collective-permute-start | bytes 786440 | tf_op jit(solution)/shard_map/ppermute | solution.py:20
  27.9 9.3 %collective-permute-start.12 = (bf16[128,1024]{1,0:T(8,128)(2,1)S(1)}, bf16[128,1024]{1,0:T(8,128)(2,1)S(1)}, u32[]{:S(2)}, u32[]{:S(2)}) collective-permute-start(bf16[128,1024]{1,0:T(8,128)(2,1)S(1)} %get-tuple-element.167), channel_id=1, source_target_pairs={{0,4},{1,2},{2,1},{3,7},{4,0},{5,6},{6,5},{7,3},{8,12},{9,10},{10,... | collective-permute-start | bytes 786440 | tf_op jit(solution)/shard_map/ppermute | solution.py:30
  34.6 6.3 %collective-permute-start.11 = (bf16[2,128,256]{2,1,0:T(8,128)(2,1)S(1)}, bf16[2,128,256]{2,1,0:T(8,128)(2,1)S(1)}, u32[]{:S(2)}, u32[]{:S(2)}) collective-permute-start(bf16[2,128,256]{2,1,0:T(8,128)(2,1)S(1)} %get-tuple-element.164.refs_1_.refs_2_), channel_id=1, source_target_pairs={{0,8},{4,12},{8,0},{12,4},{1,9},{5,13},{9,1},{13,5},{2,10},{6,14},... | collective-permute-start | bytes 393224 | tf_op jit(solution)/shard_map/ppermute | solution.py:20
  37.3 7.5 %collective-permute-start.16 = (bf16[128,1024]{1,0:T(8,128)(2,1)S(1)}, bf16[128,1024]{1,0:T(8,128)(2,1)S(1)}, u32[]{:S(2)}, u32[]{:S(2)}) collective-permute-start(bf16[128,1024]{1,0:T(8,128)(2,1)S(1)} %get-tuple-element.181), channel_id=1, source_target_pairs={{0,1},{1,0},{2,3},{3,2},{4,5},{5,4},{6,7},{7,6},{8,9},{9,8},{10,11... | collective-permute-start | bytes 786440 | tf_op jit(solution)/shard_map/ppermute | solution.py:20
  38.3 7.9 %collective-permute-start.15 = (bf16[128,1024]{1,0:T(8,128)(2,1)S(1)}, bf16[128,1024]{1,0:T(8,128)(2,1)S(1)}, u32[]{:S(2)}, u32[]{:S(2)}) collective-permute-start(bf16[128,1024]{1,0:T(8,128)(2,1)S(1)} %get-tuple-element.178), channel_id=1, source_target_pairs={{0,4},{1,2},{2,1},{3,7},{4,0},{5,6},{6,5},{7,3},{8,12},{9,10},{10,... | collective-permute-start | bytes 786440 | tf_op jit(solution)/shard_map/ppermute | solution.py:30
  46.2 7.1 %collective-permute-start.17 = (bf16[128,1024]{1,0:T(8,128)(2,1)S(1)}, bf16[128,1024]{1,0:T(8,128)(2,1)S(1)}, u32[]{:S(2)}, u32[]{:S(2)}) collective-permute-start(bf16[128,1024]{1,0:T(8,128)(2,1)S(1)} %get-tuple-element.186), channel_id=1, source_target_pairs={{0,1},{1,0},{2,3},{3,2},{4,5},{5,4},{6,7},{7,6},{8,9},{9,8},{10,11... | collective-permute-start | bytes 786440 | tf_op jit(solution)/shard_map/ppermute | solution.py:20
  47.8 7.4 %collective-permute-start.22 = (bf16[128,1024]{1,0:T(8,128)(2,1)S(1)}, bf16[128,1024]{1,0:T(8,128)(2,1)S(1)}, u32[]{:S(2)}, u32[]{:S(2)}) collective-permute-start(bf16[128,1024]{1,0:T(8,128)(2,1)S(1)} %get-tuple-element.201), channel_id=1, source_target_pairs={{0,4},{1,2},{2,1},{3,7},{4,0},{5,6},{6,5},{7,3},{8,12},{9,10},{10,... | collective-permute-start | bytes 786440 | tf_op jit(solution)/shard_map/ppermute | solution.py:30
  55.3 6.7 %collective-permute-start.26 = (bf16[128,1024]{1,0:T(8,128)(2,1)S(1)}, bf16[128,1024]{1,0:T(8,128)(2,1)S(1)}, u32[]{:S(2)}, u32[]{:S(2)}) collective-permute-start(bf16[128,1024]{1,0:T(8,128)(2,1)S(1)} %get-tuple-element.213), channel_id=1, source_target_pairs={{0,1},{1,0},{2,3},{3,2},{4,5},{5,4},{6,7},{7,6},{8,9},{9,8},{10,11... | collective-permute-start | bytes 786440 | tf_op jit(solution)/shard_map/ppermute | solution.py:20
  57.2 6.8 %collective-permute-start.25 = (bf16[128,1024]{1,0:T(8,128)(2,1)S(1)}, bf16[128,1024]{1,0:T(8,128)(2,1)S(1)}, u32[]{:S(2)}, u32[]{:S(2)}) collective-permute-start(bf16[128,1024]{1,0:T(8,128)(2,1)S(1)} %get-tuple-element.211), channel_id=1, source_target_pairs={{0,4},{1,2},{2,1},{3,7},{4,0},{5,6},{6,5},{7,3},{8,12},{9,10},{10,... | collective-permute-start | bytes 786440 | tf_op jit(solution)/shard_map/ppermute | solution.py:30
  64.1 7.2 %collective-permute-start.27 = (bf16[128,1024]{1,0:T(8,128)(2,1)S(1)}, bf16[128,1024]{1,0:T(8,128)(2,1)S(1)}, u32[]{:S(2)}, u32[]{:S(2)}) collective-permute-start(bf16[128,1024]{1,0:T(8,128)(2,1)S(1)} %get-tuple-element.218), channel_id=1, source_target_pairs={{0,1},{1,0},{2,3},{3,2},{4,5},{5,4},{6,7},{7,6},{8,9},{9,8},{10,11... | collective-permute-start | bytes 786440 | tf_op jit(solution)/shard_map/ppermute | solution.py:20
  71.5 6.8 %collective-permute-start.33 = (bf16[128,1024]{1,0:T(8,128)(2,1)S(1)}, bf16[128,1024]{1,0:T(8,128)(2,1)S(1)}, u32[]{:S(2)}, u32[]{:S(2)}) collective-permute-start(bf16[128,1024]{1,0:T(8,128)(2,1)S(1)} %get-tuple-element.236), channel_id=1, source_target_pairs={{0,1},{1,0},{2,3},{3,2},{4,5},{5,4},{6,7},{7,6},{8,9},{9,8},{10,11... | collective-permute-start | bytes 786440 | tf_op jit(solution)/shard_map/ppermute | solution.py:20
  78.4 10.3 %collective-permute-start.34 = (bf16[128,1024]{1,0:T(8,128)(2,1)S(1)}, bf16[128,1024]{1,0:T(8,128)(2,1)S(1)}, u32[]{:S(2)}, u32[]{:S(2)}) collective-permute-start(bf16[128,1024]{1,0:T(8,128)(2,1)S(1)} %get-tuple-element.239), channel_id=1, source_target_pairs={{0,1},{1,0},{2,3},{3,2},{4,5},{5,4},{6,7},{7,6},{8,9},{9,8},{10,11... | collective-permute-start | bytes 786440 | tf_op jit(solution)/shard_map/ppermute | solution.py:20
  82.7 10.1 %collective-permute-start.37 = (bf16[128,1024]{1,0:T(8,128)(2,1)S(1)}, bf16[128,1024]{1,0:T(8,128)(2,1)S(1)}, u32[]{:S(2)}, u32[]{:S(2)}) collective-permute-start(bf16[128,1024]{1,0:T(8,128)(2,1)S(1)} %get-tuple-element.250), channel_id=1, source_target_pairs={{0,1},{1,0},{2,3},{3,2},{4,5},{5,4},{6,7},{7,6},{8,9},{9,8},{10,11... | collective-permute-start | bytes 786440 | tf_op jit(solution)/shard_map/ppermute | solution.py:20
  90.0 7.0 %collective-permute-start.40 = (bf16[2,128,256]{2,1,0:T(8,128)(2,1)S(1)}, bf16[2,128,256]{2,1,0:T(8,128)(2,1)S(1)}, u32[]{:S(2)}, u32[]{:S(2)}) collective-permute-start(bf16[2,128,256]{2,1,0:T(8,128)(2,1)S(1)} %get-tuple-element.263), channel_id=1, source_target_pairs={{0,1},{1,0},{2,3},{3,2},{4,5},{5,4},{6,7},{7,6},{8,9},{9,8},{10,11... | collective-permute-start | bytes 393224 | tf_op jit(solution)/shard_map/ppermute | solution.py:20
  92.9 7.5 %collective-permute-start.39 = (bf16[2,128,256]{2,1,0:T(8,128)(2,1)S(1)}, bf16[2,128,256]{2,1,0:T(8,128)(2,1)S(1)}, u32[]{:S(2)}, u32[]{:S(2)}) collective-permute-start(bf16[2,128,256]{2,1,0:T(8,128)(2,1)S(1)} %get-tuple-element.261), channel_id=1, source_target_pairs={{0,4},{1,2},{2,1},{3,7},{4,0},{5,6},{6,5},{7,3},{8,12},{9,10},{10,... | collective-permute-start | bytes 393224 | tf_op jit(solution)/shard_map/ppermute | solution.py:30
  94.1 8.5 %collective-permute-start.38 = (bf16[128,256]{1,0:T(8,128)(2,1)S(1)}, bf16[128,256]{1,0:T(8,128)(2,1)S(1)}, u32[]{:S(2)}, u32[]{:S(2)}) collective-permute-start(bf16[128,256]{1,0:T(8,128)(2,1)S(1)} %get-tuple-element.259), channel_id=1, source_target_pairs={{0,1},{1,0},{2,3},{3,2},{4,5},{5,4},{6,7},{7,6},{8,9},{9,8},{10,11... | collective-permute-start | bytes 196616 | tf_op jit(solution)/shard_map/ppermute | solution.py:20
  97.0 9.0 %collective-permute-start.42 = (bf16[1,128,256]{2,1,0:T(8,128)(2,1)S(1)}, bf16[1,128,256]{2,1,0:T(8,128)(2,1)S(1)}, u32[]{:S(2)}, u32[]{:S(2)}) collective-permute-start(bf16[1,128,256]{2,1,0:T(8,128)(2,1)S(1)} %get-tuple-element.270), channel_id=1, source_target_pairs={{0,2},{1,3},{2,0},{3,1},{4,6},{5,7},{6,4},{7,5},{8,10},{9,11},{10,... | collective-permute-start | bytes 196616 | tf_op jit(solution)/shard_map/ppermute | solution.py:20
  98.2 7.8 %collective-permute-start.43 = (bf16[128,256]{1,0:T(8,128)(2,1)S(1)}, bf16[128,256]{1,0:T(8,128)(2,1)S(1)}, u32[]{:S(2)}, u32[]{:S(2)}) collective-permute-start(bf16[128,256]{1,0:T(8,128)(2,1)S(1)} %get-tuple-element.272), channel_id=1, source_target_pairs={{0,3},{1,2},{2,1},{3,0},{4,7},{5,6},{6,5},{7,4},{8,11},{9,10},{10,... | collective-permute-start | bytes 196616 | tf_op jit(solution)/shard_map/ppermute | solution.py:20
  100.1 7.9 %collective-permute-start.44 = (bf16[128,256]{1,0:T(8,128)(2,1)S(1)}, bf16[128,256]{1,0:T(8,128)(2,1)S(1)}, u32[]{:S(2)}, u32[]{:S(2)}) collective-permute-start(bf16[128,256]{1,0:T(8,128)(2,1)S(1)} %get-tuple-element.273), channel_id=1, source_target_pairs={{0,2},{1,3},{2,0},{3,1},{4,6},{5,7},{6,4},{7,5},{8,10},{9,11},{10,... | collective-permute-start | bytes 196616 | tf_op jit(solution)/shard_map/ppermute | solution.py:20
  100.4 7.5 %collective-permute-start.45 = (bf16[128,256]{1,0:T(8,128)(2,1)S(1)}, bf16[128,256]{1,0:T(8,128)(2,1)S(1)}, u32[]{:S(2)}, u32[]{:S(2)}) collective-permute-start(bf16[128,256]{1,0:T(8,128)(2,1)S(1)} %get-tuple-element.274), channel_id=1, source_target_pairs={{0,1},{1,0},{2,3},{3,2},{4,5},{5,4},{6,7},{7,6},{8,9},{9,8},{10,11... | collective-permute-start | bytes 196616 | tf_op jit(solution)/shard_map/ppermute | solution.py:20
  (31 other events, 121.8 us)
